TPU v7x, 32 devices: a whole 2x2x4 slice. The times are simulated.
32 devices in a mesh: dp: 8 (over z, y), expert: 4 (over x, core).
Axes of the slice: x: 2, y: 2, z: 4, core: 2. Of those that a mesh axis runs over, the one named last changes fastest.
Arguments:
- tokens: bfloat16 [24, 1024, 384], P('expert', 'dp'), may hold values from -36 to 36
- cotangent: bfloat16 [24, 1024, 384], P('expert', 'dp'), may hold values from -6 to 6
- lengths: int32 [24], P('expert'), may hold values from 128 to 1024, as said below
- routes: int32 [8, 4, 768, 2], P('dp', 'expert'), may hold values from 0 to 7, all different within a row; in each aligned block of 768 rows (0 to 767, 768 to 1535, ..., all dimensions but the last counted through in order) at most 384 rows name the same one
- dense_weights: float32 [2363520], P(('dp', 'expert')), may hold values from -0.8164966 to 1.4
- dense_first: float32 [2363520], P(('dp', 'expert')), may hold values from -940.60406 to 940.60406
- dense_second: float32 [2363520], P(('dp', 'expert')), may hold values from 0 to 393216, as said below
- dense_average: float32 [2363520], P(('dp', 'expert')), may hold values from -0.8164966 to 1.4
- expert_weights: float32 [8, 1769472], P('expert', 'dp'), may hold values from -0.4082483 to 0.4082483
- expert_first: float32 [8, 1769472], P('expert', 'dp'), may hold values from -156.767344 to 156.767344
- expert_second: float32 [8, 1769472], P('expert', 'dp'), may hold values from 0 to 24576, as said below
- expert_average: float32 [8, 1769472], P('expert', 'dp'), may hold values from -0.4082483 to 0.4082483
Outputs:
- output: bfloat16 [24, 1024, 384], P('expert', 'dp')
- grad_tokens: float32 [24, 1024, 384], P('expert', 'dp')
- dense_grad: float32 [2363520], P(('dp', 'expert'))
- dense_first_new: float32 [2363520], P(('dp', 'expert'))
- dense_second_new: float32 [2363520], P(('dp', 'expert'))
- dense_new: float32 [2363520], P(('dp', 'expert'))
- dense_average_new: float32 [2363520], P(('dp', 'expert'))
- expert_grad: float32 [8, 1769472], P('expert', 'dp')
- expert_first_new: float32 [8, 1769472], P('expert', 'dp')
- expert_second_new: float32 [8, 1769472], P('expert', 'dp')
- expert_new: float32 [8, 1769472], P('expert', 'dp')
- expert_average_new: float32 [8, 1769472], P('expert', 'dp')
Inputs may be any that keep to these rules, and one draw needn't show every extreme that they name: Series lengths run from an eighth of 1024 to 1024, the positions beyond a series' length padding; some series fills its slot. `routes`: among the positions of one device no expert is named more than 384 times. `dense_second`: positive. `expert_second`: positive.
All inputs are finite; a program needn't handle non-finite values.
Results may differ from a plain program's by a relative error of at most 0.017.
The roundings to bfloat16 on the way count: a program that leaves them out, or rounds other values in their place, can miss the bound.
Values may be sent and summed in bfloat16 or wider, within the bound.
A program may use at most 256 MiB of HBM per device.

v0:
```python
import math

import jax
import jax.numpy as jnp
from jax import lax
from jax.sharding import PartitionSpec as P

D = 384
HEADS = 12
HEAD_DIM = 32
FF = 1536
EXPERTS = 8
TOP = 2
SEG = 128
SERIES_DEV = 6
STEP = 8
TOK_DEV = 768
CAP = 384


eps_norm = 1e-06
beta_one = 0.5
beta_two = 0.5
learn_rate = 0.02
weight_decay = 0.1
eps_adam = 1e-08
average_keep = 0.9
rope_base = 10000.0
neg_fill = -1e30


def rotate(values, positions, direction):
    half_dim = HEAD_DIM // 2
    inverse = rope_base ** (-jnp.arange(half_dim, dtype=jnp.float32) * 2.0 / HEAD_DIM)
    angles = positions.astype(jnp.float32)[:, None] * inverse[None, :]
    cosine = jnp.cos(angles)[:, None, :]
    sine = jnp.sin(angles)[:, None, :] * direction
    first = values[..., :half_dim]
    second = values[..., half_dim:]
    return jnp.concatenate(
        [first * cosine - second * sine, second * cosine + first * sine], axis=-1
    )


def dense_pieces(flat_params):
    row_width = 4 * D + EXPERTS + 3 * FF + 3
    row_table = flat_params.reshape(D, row_width)
    column_widths = [D, D, D, D, EXPERTS, FF, FF, FF, 1, 1, 1]
    pieces = []
    offset = 0
    for column_width in column_widths:
        pieces.append(row_table[:, offset : offset + column_width])
        offset = offset + column_width
    w_query, w_key, w_value, w_output, w_router, w_sgate, w_sup = pieces[:7]
    w_sdown = pieces[7].T
    return [
        w_query,
        w_key,
        w_value,
        w_output,
        w_router,
        w_sgate,
        w_sup,
        w_sdown,
        pieces[8][:, 0],
        pieces[9][:, 0],
        pieces[10][:, 0],
    ]


def expert_pieces(flat_params):
    first_end = D * FF
    gate_part = flat_params[:, :first_end].reshape(-1, D, FF)
    up_part = flat_params[:, first_end : 2 * first_end].reshape(-1, D, FF)
    down_part = flat_params[:, 2 * first_end :].reshape(-1, FF, D)
    return (gate_part, up_part, down_part)


def masked_scores(query_block, key_block, query_pos, key_pos, series_lengths):
    scores = jnp.einsum(
        "sqhd,skhd->shqk", query_block, key_block, preferred_element_type=jnp.float32
    ) * HEAD_DIM ** (-0.5)
    causal = key_pos[None, :] <= query_pos[:, None]
    inside = key_pos[None, :] < series_lengths[:, None]
    allowed = causal[None, None, :, :] & inside[:, None, None, :]
    return jnp.where(allowed, scores, neg_fill)


def block_rows(values, index, extent):
    return lax.dynamic_slice_in_dim(values, index * extent, extent, 1)


def weight_grad(left, right):
    return jnp.einsum("td,te->de", left, right, preferred_element_type=jnp.float32)


def input_grad(grad_rows, weight):
    return jnp.einsum("te,de->td", grad_rows, weight, preferred_element_type=jnp.float32)


def adamw_update(weights, grads, first, second, average):
    first_new = beta_one * first + (1.0 - beta_one) * grads
    second_new = beta_two * second + (1.0 - beta_two) * grads * grads
    first_hat = first_new / (1.0 - beta_one**STEP)
    second_hat = second_new / (1.0 - beta_two**STEP)
    weights_new = weights - learn_rate * (
        first_hat / (jnp.sqrt(second_hat) + eps_adam) + weight_decay * weights
    )
    average_new = average_keep * average + (1.0 - average_keep) * weights_new
    return (first_new, second_new, weights_new, average_new)


def local(
    tokens,
    cotangent,
    lengths,
    routes,
    dense_weights,
    dense_first,
    dense_second,
    dense_average,
    expert_weights,
    expert_first,
    expert_second,
    expert_average,
):
    dp_count = lax.axis_size("dp")
    dp_place = lax.axis_index("dp")
    expert_count = lax.axis_size("expert")
    local_experts = EXPERTS // expert_count
    series_length = SEG * dp_count
    block_size = math.gcd(series_length, 512)
    block_count = series_length // block_size
    dense_all = lax.all_gather(
        dense_weights.astype(jnp.bfloat16), ("dp", "expert"), axis=0, tiled=True
    )
    expert_all = lax.all_gather(expert_weights.astype(jnp.bfloat16), "dp", axis=1, tiled=True)
    (
        w_query,
        w_key,
        w_value,
        w_output,
        w_router,
        w_sgate,
        w_sup,
        w_sdown,
        w_svec,
        gain_one,
        gain_two,
    ) = dense_pieces(dense_all)
    e_gate, e_up, e_down = expert_pieces(expert_all)
    gain_first = gain_one.astype(jnp.float32)
    gain_second = gain_two.astype(jnp.float32)
    residual = tokens.astype(jnp.float32).reshape(TOK_DEV, D)
    scale_one = lax.rsqrt(jnp.mean(residual * residual, axis=-1, keepdims=True) + eps_norm)
    normed_one = residual * scale_one
    act_one = (normed_one * gain_first).astype(jnp.bfloat16)
    local_pos = dp_place * SEG + jnp.arange(SEG, dtype=jnp.int32)
    head_shape = (SERIES_DEV, SEG, HEADS, HEAD_DIM)
    flat_shape = (SERIES_DEV, SEG, D)
    whole_shape = (SERIES_DEV, series_length, HEADS, HEAD_DIM)
    stat_shape = (SERIES_DEV, HEADS, SEG)
    query_lin = jnp.dot(act_one, w_query, preferred_element_type=jnp.float32)
    key_lin = jnp.dot(act_one, w_key, preferred_element_type=jnp.float32)
    value_low = jnp.dot(act_one, w_value, preferred_element_type=jnp.float32).astype(jnp.bfloat16)
    query_rot = rotate(query_lin.reshape(head_shape), local_pos, 1.0).astype(jnp.bfloat16)
    key_rot = rotate(key_lin.reshape(head_shape), local_pos, 1.0).astype(jnp.bfloat16)
    keys_all, values_all = (
        lax.all_gather(key_rot.reshape(flat_shape), "dp", axis=1, tiled=True),
        lax.all_gather(value_low.reshape(flat_shape), "dp", axis=1, tiled=True),
    )
    keys_heads = keys_all.reshape(whole_shape)
    values_heads = values_all.reshape(whole_shape)

    def block_scores(index):
        key_pos = index * block_size + jnp.arange(block_size, dtype=jnp.int32)
        return masked_scores(
            query_rot, block_rows(keys_heads, index, block_size), local_pos, key_pos, lengths
        )

    def stats_step(carry, index):
        run_max, run_total = carry
        scores = block_scores(index)
        new_max = jnp.maximum(run_max, jnp.max(scores, axis=-1))
        run_total = run_total * jnp.exp(run_max - new_max) + jnp.sum(
            jnp.exp(scores - new_max[..., None]), axis=-1
        )
        return ((new_max, run_total), None)

    (run_max, run_total), unused = lax.scan(
        stats_step,
        (jnp.full(stat_shape, neg_fill, jnp.float32), jnp.zeros(stat_shape, jnp.float32)),
        jnp.arange(block_count),
    )
    log_total = run_max + jnp.log(run_total)

    def output_step(total, index):
        probs_low = jnp.exp(block_scores(index) - log_total[..., None]).astype(jnp.bfloat16)
        added = jnp.einsum(
            "shqk,skhd->sqhd",
            probs_low,
            block_rows(values_heads, index, block_size),
            preferred_element_type=jnp.float32,
        )
        return (total + added, None)

    heads_out, unused = lax.scan(
        output_step, jnp.zeros(head_shape, jnp.float32), jnp.arange(block_count)
    )
    attn_low = heads_out.reshape(TOK_DEV, D).astype(jnp.bfloat16)
    mixed_rows = residual + jnp.dot(attn_low, w_output, preferred_element_type=jnp.float32)
    scale_two = lax.rsqrt(jnp.mean(mixed_rows * mixed_rows, axis=-1, keepdims=True) + eps_norm)
    normed_two = mixed_rows * scale_two
    act_two = (normed_two * gain_second).astype(jnp.bfloat16)
    logits_low = jnp.dot(act_two, w_router, preferred_element_type=jnp.float32)
    router_probs = jax.nn.softmax(logits_low, axis=-1)
    routes_flat = routes.reshape(TOK_DEV * TOP)
    chosen = (routes_flat[:, None] == jnp.arange(EXPERTS, dtype=jnp.int32)[None, :]).astype(
        jnp.int32
    )
    slot_index = jnp.sum((jnp.cumsum(chosen, axis=0) - chosen) * chosen, axis=-1)
    targets = routes_flat * CAP + slot_index
    chosen_float = chosen.reshape(TOK_DEV, TOP, EXPERTS).astype(jnp.float32)
    route_gates = jnp.sum(router_probs[:, None, :] * chosen_float, axis=-1)
    dispatched = jnp.repeat(act_two, TOP, axis=0)
    send_buffer = jnp.zeros((EXPERTS * CAP, D), jnp.bfloat16).at[targets].set(dispatched)
    sgate_lin = jnp.dot(act_two, w_sgate, preferred_element_type=jnp.float32)
    sup_lin = jnp.dot(act_two, w_sup, preferred_element_type=jnp.float32)
    shared_hidden = (jax.nn.silu(sgate_lin) * sup_lin).astype(jnp.bfloat16)
    shared_lin = jnp.dot(shared_hidden, w_sdown, preferred_element_type=jnp.float32)
    shared_gate = jax.nn.sigmoid(
        jnp.dot(act_two, w_svec[:, None], preferred_element_type=jnp.float32)
    )
    received = lax.all_to_all(
        send_buffer.reshape(EXPERTS, CAP, D), "expert", split_axis=0, concat_axis=0, tiled=True
    )
    grouped = received.reshape(expert_count, local_experts, -1, D)
    gate_lin = jnp.einsum("nerd,edf->nerf", grouped, e_gate, preferred_element_type=jnp.float32)
    up_lin = jnp.einsum("nerd,edf->nerf", grouped, e_up, preferred_element_type=jnp.float32)
    hidden = (jax.nn.silu(gate_lin) * up_lin).astype(jnp.bfloat16)
    result = jnp.einsum(
        "nerf,efd->nerd", hidden, e_down, preferred_element_type=jnp.float32
    ).astype(jnp.bfloat16)
    returned = lax.all_to_all(
        result.reshape(received.shape), "expert", split_axis=0, concat_axis=0, tiled=True
    )
    returned, kept_rows = (returned, received)
    expert_out = (
        returned.reshape(EXPERTS * CAP, D)[targets].astype(jnp.float32).reshape(TOK_DEV, TOP, D)
    )
    routed = jnp.sum(route_gates[..., None] * expert_out, axis=1)
    result_rows = mixed_rows + routed + shared_gate * shared_lin
    output = result_rows.astype(jnp.bfloat16).reshape(flat_shape)
    live = (local_pos[None, :] < lengths[:, None]).astype(jnp.float32)
    grad_out = (cotangent.astype(jnp.float32) * live[..., None]).reshape(TOK_DEV, D)
    grad_gates = jnp.sum(grad_out[:, None, :] * expert_out, axis=-1)
    grad_expert_out = (
        (route_gates[..., None] * grad_out[:, None, :])
        .astype(jnp.bfloat16)
        .reshape(TOK_DEV * TOP, D)
    )
    grad_buffer = jnp.zeros((EXPERTS * CAP, D), jnp.bfloat16).at[targets].set(grad_expert_out)
    grad_received = lax.all_to_all(
        grad_buffer.reshape(EXPERTS, CAP, D), "expert", split_axis=0, concat_axis=0, tiled=True
    )
    grouped = kept_rows.reshape(expert_count, local_experts, -1, D)
    grad_grouped = grad_received.reshape(expert_count, local_experts, -1, D)
    gate_lin = jnp.einsum("nerd,edf->nerf", grouped, e_gate, preferred_element_type=jnp.float32)
    up_lin = jnp.einsum("nerd,edf->nerf", grouped, e_up, preferred_element_type=jnp.float32)
    gate_sigmoid = jax.nn.sigmoid(gate_lin)
    gate_silu = jax.nn.silu(gate_lin)
    hidden = (gate_silu * up_lin).astype(jnp.bfloat16)
    grad_hidden = jnp.einsum(
        "nerd,efd->nerf", grad_grouped, e_down, preferred_element_type=jnp.float32
    )
    grad_e_down = jnp.einsum(
        "nerf,nerd->efd", hidden, grad_grouped, preferred_element_type=jnp.float32
    )
    silu_slope = gate_sigmoid * (1.0 + gate_lin * (1.0 - gate_sigmoid))
    grad_gate_lin = (grad_hidden * up_lin * silu_slope).astype(jnp.bfloat16)
    grad_up_lin = (grad_hidden * gate_silu).astype(jnp.bfloat16)
    grad_e_gate = jnp.einsum(
        "nerd,nerf->edf", grouped, grad_gate_lin, preferred_element_type=jnp.float32
    )
    grad_e_up = jnp.einsum(
        "nerd,nerf->edf", grouped, grad_up_lin, preferred_element_type=jnp.float32
    )
    grad_in = jnp.einsum(
        "nerf,edf->nerd", grad_gate_lin, e_gate, preferred_element_type=jnp.float32
    ) + jnp.einsum("nerf,edf->nerd", grad_up_lin, e_up, preferred_element_type=jnp.float32)
    grad_in = grad_in.astype(jnp.bfloat16).reshape(EXPERTS, -1, D)
    grad_back = lax.all_to_all(grad_in, "expert", split_axis=0, concat_axis=0, tiled=True)
    grad_routed = jnp.sum(
        grad_back.reshape(EXPERTS * CAP, D)[targets].astype(jnp.float32).reshape(TOK_DEV, TOP, D),
        axis=1,
    )
    grad_router_probs = jnp.sum(grad_gates[..., None] * chosen_float, axis=1)
    grad_logits = (
        router_probs
        * (grad_router_probs - jnp.sum(router_probs * grad_router_probs, axis=-1, keepdims=True))
    ).astype(jnp.bfloat16)
    grad_shared_lin = (grad_out * shared_gate).astype(jnp.bfloat16)
    grad_svec_logit = (
        shared_gate * (1.0 - shared_gate) * jnp.sum(grad_out * shared_lin, axis=-1, keepdims=True)
    ).astype(jnp.bfloat16)
    grad_shared_hidden = input_grad(grad_shared_lin, w_sdown)
    sgate_sigmoid = jax.nn.sigmoid(sgate_lin)
    grad_sgate_lin = (
        grad_shared_hidden * sup_lin * sgate_sigmoid * (1.0 + sgate_lin * (1.0 - sgate_sigmoid))
    ).astype(jnp.bfloat16)
    grad_sup_lin = (grad_shared_hidden * jax.nn.silu(sgate_lin)).astype(jnp.bfloat16)
    grad_act_two = (
        grad_routed
        + input_grad(grad_sgate_lin, w_sgate)
        + input_grad(grad_sup_lin, w_sup)
        + input_grad(grad_logits, w_router)
        + grad_svec_logit.astype(jnp.float32) * w_svec.astype(jnp.float32)[None, :]
    )
    grad_gain_two = jnp.sum(grad_act_two * normed_two, axis=0)
    weighted_two = grad_act_two * gain_second
    grad_mixed = grad_out + scale_two * (
        weighted_two - normed_two * jnp.mean(weighted_two * normed_two, axis=-1, keepdims=True)
    )
    grad_attn_low = grad_mixed.astype(jnp.bfloat16)
    grad_heads = input_grad(grad_attn_low, w_output).astype(jnp.bfloat16).reshape(head_shape)

    def delta_step(total, index):
        attn_probs = jnp.exp(block_scores(index) - log_total[..., None])
        grad_probs = jnp.einsum(
            "sqhd,skhd->shqk",
            grad_heads,
            block_rows(values_heads, index, block_size),
            preferred_element_type=jnp.float32,
        )
        return (total + jnp.sum(attn_probs * grad_probs, axis=-1), None)

    row_delta, unused = lax.scan(
        delta_step, jnp.zeros(stat_shape, jnp.float32), jnp.arange(block_count)
    )

    def grad_step(carry, index):
        grad_query, grad_keys, grad_values = carry
        keys_block = block_rows(keys_heads, index, block_size)
        values_block = block_rows(values_heads, index, block_size)
        attn_probs = jnp.exp(block_scores(index) - log_total[..., None])
        grad_probs = jnp.einsum(
            "sqhd,skhd->shqk", grad_heads, values_block, preferred_element_type=jnp.float32
        )
        grad_scores = (attn_probs * (grad_probs - row_delta[..., None])).astype(jnp.bfloat16)
        grad_query = grad_query + jnp.einsum(
            "shqk,skhd->sqhd", grad_scores, keys_block, preferred_element_type=jnp.float32
        )
        key_part = jnp.einsum(
            "shqk,sqhd->skhd", grad_scores, query_rot, preferred_element_type=jnp.float32
        )
        value_part = jnp.einsum(
            "shqk,sqhd->skhd",
            attn_probs.astype(jnp.bfloat16),
            grad_heads,
            preferred_element_type=jnp.float32,
        )
        grad_keys = lax.dynamic_update_slice_in_dim(grad_keys, key_part, index * block_size, 1)
        grad_values = lax.dynamic_update_slice_in_dim(
            grad_values, value_part, index * block_size, 1
        )
        return ((grad_query, grad_keys, grad_values), None)

    zeros_whole = jnp.zeros(whole_shape, jnp.float32)
    (grad_query, grad_keys_whole, grad_values_whole), unused = lax.scan(
        grad_step,
        (jnp.zeros(head_shape, jnp.float32), zeros_whole, zeros_whole),
        jnp.arange(block_count),
    )
    whole_flat = (SERIES_DEV, series_length, D)
    grad_keys, grad_values = (
        lax.psum_scatter(
            grad_keys_whole.reshape(whole_flat).astype(jnp.bfloat16),
            "dp",
            scatter_dimension=1,
            tiled=True,
        ).astype(jnp.float32),
        lax.psum_scatter(
            grad_values_whole.reshape(whole_flat).astype(jnp.bfloat16),
            "dp",
            scatter_dimension=1,
            tiled=True,
        ).astype(jnp.float32),
    )
    score_scale = HEAD_DIM ** (-0.5)
    grad_query_lin = (
        rotate(grad_query * score_scale, local_pos, -1.0).reshape(TOK_DEV, D).astype(jnp.bfloat16)
    )
    grad_key_lin = (
        rotate(grad_keys.reshape(head_shape) * score_scale, local_pos, -1.0)
        .reshape(TOK_DEV, D)
        .astype(jnp.bfloat16)
    )
    grad_value_low = grad_values.reshape(TOK_DEV, D).astype(jnp.bfloat16)
    grad_act_one = (
        input_grad(grad_query_lin, w_query)
        + input_grad(grad_key_lin, w_key)
        + input_grad(grad_value_low, w_value)
    )
    grad_gain_one = jnp.sum(grad_act_one * normed_one, axis=0)
    weighted_one = grad_act_one * gain_first
    grad_tokens = grad_mixed + scale_one * (
        weighted_one - normed_one * jnp.mean(weighted_one * normed_one, axis=-1, keepdims=True)
    )
    dense_parts = [
        weight_grad(act_one, grad_query_lin),
        weight_grad(act_one, grad_key_lin),
        weight_grad(act_one, grad_value_low),
        weight_grad(attn_low, grad_attn_low),
        weight_grad(act_two, grad_logits),
        weight_grad(act_two, grad_sgate_lin),
        weight_grad(act_two, grad_sup_lin),
        weight_grad(grad_shared_lin, shared_hidden),
        weight_grad(act_two, grad_svec_logit),
        grad_gain_one[:, None],
        grad_gain_two[:, None],
    ]
    dense_terms = jnp.concatenate(dense_parts, axis=1).reshape(-1)
    dense_grad = lax.psum_scatter(dense_terms, ("dp", "expert"), scatter_dimension=0, tiled=True)
    expert_terms = jnp.concatenate(
        [
            grad_e_gate.reshape(local_experts, -1),
            grad_e_up.reshape(local_experts, -1),
            grad_e_down.reshape(local_experts, -1),
        ],
        axis=1,
    )
    expert_grad = lax.psum_scatter(
        expert_terms.astype(jnp.bfloat16), "dp", scatter_dimension=1, tiled=True
    ).astype(jnp.float32)
    dense_first_new, dense_second_new, dense_new, dense_average_new = adamw_update(
        dense_weights, dense_grad, dense_first, dense_second, dense_average
    )
    expert_first_new, expert_second_new, expert_new, expert_average_new = adamw_update(
        expert_weights, expert_grad, expert_first, expert_second, expert_average
    )
    return (
        output,
        grad_tokens.reshape(flat_shape),
        dense_grad,
        dense_first_new,
        dense_second_new,
        dense_new,
        dense_average_new,
        expert_grad,
        expert_first_new,
        expert_second_new,
        expert_new,
        expert_average_new,
    )


def solution(mesh):
    placed = (
        P("expert", "dp", None),
        P("expert", "dp", None),
        P("expert"),
        P("dp", "expert", None, None),
        P(("dp", "expert")),
        P(("dp", "expert")),
        P(("dp", "expert")),
        P(("dp", "expert")),
        P("expert", "dp"),
        P("expert", "dp"),
        P("expert", "dp"),
        P("expert", "dp"),
    )
    return jax.shard_map(
        local,
        mesh=mesh,
        in_specs=placed,
        out_specs=(
            P("expert", "dp", None),
            P("expert", "dp", None),
            P(("dp", "expert")),
            P(("dp", "expert")),
            P(("dp", "expert")),
            P(("dp", "expert")),
            P(("dp", "expert")),
            P("expert", "dp"),
            P("expert", "dp"),
            P("expert", "dp"),
            P("expert", "dp"),
            P("expert", "dp"),
        ),
        check_vma=False,
    )
```

profile of v0, /device:TPU:0, one launch (start us, length us, event | category | flops | bytes accessed | tf_op | source)
XLA Modules:
  0.0 1419.0 jit_solution(7639999654146513691)
XLA Ops:
  15.4 146.4 %all-reduce.7.cloned.1.call-done = bf16[2363520]{0:T(1024)(128)(2,1)} async-done(((bf16[2363520]{0:T(1024)(128)(2,1)}), bf16[2363520]{0:T(1024)(128)(2,1)}) %all-reduce.7.cloned.1.call-update) | async-done | bytes 4727056
  161.7 12.0 reshape.724
  198.2 58.8 %all-gather.4.cloned.1.call-done = bf16[6,1024,384]{2,1,0:T(8,128)(2,1)} async-done(((bf16[6,128,384]{2,1,0:T(8,128)(2,1)}), bf16[6,1024,384]{2,1,0:T(8,128)(2,1)}) %all-gather.4.cloned.1.call-update) | async-done | bytes 4718608 | tf_op jit(solution)/shard_map/all_gather | solution.py:170
  263.6 75.1 %all-gather.6.cloned.1.call-done = bf16[6,1024,384]{1,2,0:T(8,128)(2,1)} async-done(((bf16[6,128,384]{1,2,0:T(8,128)(2,1)}), bf16[6,1024,384]{1,2,0:T(8,128)(2,1)}) %all-gather.6.cloned.1.call-update) | async-done | bytes 4718608 | tf_op jit(solution)/shard_map/all_gather | solution.py:169
  338.7 46.2 %while.50 = (s32[]{:T(128)}, f32[6,12,128]{2,1,0:T(8,128)S(1)}, f32[6,12,128]{2,1,0:T(8,128)S(1)}, s32[2]{0:T(128)S(1)}, s32[6]{0:T(128)S(1)}, /*index=5*/bf16[6...) while((s32[]{:T(128)}, f32[6,12,128]{2,1,0:T(8,128)S(1)}, ...), condition=%wide.region_4.5_spmd.clone, body=%wide.region_1.4_spmd.clone.sunk | while | flops 335528576 | bytes 42501340 | solution.py:190
  340.8 10.2 fusion.259
  351.0 11.0 exponential_reduce_fusion.2
  364.1 9.8 fusion.259
  374.0 10.9 exponential_reduce_fusion.2
  385.0 22.9 %while.51 = (s32[]{:T(128)}, f32[6,128,12,32]{1,3,2,0:T(8,128)S(1)}, s32[2]{0:T(128)S(1)}, bf16[6,1024,12,32]{1,3,2,0:T(8,128)(2,1)}, s32[6]{0:T(128)S(1)}, /*in...) while((s32[]{:T(128)}, ...), condition=%wide.region_6.7_spmd.clone, body=%wide.region_5.6_spmd.clone.sunk | while | flops 623906432 | bytes 8637152 | solution.py:207
  387.3 9.3 fusion.265
  398.7 9.3 fusion.265
  415.9 9.5 scatter_custom_fusion
  429.0 10.2 scatter_custom_fusion.1
  451.8 9.1 fusion.181
  465.6 11.0 fusion.104
  476.6 9.1 fusion.106
  485.7 8.4 all-to-all-done.2
  494.1 28.3 %fusion.76 = (bf16[4,2,384,1536]{3,2,0,1:T(8,128)(2,1)}, bf16[4,2,384,1536]{3,2,0,1:T(8,128)(2,1)}, bf16[4,2,384,1536]{3,2,0,1:T(8,128)(2,1)}) fusion(f32[2,4,384,1536]{3,2,1,0:T(8,128)} %fusion.104, f32[2,4,384,1536]{3,2,1,0:T(8,128)} %fusion.106, bf16[1,2,1536,384]{3,1,2,0:T(2,128)(2,1)} %bitcast.433, bf16[4,2,384,384]{3,2,1,0:T(8,128)(2,1)} %bitcast.30), kind=kOutput, calls=%fused_computation.87 | convolution fusion | flops 3694657536 | bytes 70778880 | tf_op jit(solution)/shard_map/nerd,efd->nerf/dot_general | solution.py:273
  522.4 7.7 convert_bitcast_fusion
  535.6 8.5 fusion.103
  544.2 7.8 fusion.100
  553.7 10.4 all-to-all-done.1
  569.2 9.7 multiply_convert_fusion
  584.2 7.2 gather_fusion
  595.1 8.2 multiply_reduce_fusion
  634.5 28.6 %while.52 = (s32[]{:T(128)}, f32[6,12,128]{2,1,0:T(8,128)S(1)}, s32[2]{0:T(128)S(1)}, s32[6]{0:T(128)S(1)}, bf16[6,1024,12,32]{1,3,2,0:T(8,128)(2,1)}, /*index=5...) while((s32[]{:T(128)}, f32[6,12,128]{2,1,0:T(8,128)S(1)}, ...), condition=%wide.region_25.26_spmd.clone, body=%wide.region_23.25_spmd.clone.sunk | while | flops 628044416 | bytes 44762352 | solution.py:337
  641.1 7.8 fusion.271
  655.3 7.8 fusion.271
  668.7 96.7 %while.53 = (s32[]{:T(128)}, f32[6,128,12,32]{1,3,2,0:T(8,128)S(1)}, bf16[6,1024,12,32]{1,3,2,0:T(8,128)(2,1)}, bf16[6,1024,12,32]{1,3,2,0:T(8,128)(2,1)}, s32[2...) while((s32[]{:T(128)}, ...), condition=%wide.region_27.28_spmd.clone, body=%wide.region_26.27_spmd.clone.sunk | while | flops 1558187648 | bytes 146924880 | solution.py:369
  670.1 9.3 fusion.282
  680.9 10.9 fusion.283
  707.1 10.0 bitcast_dynamic-update-slice_fusion.5
  718.4 9.3 fusion.282
  729.1 10.9 fusion.283
  755.4 10.1 bitcast_dynamic-update-slice_fusion.5
  765.4 8.5 copy.251
  779.9 8.8 fusion.93
  788.8 12.6 copy.269
  801.5 7.8 fusion.94
  821.2 8.6 copy.253
  835.8 35.2 %pad_maximum_fusion = bf16[2,1769472]{1,0:T(2,128)(2,1)} fusion(bf16[2,589824]{1,0:T(2,128)(2,1)} %bitcast.416, bf16[2,589824]{1,0:T(2,128)(2,1)} %bitcast.418, bf16[2,589824]{1,0:T(2,128)(2,1)} %bitcast.417), kind=kLoop, calls=%fused_computation.103 | loop fusion | flops 21233664 | bytes 14155776 | tf_op jit(solution)/shard_map/concatenate | solution.py:424
  889.1 84.3 %reduce-scatter.10.cloned.1.call-done = bf16[128,2304]{1,0:T(8,128)(2,1)} async-done(((bf16[1024,2304]{1,0:T(8,128)(2,1)}), bf16[128,2304]{1,0:T(8,128)(2,1)}) %reduce-scatter.10.cloned.1.call-update) | async-done | bytes 589840
  983.6 12.2 concatenate.25
  995.8 14.0 reshape.746
  1009.9 201.1 %all-reduce.11.cloned.1.call-done = bf16[2,1769472]{1,0:T(2,128)(2,1)} async-done(((bf16[2,1769472]{1,0:T(2,128)(2,1)}), bf16[2,1769472]{1,0:T(2,128)(2,1)}) %all-reduce.11.cloned.1.call-update) | async-done | bytes 7077904
  1211.0 14.4 %multiply_add_fusion.1 = (f32[2,221184]{1,0:T(2,128)}, f32[2,221184]{1,0:T(2,128)}, f32[2,221184]{1,0:T(2,128)}, f32[2,221184]{1,0:T(2,128)}, f32[2,221184]{1,0:T(2,128)}) fusion(f32[2,221184]{1,0:T(2,128)} %param.31, f32[2,221184]{1,0:T(2,128)S(1)} %copy-done.22, f32[2,221184]{1,0:T(2,128)} %param.30, f32[2,221184]{1,0:T(2,128)} %param.29, ...), kind=kLoop, calls=%fused_computation.143 | loop fusion | flops 7962624 | bytes 16809988 | tf_op jit(solution)/shard_map/add | solution.py:109
  1226.8 182.6 %all-reduce.9.cloned.1.call-done = f32[2363520]{0:T(1024)} async-done(((f32[2363520]{0:T(1024)}), f32[2363520]{0:T(1024)}) %all-reduce.9.cloned.1.call-update) | async-done | bytes 9454096
  (373 shorter events, 231.9 us)
Async XLA Ops:
  7.2 154.5 %all-reduce.7.cloned.1.call-start = ((), (), s32[]{:S(2)}) async-start(), calls=%async_computation.9 | async-start | bytes 9457664
  14.1 242.8 %all-gather.4.cloned.1.call-start = ((), (), s32[]{:S(2)}) async-start(), calls=%async_computation.6 | async-start | bytes 5308416 | tf_op jit(solution)/shard_map/all_gather | solution.py:170
  15.3 159.6 %copy-start.52 = (f32[768]{0:T(1024)}, f32[768]{0:T(1024)S(1)}, u32[]{:S(2)}) copy-start(f32[768]{0:T(1024)S(1)} %get-tuple-element.658) | copy-start | bytes 9220
  174.9 4.9 copy-start.57
  174.9 235.5 %copy-start.66 = (f32[384]{0:T(512)}, f32[384]{0:T(512)S(1)}, u32[]{:S(2)}) copy-start(f32[384]{0:T(512)S(1)} %get-tuple-element.530) | copy-start | bytes 4612
  177.5 161.2 %all-gather.6.cloned.1.call-start = ((), (), s32[]{:S(2)}) async-start(), calls=%async_computation.7 | async-start | bytes 5308416 | tf_op jit(solution)/shard_map/all_gather | solution.py:169
  183.4 268.3 %all-gather.8.cloned.1.call-start = ((), (), s32[]{:S(2)}) async-start(), calls=%async_computation.8 | async-start | bytes 7962624 | tf_op jit(solution)/shard_map/all_gather | solution.py:137
  338.7 46.3 %copy-start.37 = (f32[6,128,12,32]{1,3,2,0:T(8,128)S(1)}, f32[6,128,12,32]{1,3,2,0:T(8,128)}, u32[]{:S(2)}) copy-start(f32[6,128,12,32]{1,3,2,0:T(8,128)} %custom-call.2) | copy-start | bytes 3538948
  411.6 35.2 %copy-start.1 = (bf16[768,384]{1,0:T(8,128)(2,1)}, bf16[768,384]{1,0:T(8,128)(2,1)S(1)}, u32[]{:S(2)}) copy-start(bf16[768,384]{1,0:T(8,128)(2,1)S(1)} %multiply_convert_fusion.6) | copy-start | bytes 1769476
  413.0 192.8 %copy-start.54 = (f32[768]{0:T(1024)}, f32[768]{0:T(1024)S(1)}, u32[]{:S(2)}) copy-start(f32[768]{0:T(1024)S(1)} %fusion.171) | copy-start | bytes 9220
  425.4 35.5 %all-to-all-start = ((bf16[8,384,384]{2,1,0:T(8,128)(2,1)}), bf16[8,384,384]{2,1,0:T(8,128)(2,1)S(1)}, u32[]{:S(2)}, u32[]{:S(2)}) async-start(bf16[8,384,384]{2,1,0:T(8,128)(2,1)} %bitcast.421), calls=%async_computation | async-start | bytes 4718592 | tf_op jit(solution)/shard_map/all_to_all | solution.py:234
  439.4 7.3 copy-start.63
  439.5 7.3 copy-start.61
  460.9 15.7 %copy-start.5 = (bf16[8,384,384]{2,1,0:T(8,128)(2,1)}, bf16[8,384,384]{2,1,0:T(8,128)(2,1)S(1)}, u32[]{:S(2)}) copy-start(bf16[8,384,384]{2,1,0:T(8,128)(2,1)S(1)} %all-to-all-done) | copy-start | bytes 7077892
  460.9 33.2 %all-to-all-start.2 = ((bf16[8,384,384]{2,1,0:T(8,128)(2,1)}), bf16[8,384,384]{2,1,0:T(8,128)(2,1)}, u32[]{:S(2)}, u32[]{:S(2)}) async-start(bf16[8,384,384]{2,1,0:T(8,128)(2,1)} %bitcast.419), calls=%async_computation.2 | async-start | bytes 4718592 | tf_op jit(solution)/shard_map/all_to_all | solution.py:263
  465.6 11.0 copy-start.19
  494.1 28.3 %copy-start.28 = (bf16[2,589824]{1,0:T(2,128)(2,1)S(1)}, bf16[2,589824]{1,0:T(2,128)(2,1)}, u32[]{:S(2)}) copy-start(bf16[2,589824]{1,0:T(2,128)(2,1)} %get-tuple-element.638) | copy-start | bytes 7077892
  531.8 32.3 %all-to-all-start.1 = ((bf16[8,384,384]{2,1,0:T(8,128)(2,1)}), bf16[8,384,384]{2,1,0:T(8,128)(2,1)S(1)}, u32[]{:S(2)}, u32[]{:S(2)}) async-start(bf16[8,384,384]{2,1,0:T(8,128)(2,1)} %bitcast.422), calls=%async_computation.1 | async-start | bytes 4718592 | tf_op jit(solution)/shard_map/all_to_all | solution.py:244
  535.6 8.5 copy-start.20
  565.5 41.8 %all-to-all-start.3 = ((bf16[8,384,384]{2,1,0:T(8,128)(2,1)}), bf16[8,384,384]{2,1,0:T(8,128)(2,1)S(1)}, u32[]{:S(2)}, u32[]{:S(2)}) async-start(bf16[8,384,384]{2,1,0:T(8,128)(2,1)} %bitcast.420), calls=%async_computation.3 | async-start | bytes 4718592 | tf_op jit(solution)/shard_map/all_to_all | solution.py:292
  569.2 9.8 copy-start.8
  569.2 316.1 %reduce-scatter.8.cloned.1.call-start = ((), (), s32[]{:S(2)}) async-start(), calls=%async_computation.10 | async-start | bytes 5308416
  578.9 4.7 copy-start.33
  579.0 4.7 copy-start.64
  607.3 19.9 %copy-start.47 = (bf16[768,8]{0,1:T(8,128)(2,1)}, bf16[768,8]{0,1:T(8,128)(2,1)S(1)}, u32[]{:S(2)}) copy-start(bf16[768,8]{0,1:T(8,128)(2,1)S(1)} %multiply_convert_fusion.9) | copy-start | bytes 36868
  620.1 4.0 copy-start.30
  691.8 3.7 copy-start
  701.1 6.0 copy-start.18
  740.0 3.7 copy-start
  749.4 6.0 copy-start.18
  779.9 193.6 %reduce-scatter.10.cloned.1.call-start = ((), (), s32[]{:S(2)}) async-start(), calls=%async_computation.11 | async-start | bytes 5308416
  788.8 12.7 copy-start.6
  788.8 24.2 %slice-start = ((s8[9437184]{0:T(1024)(128)(4,1)}), s8[4194304]{0:T(1024)(128)(4,1)S(1)}, s32[]{:S(2)}) async-start(s8[9437184]{0:T(1024)(128)(4,1)} %bitcast.444), calls=%async_computation.14 | async-start | bytes 8388608
  801.5 11.6 slice-start.1
  801.5 11.6 slice-start.2
  835.7 375.2 %all-reduce.11.cloned.1.call-start = ((), (), s32[]{:S(2)}) async-start(), calls=%async_computation.13 | async-start | bytes 14155776
  871.0 538.3 %all-reduce.9.cloned.1.call-start = ((), (), s32[]{:S(2)}) async-start(), calls=%async_computation.12 | async-start | bytes 18915328
  873.2 4.4 copy-start.32
  880.1 3.7 copy-start.12
  880.1 3.7 copy-start.27
  975.3 3.2 copy-start.15
  1009.8 201.1 %copy-start.22 = (f32[2,221184]{1,0:T(2,128)S(1)}, f32[2,221184]{1,0:T(2,128)}, u32[]{:S(2)}) copy-start(f32[2,221184]{1,0:T(2,128)} %param.28) | copy-start | bytes 5308420
  1009.9 215.5 %copy-start.13 = (f32[768,384]{1,0:T(8,128)S(1)}, f32[768,384]{1,0:T(8,128)}, u32[]{:S(2)}) copy-start(f32[768,384]{1,0:T(8,128)} %copy-done.11) | copy-start | bytes 3538948
  1211.0 14.4 %copy-start.23 = (f32[768,384]{1,0:T(8,128)S(1)}, f32[768,384]{1,0:T(8,128)}, u32[]{:S(2)}) copy-start(f32[768,384]{1,0:T(8,128)} %get-tuple-element.669) | copy-start | bytes 3538948
  1225.3 184.0 %copy-start.35 = (f32[73860]{0:T(1024)S(1)}, f32[73860]{0:T(1024)}, u32[]{:S(2)}) copy-start(f32[73860]{0:T(1024)} %param.24) | copy-start | bytes 886324
  1225.3 184.0 %copy-start.41 = (f32[73860]{0:T(1024)S(1)}, f32[73860]{0:T(1024)}, u32[]{:S(2)}) copy-start(f32[73860]{0:T(1024)} %param.27) | copy-start | bytes 886324
  1225.3 184.0 %copy-start.42 = (f32[73860]{0:T(1024)S(1)}, f32[73860]{0:T(1024)}, u32[]{:S(2)}) copy-start(f32[73860]{0:T(1024)} %param.26) | copy-start | bytes 886324
  1225.3 184.0 %copy-start.43 = (f32[73860]{0:T(1024)S(1)}, f32[73860]{0:T(1024)}, u32[]{:S(2)}) copy-start(f32[73860]{0:T(1024)} %param.25) | copy-start | bytes 886324
  (42 other events, 88.6 us)
Sparse Core Ops, SparseCore 0:
  14.2 147.4 all-reduce.6
  177.6 79.2 all-gather.3
  259.6 79.1 all-gather.5
  341.4 106.9 all-gather.7
  780.0 94.8 reduce-scatter.7
  878.4 95.0 reduce-scatter.9
  977.3 233.6 all-reduce.10
  1217.9 191.4 all-reduce.8
where the time goes:
time: 1430 us; the launch traced here: 1420 us
  waiting for transfers between devices  767 us (54%)
  matrix products  302 us (21%)
  local copies, waits for them, and re-layouts  185 us (13%)
  other arithmetic  126 us (9%)
  between operations  16.7 us (1%)
  starting transfers between devices  16.3 us (1%)
    unnamed x13, waiting for transfers between devices  615 us
    all_gather x1, waiting for transfers between devices, local(): lax.all_gather(key_rot.reshape(flat_shape), 'dp', axis=1, tiled=True)  75.1 us
    unnamed x164, local copies, waits for them, and re-layouts  68 us
    all_gather x1, waiting for transfers between devices, local(): lax.all_gather(value_low.reshape(flat_shape), 'dp', axis=1, tiled=True)  58.8 us
    dot_general x6, matrix products, masked_scores(): jnp.einsum('sqhd,skhd->shqk', query_block, key_block, preferred_element_t...  54.2 us
    concatenate x1, other arithmetic, local(): jnp.concatenate([grad_e_gate.reshape(local_experts, -1), grad_e_up.reshap...  35.2 us
  transfers between devices with their start and end apart: 12, of which 8 were waited for; matrix products, arithmetic and copies ran while one was open for 26% of the time, Pallas kernels for 0%

commit v1 on v0

v1 whole, which is shorter than its diff:
```python
import functools
import math

import jax
import jax.numpy as jnp
from jax import lax
from jax.experimental import pallas as pl
from jax.experimental.pallas import tpu as pltpu
from jax.sharding import PartitionSpec as P

D = 384
HEADS = 12
HEAD_DIM = 32
FF = 1536
EXPERTS = 8
TOP = 2
SEG = 128
SERIES_DEV = 6
STEP = 8
TOK_DEV = 768
CAP = 384
ROW_PAD = 16
MISC = 128
UNITS_ALL = SERIES_DEV * HEADS
QBLOCK = 256
MIB = 1 << 20

eps_norm = 1e-06
beta_one = 0.5
beta_two = 0.5
learn_rate = 0.02
weight_decay = 0.1
eps_adam = 1e-08
average_keep = 0.9
rope_base = 10000.0
neg_fill = -1e30

MESH = pl.DeviceIdType.MESH
F32 = jnp.float32
BF16 = jnp.bfloat16


def adamw_update(weights, grads, first, second, average):
    first_new = beta_one * first + (1.0 - beta_one) * grads
    second_new = beta_two * second + (1.0 - beta_two) * grads * grads
    first_hat = first_new / (1.0 - beta_one**STEP)
    second_hat = second_new / (1.0 - beta_two**STEP)
    weights_new = weights - learn_rate * (
        first_hat / (jnp.sqrt(second_hat) + eps_adam) + weight_decay * weights
    )
    average_new = average_keep * average + (1.0 - average_keep) * weights_new
    return (first_new, second_new, weights_new, average_new)


def dot(left, right, left_dim=1, right_dim=0):
    return lax.dot_general(
        left, right, (((left_dim,), (right_dim,)), ((), ())), preferred_element_type=F32
    )


class Grid:
    def __init__(self, ndp, nex):
        self.ndp, self.nex = ndp, nex
        self.nz = math.gcd(ndp, 4)
        self.ny = ndp // self.nz
        self.nc = math.gcd(nex, 2)
        self.nx = nex // self.nc
        self.ndev = ndp * nex
        self.units = -(-UNITS_ALL // ndp)
        spans = [
            [u // HEADS for u in range(self.units * o, min(self.units * (o + 1), UNITS_ALL))]
            for o in range(ndp)
        ]
        self.owned = [sorted(set(s)) for s in spans]
        self.slots = max(len(s) for s in self.owned)

    def first_series(self, owner):
        return (owner * self.units) // HEADS

    def holds(self, owner, slot):
        begin = owner * self.units
        end = jnp.minimum(begin + self.units, UNITS_ALL)
        return (begin // HEADS + slot) * HEADS < end


def remote(src, dst, send, recv, target):
    return pltpu.make_async_remote_copy(
        src_ref=src,
        dst_ref=dst,
        send_sem=send,
        recv_sem=recv,
        device_id=target,
        device_id_type=MESH,
    )


def greet(peers):
    barrier = pltpu.get_barrier_semaphore()
    for peer in peers:
        pl.semaphore_signal(barrier, inc=1, device_id=peer, device_id_type=MESH)
    pl.semaphore_wait(barrier, len(peers))


def any_spec():
    return pl.BlockSpec(memory_space=pl.ANY)


def far_first(n):
    return sorted(range(1, n), key=lambda d: -min(d, n - d))


def comm_params(number):
    return pltpu.CompilerParams(collective_id=number, has_side_effects=True)


def first_exchange(grid, tokens, shard, cot, ranks):
    ndp, nex, nz, ny, nx, nc = grid.ndp, grid.nex, grid.nz, grid.ny, grid.nx, grid.nc

    def kernel(tok, shd, cot_in, rank_in, tok_out, dense_out, cot_out, rank_out,
               t_send, t_recv, d_send, d_recv, e_send, e_recv, loc):
        dp, ex = lax.axis_index("dp"), lax.axis_index("expert")
        z, y = dp // ny, lax.rem(dp, ny)
        x, c = ex // nc, lax.rem(ex, nc)

        def place(zz, yy, xx, cc):
            return (zz * ny + yy, xx * nc + cc)

        def slot_of(zz, yy, xx, cc):
            return (zz * ny + yy) * nex + xx * nc + cc

        def off(value, by, n):
            return lax.rem(value + by, n)

        peers = [(off(dp, d, ndp), ex) for d in range(1, ndp)]
        peers += [(dp, off(ex, d, nex)) for d in range(1, nex)]
        greet(peers)

        local = []

        def keep(src, dst):
            copy = pltpu.make_async_copy(src, dst, loc.at[len(local)])
            copy.start()
            local.append(copy)

        sends = []

        def dense_send(src, slot, target):
            copy = remote(src, dense_out.at[slot], d_send.at[len(sends)], d_recv.at[slot], target)
            copy.start()
            sends.append(copy)

        def dense_wait(slot):
            remote(shd, dense_out.at[slot], d_send.at[0], d_recv.at[slot], (dp, ex)).wait_recv()

        own = slot_of(z, y, x, c)
        for dz in far_first(nz):
            dense_send(shd, own, place(off(z, dz, nz), y, x, c))
        for dy in range(1, ny):
            dense_send(shd, own, place(z, off(y, dy, ny), x, c))
        for dx in range(1, nx):
            dense_send(shd, own, place(z, y, off(x, dx, nx), c))
        for dc in range(1, nc):
            dense_send(shd, own, place(z, y, x, off(c, dc, nc)))

        e_sends = []
        for d in far_first(nex):
            target = (dp, off(ex, d, nex))
            for n, (src, dst) in enumerate(((cot_in, cot_out), (rank_in, rank_out))):
                copy = remote(src, dst.at[ex], e_send.at[d - 1, n], e_recv.at[d - 1, n], target)
                copy.start()
                e_sends.append(copy)

        def token_copy(d, slot, src_series, sender, target):
            return remote(
                tok.at[src_series],
                tok_out.at[slot, sender],
                t_send.at[d - 1, slot],
                t_recv.at[d - 1, slot],
                (target, ex),
            )

        for d in far_first(ndp):
            target = off(dp, d, ndp)
            for slot in range(grid.slots):

                @pl.when(grid.holds(target, slot))
                def _():
                    token_copy(d, slot, grid.first_series(target) + slot, dp, target).start()

        for slot in range(grid.slots):

            @pl.when(grid.holds(dp, slot))
            def _():
                copy = pltpu.make_async_copy(
                    tok.at[grid.first_series(dp) + slot], tok_out.at[slot, dp], loc.at[8 + slot]
                )
                copy.start()
                copy.wait()

        keep(shd, dense_out.at[own])
        keep(cot_in, cot_out.at[ex])
        keep(rank_in, rank_out.at[ex])

        zs = [0] + far_first(nz)[::-1]
        for dz in zs[1:]:
            zz = off(z, nz - dz, nz)
            slot = slot_of(zz, y, x, c)
            dense_wait(slot)
            for dy in range(1, ny):
                dense_send(dense_out.at[slot], slot, place(z, off(y, dy, ny), x, c))
            for dx in range(1, nx):
                dense_send(dense_out.at[slot], slot, place(z, y, off(x, dx, nx), c))
            for dc in range(1, nc):
                dense_send(dense_out.at[slot], slot, place(z, y, x, off(c, dc, nc)))
        for dy in range(1, ny):
            for dz in zs:
                slot = slot_of(off(z, nz - dz, nz), off(y, ny - dy, ny), x, c)
                dense_wait(slot)
                for dx in range(1, nx):
                    dense_send(dense_out.at[slot], slot, place(z, y, off(x, dx, nx), c))
                for dc in range(1, nc):
                    dense_send(dense_out.at[slot], slot, place(z, y, x, off(c, dc, nc)))
        for dx in range(1, nx):
            for dy in range(ny):
                for dz in zs:
                    slot = slot_of(
                        off(z, nz - dz, nz), off(y, ny - dy, ny), off(x, nx - dx, nx), c
                    )
                    dense_wait(slot)
                    for dc in range(1, nc):
                        dense_send(dense_out.at[slot], slot, place(z, y, x, off(c, dc, nc)))
        for dc in range(1, nc):
            for dx in range(nx):
                for dy in range(ny):
                    for dz in zs:
                        dense_wait(
                            slot_of(
                                off(z, nz - dz, nz),
                                off(y, ny - dy, ny),
                                off(x, nx - dx, nx),
                                off(c, nc - dc, nc),
                            )
                        )
        for d in range(1, ndp):
            for slot in range(grid.slots):

                @pl.when(grid.holds(dp, slot))
                def _():
                    token_copy(d, slot, 0, dp, off(dp, d, ndp)).wait_recv()

                @pl.when(grid.holds(off(dp, d, ndp), slot))
                def _():
                    token_copy(d, slot, 0, dp, off(dp, d, ndp)).wait_send()

        for copy in e_sends:
            copy.wait()
        for copy in sends:
            copy.wait_send()
        for copy in local:
            copy.wait()

    seg, width = tokens.shape[1:]
    dma = pltpu.SemaphoreType.DMA
    return pl.pallas_call(
        kernel,
        out_shape=(
            jax.ShapeDtypeStruct((grid.slots, ndp, seg, width), tokens.dtype),
            jax.ShapeDtypeStruct((grid.ndev,) + shard.shape, shard.dtype),
            jax.ShapeDtypeStruct((nex,) + cot.shape, cot.dtype),
            jax.ShapeDtypeStruct((nex,) + ranks.shape, ranks.dtype),
        ),
        in_specs=[any_spec()] * 4,
        out_specs=(any_spec(),) * 4,
        scratch_shapes=[
            dma((ndp - 1, grid.slots)),
            dma((ndp - 1, grid.slots)),
            dma((grid.ndev,)),
            dma((grid.ndev,)),
            dma((nex - 1, 2)),
            dma((nex - 1, 2)),
            dma((16,)),
        ],
        compiler_params=comm_params(0),
        name="first_exchange",
    )(tokens, shard, cot, ranks)


def heads_out(grid, values):
    ndp = grid.ndp

    def kernel(src, dst, send, recv, loc):
        dp, ex = lax.axis_index("dp"), lax.axis_index("expert")
        greet([(lax.rem(dp + d, ndp), ex) for d in range(1, ndp)])
        copies = []
        for d in far_first(ndp):
            target = lax.rem(dp + d, ndp)
            lanes = pl.ds(pl.multiple_of(target * SEG, SEG), SEG)
            copy = remote(
                src.at[:, :, lanes], dst.at[dp], send.at[d - 1], recv.at[d - 1], (target, ex)
            )
            copy.start()
            copies.append(copy)
        mine = pltpu.make_async_copy(
            src.at[:, :, pl.ds(pl.multiple_of(dp * SEG, SEG), SEG)], dst.at[dp], loc
        )
        mine.start()
        mine.wait()
        for copy in copies:
            copy.wait()

    dma = pltpu.SemaphoreType.DMA
    return pl.pallas_call(
        kernel,
        out_shape=jax.ShapeDtypeStruct((ndp,) + values.shape[:2] + (SEG,), values.dtype),
        in_specs=[any_spec()],
        out_specs=any_spec(),
        scratch_shapes=[dma((ndp - 1,)), dma((ndp - 1,)), dma],
        compiler_params=comm_params(1),
        name="heads_out",
    )(values)


def heads_in(grid, values):
    ndp = grid.ndp

    def kernel(src, dst, send, recv, loc):
        dp, ex = lax.axis_index("dp"), lax.axis_index("expert")
        greet([(lax.rem(dp + d, ndp), ex) for d in range(1, ndp)])
        lanes = pl.ds(pl.multiple_of(dp * SEG, SEG), SEG)
        copies = []
        for d in far_first(ndp):
            target = lax.rem(dp + d, ndp)
            copy = remote(
                src.at[target], dst.at[:, :, lanes], send.at[d - 1], recv.at[d - 1], (target, ex)
            )
            copy.start()
            copies.append(copy)
        mine = pltpu.make_async_copy(src.at[dp], dst.at[:, :, lanes], loc)
        mine.start()
        mine.wait()
        for copy in copies:
            copy.wait()

    dma = pltpu.SemaphoreType.DMA
    return pl.pallas_call(
        kernel,
        out_shape=jax.ShapeDtypeStruct(values.shape[1:3] + (SEG * ndp,), values.dtype),
        in_specs=[any_spec()],
        out_specs=any_spec(),
        scratch_shapes=[dma((ndp - 1,)), dma((ndp - 1,)), dma],
        compiler_params=comm_params(2),
        name="heads_in",
    )(values)


def rows_back(grid, values):
    ndp = grid.ndp

    def kernel(src, dst, send, recv, loc):
        dp, ex = lax.axis_index("dp"), lax.axis_index("expert")
        greet([(lax.rem(dp + d, ndp), ex) for d in range(1, ndp)])

        def block(d, slot):
            target = lax.rem(dp + d, ndp)
            return remote(
                src.at[slot, target],
                dst.at[dp, slot],
                send.at[d - 1, slot],
                recv.at[d - 1, slot],
                (target, ex),
            )

        for slot in range(grid.slots):

            @pl.when(grid.holds(dp, slot))
            def _():
                for d in far_first(ndp):
                    block(d, slot).start()
                mine = pltpu.make_async_copy(src.at[slot, dp], dst.at[dp, slot], loc.at[slot])
                mine.start()
                mine.wait()

        for slot in range(grid.slots):
            for d in range(1, ndp):

                @pl.when(grid.holds(lax.rem(dp + ndp - d, ndp), slot))
                def _():
                    block(d, slot).wait_recv()

            @pl.when(grid.holds(dp, slot))
            def _():
                for d in range(1, ndp):
                    block(d, slot).wait_send()

    dma = pltpu.SemaphoreType.DMA
    return pl.pallas_call(
        kernel,
        out_shape=jax.ShapeDtypeStruct((ndp, grid.slots) + values.shape[2:], values.dtype),
        in_specs=[any_spec()],
        out_specs=any_spec(),
        scratch_shapes=[
            dma((ndp - 1, grid.slots)),
            dma((ndp - 1, grid.slots)),
            dma((grid.slots,)),
        ],
        compiler_params=comm_params(3),
        name="rows_back",
    )(values)


def expert_gather(grid, rows, gates):
    nex, nx, nc = grid.nex, grid.nx, grid.nc
    parts = 3
    extent = TOK_DEV // parts

    def kernel(src, gate, dst, gate_dst, send, recv, fsend, g_send, g_recv, loc):
        dp, ex = lax.axis_index("dp"), lax.axis_index("expert")
        x, c = ex // nc, lax.rem(ex, nc)
        greet([(dp, lax.rem(ex + d, nex)) for d in range(1, nex)])
        sends = []

        def go(ref, slot, part, sem, target):
            rows_part = pl.ds(part * extent, extent)
            copy = remote(
                ref, dst.at[slot, rows_part], sem, recv.at[slot, part], (dp, target)
            )
            copy.start()
            sends.append(copy)

        def arrived(slot, part):
            rows_part = pl.ds(part * extent, extent)
            remote(
                src.at[rows_part], dst.at[slot, rows_part], send.at[0, 0], recv.at[slot, part],
                (dp, ex),
            ).wait_recv()

        gate_copies = []
        for d in range(1, nex):
            copy = remote(
                gate, gate_dst.at[ex], g_send.at[d - 1], g_recv.at[d - 1],
                (dp, lax.rem(ex + d, nex)),
            )
            copy.start()
            gate_copies.append(copy)
        for part in range(parts):
            for dx in range(1, nx):
                target = lax.rem(x + dx, nx) * nc + c
                go(src.at[pl.ds(part * extent, extent)], ex, part, send.at[dx - 1, part], target)
        for part in range(parts):
            for dc in range(1, nc):
                target = x * nc + lax.rem(c + dc, nc)
                go(
                    src.at[pl.ds(part * extent, extent)], ex, part,
                    send.at[nx - 1 + dc - 1, part], target,
                )
        own = [
            pltpu.make_async_copy(src, dst.at[ex], loc.at[0]),
            pltpu.make_async_copy(gate, gate_dst.at[ex], loc.at[1]),
        ]
        for copy in own:
            copy.start()
        for part in range(parts):
            for dx in range(1, nx):
                slot = lax.rem(x + nx - dx, nx) * nc + c
                arrived(slot, part)
                for dc in range(1, nc):
                    target = x * nc + lax.rem(c + dc, nc)
                    go(
                        dst.at[slot, pl.ds(part * extent, extent)], slot, part,
                        fsend.at[dx - 1, part], target,
                    )
        for part in range(parts):
            for dc in range(1, nc):
                for dx in range(nx):
                    arrived(lax.rem(x + nx - dx, nx) * nc + lax.rem(c + nc - dc, nc), part)
        for copy in gate_copies + own:
            copy.wait()
        for copy in sends:
            copy.wait_send()

    dma = pltpu.SemaphoreType.DMA
    return pl.pallas_call(
        kernel,
        out_shape=(
            jax.ShapeDtypeStruct((nex,) + rows.shape, rows.dtype),
            jax.ShapeDtypeStruct((nex,) + gates.shape, gates.dtype),
        ),
        in_specs=[any_spec()] * 2,
        out_specs=(any_spec(),) * 2,
        scratch_shapes=[
            dma((nx + nc, parts)),
            dma((nex, parts)),
            dma((nx, parts)),
            dma((nex - 1,)),
            dma((nex - 1,)),
            dma((2,)),
        ],
        compiler_params=comm_params(4),
        name="expert_gather",
    )(rows, gates)


def turn(values, cosine, sine):
    first, second = values[: HEAD_DIM // 2], values[HEAD_DIM // 2 :]
    return jnp.concatenate(
        [first * cosine - second * sine, second * cosine + first * sine], axis=0
    )


def allowed_mask(extent, block, length):
    keys = lax.broadcasted_iota(jnp.int32, (extent, QBLOCK), 0)
    queries = lax.broadcasted_iota(jnp.int32, (extent, QBLOCK), 1) + block * QBLOCK
    return (keys <= queries) & (keys < length)


def attend(grid, info, tok, weights, gain, cosine, sine):
    units, length = grid.units, tok.shape[1]
    blocks = length // QBLOCK

    def kernel(info_ref, tok_ref, w_ref, gain_ref, cos_ref, sin_ref,
               out_ref, act_ref, q_ref, k_ref, v_ref, lse_ref):
        i = pl.program_id(0)
        fresh = (i == 0) | (info_ref[0, i] != info_ref[0, jnp.maximum(i - 1, 0)])

        @pl.when(fresh)
        def _():
            residual = tok_ref[0].astype(F32)
            scale = lax.rsqrt(jnp.mean(residual * residual, axis=-1, keepdims=True) + eps_norm)
            act_ref[0] = (residual * scale * gain_ref[...]).astype(BF16)

        cos, sin = cos_ref[...], sin_ref[...]
        qkv = dot(w_ref[:, 0].reshape(3 * HEAD_DIM, D), act_ref[0], 1, 1)
        query = turn(qkv[:HEAD_DIM], cos, sin).astype(BF16)
        key_wide = turn(qkv[HEAD_DIM : 2 * HEAD_DIM], cos, sin)
        key = key_wide.astype(BF16)
        value = qkv[2 * HEAD_DIM :].astype(BF16)
        key_rows = key_wide.T.astype(BF16)
        q_ref[0], k_ref[0], v_ref[0] = query, key, value
        live = info_ref[2, i]
        for block in range(blocks):
            extent = QBLOCK * (block + 1)
            lanes = slice(QBLOCK * block, extent)
            scores = dot(key_rows[:extent], query[:, lanes]) * HEAD_DIM ** (-0.5)
            scores = jnp.where(allowed_mask(extent, block, live), scores, neg_fill)
            top = jnp.max(scores, axis=0, keepdims=True)
            probs = jnp.exp(scores - top)
            total = jnp.sum(probs, axis=0, keepdims=True)
            result = dot(value[:, :extent], probs.astype(BF16))
            out_ref[0, :, lanes] = (result * (1.0 / total)).astype(BF16)
            lse_ref[0, :, lanes] = top + jnp.log(total)

    def unit(i, info_ref):
        return (i, 0, 0)

    feature = jax.ShapeDtypeStruct((units, HEAD_DIM, length), BF16)
    flops = units * length * length * HEAD_DIM * 2 * 8
    return pl.pallas_call(
        kernel,
        out_shape=(
            feature,
            jax.ShapeDtypeStruct((grid.slots, length, D), BF16),
            feature,
            feature,
            feature,
            jax.ShapeDtypeStruct((units, 1, length), F32),
        ),
        grid_spec=pltpu.PrefetchScalarGridSpec(
            num_scalar_prefetch=1,
            grid=(units,),
            in_specs=[
                pl.BlockSpec((1, length, D), lambda i, n: (n[0, i], 0, 0)),
                pl.BlockSpec((3, 1, HEAD_DIM, D), lambda i, n: (0, n[1, i], 0, 0)),
                pl.BlockSpec((1, D), lambda i, n: (0, 0)),
                pl.BlockSpec((HEAD_DIM // 2, length), lambda i, n: (0, 0)),
                pl.BlockSpec((HEAD_DIM // 2, length), lambda i, n: (0, 0)),
            ],
            out_specs=(
                pl.BlockSpec((1, HEAD_DIM, length), unit),
                pl.BlockSpec((1, length, D), lambda i, n: (n[0, i], 0, 0)),
                pl.BlockSpec((1, HEAD_DIM, length), unit),
                pl.BlockSpec((1, HEAD_DIM, length), unit),
                pl.BlockSpec((1, HEAD_DIM, length), unit),
                pl.BlockSpec((1, 1, length), unit),
            ),
        ),
        compiler_params=pltpu.CompilerParams(vmem_limit_bytes=40 * MIB),
        cost_estimate=pl.CostEstimate(
            flops=flops, bytes_accessed=8 * MIB, transcendentals=units * length * length
        ),
        name="attend",
    )(info, tok, weights, gain, cosine, sine)


def attend_back(grid, info, act, weights, query, key, value, lse, grad_heads, cosine, sine):
    units, length = grid.units, act.shape[1]
    blocks = length // QBLOCK
    scale = HEAD_DIM ** (-0.5)

    def kernel(info_ref, act_ref, w_ref, q_ref, k_ref, v_ref, lse_ref, do_ref, cos_ref, sin_ref,
               back_ref, grad_ref, acc, dq, dk, dv):
        i = pl.program_id(0)
        live_unit = info_ref[3, i] == 1

        @pl.when((i == 0) | (info_ref[0, i] != info_ref[0, jnp.maximum(i - 1, 0)]))
        def _():
            acc[...] = jnp.zeros_like(acc)

        @pl.when(jnp.logical_not(live_unit))
        def _():
            grad_ref[...] = jnp.zeros_like(grad_ref)

        @pl.when(live_unit)
        def _():
            live = info_ref[2, i]
            query, key, value, grad = q_ref[0], k_ref[0], v_ref[0], do_ref[0]
            key_rows = key.astype(F32).T.astype(BF16)
            value_rows = value.astype(F32).T.astype(BF16)
            dk[...] = jnp.zeros_like(dk)
            dv[...] = jnp.zeros_like(dv)
            for block in range(blocks):
                extent = QBLOCK * (block + 1)
                lanes = slice(QBLOCK * block, extent)
                scores = dot(key_rows[:extent], query[:, lanes]) * scale
                scores = jnp.where(allowed_mask(extent, block, live), scores, neg_fill)
                probs = jnp.exp(scores - lse_ref[0, :, lanes])
                grad_probs = dot(value_rows[:extent], grad[:, lanes])
                delta = jnp.sum(probs * grad_probs, axis=0, keepdims=True)
                grad_scores = (probs * (grad_probs - delta)).astype(BF16)
                probs_low = probs.astype(BF16)
                dq[:, lanes] = dot(key[:, :extent], grad_scores)
                dk[:, :extent] += dot(query[:, lanes], grad_scores, 1, 1)
                dv[:, :extent] += dot(grad[:, lanes], probs_low, 1, 1)
            cos, sin = cos_ref[...], -sin_ref[...]
            stacked = jnp.concatenate(
                [
                    turn(dq[...] * scale, cos, sin),
                    turn(dk[...] * scale, cos, sin),
                    dv[...],
                ],
                axis=0,
            ).astype(BF16)
            w_rows = w_ref[:, 0].reshape(3 * HEAD_DIM, D)
            grad_ref[:, 0] = dot(stacked, act_ref[0]).reshape(3, HEAD_DIM, D)
            acc[...] += dot(stacked, w_rows, 0, 0)
            back_ref[0] = acc[...].astype(BF16)

    def unit(i, n):
        return (jnp.minimum(i, units - 1), 0, 0)

    feature = pl.BlockSpec((1, HEAD_DIM, length), unit)
    table = pl.BlockSpec((HEAD_DIM // 2, length), lambda i, n: (0, 0))
    return pl.pallas_call(
        kernel,
        out_shape=(
            jax.ShapeDtypeStruct((grid.slots, length, D), BF16),
            jax.ShapeDtypeStruct((3, HEADS, HEAD_DIM, D), F32),
        ),
        grid_spec=pltpu.PrefetchScalarGridSpec(
            num_scalar_prefetch=1,
            grid=(HEADS,),
            in_specs=[
                pl.BlockSpec((1, length, D), lambda i, n: (n[0, i], 0, 0)),
                pl.BlockSpec((3, 1, HEAD_DIM, D), lambda i, n: (0, n[1, i], 0, 0)),
                feature,
                feature,
                feature,
                pl.BlockSpec((1, 1, length), unit),
                feature,
                table,
                table,
            ],
            out_specs=(
                pl.BlockSpec((1, length, D), lambda i, n: (n[0, i], 0, 0)),
                pl.BlockSpec((3, 1, HEAD_DIM, D), lambda i, n: (0, n[1, i], 0, 0)),
            ),
            scratch_shapes=[
                pltpu.VMEM((length, D), F32),
                pltpu.VMEM((HEAD_DIM, length), F32),
                pltpu.VMEM((HEAD_DIM, length), F32),
                pltpu.VMEM((HEAD_DIM, length), F32),
            ],
        ),
        compiler_params=pltpu.CompilerParams(vmem_limit_bytes=40 * MIB),
        cost_estimate=pl.CostEstimate(
            flops=units * length * length * HEAD_DIM * 2 * 20,
            bytes_accessed=12 * MIB,
            transcendentals=units * length * length,
        ),
        name="attend_back",
    )(info, act, weights, query, key, value, lse, grad_heads, cosine, sine)


def experts_step(weights, act_all, cot_all, rank_row, rank_col, gates):
    sources, rows = act_all.shape[:2]
    local = weights.shape[0]
    parts = FF // D

    def kernel(w_ref, act_ref, cot_ref, rrow_ref, rcol_ref, gate_ref,
               routed_ref, gin_ref, ggate_ref, x_ref, dg_ref, du_ref, hid_ref, dy_ref):
        act, cot = act_ref[0], cot_ref[0]
        slot_down = lax.broadcasted_iota(jnp.int32, (CAP, rows), 0)
        slot_across = lax.broadcasted_iota(jnp.int32, (rows, CAP), 1)
        routed = jnp.zeros((rows, D), F32)
        grad_in = jnp.zeros((rows, D), F32)
        for e in range(local):
            pick = slot_down == rrow_ref[0, e : e + 1, :]
            pick_low = pick.astype(F32).astype(BF16)
            spread = (slot_across == rcol_ref[0, :, e : e + 1]).astype(F32).astype(BF16)
            taken = dot(pick_low, act).astype(BF16)
            grad_rows = dot(pick_low, cot)
            gate = jnp.sum(jnp.where(pick, gate_ref[0, e : e + 1, :], 0.0), axis=1, keepdims=True)
            grad_result = (gate * grad_rows).astype(BF16)
            x_ref[e, 0] = taken
            dy_ref[e, 0] = grad_result
            result = jnp.zeros((CAP, D), F32)
            grad_taken = jnp.zeros((CAP, D), F32)
            for part in range(parts):
                lanes = slice(part * D, (part + 1) * D)
                w_gate = w_ref[e, 0:D, lanes]
                w_up = w_ref[e, D : 2 * D, lanes]
                w_down = w_ref[e, 2 * D : 3 * D, lanes]
                gate_lin = dot(taken, w_gate)
                up_lin = dot(taken, w_up)
                sig = jax.nn.sigmoid(gate_lin)
                silu = gate_lin * sig
                hidden = (silu * up_lin).astype(BF16)
                result += dot(hidden, w_down)
                grad_hidden = dot(grad_result, w_down, 1, 1)
                slope = sig * (1.0 + gate_lin * (1.0 - sig))
                grad_gate = (grad_hidden * up_lin * slope).astype(BF16)
                grad_up = (grad_hidden * silu).astype(BF16)
                hid_ref[e, 0, :, lanes] = hidden
                dg_ref[e, 0, :, lanes] = grad_gate
                du_ref[e, 0, :, lanes] = grad_up
                grad_taken += dot(grad_gate, w_gate, 1, 1) + dot(grad_up, w_up, 1, 1)
            result = result.astype(BF16).astype(F32)
            grad_gate_slot = jnp.sum(grad_rows * result, axis=1, keepdims=True)
            ggate_ref[0, e : e + 1, :] = jnp.sum(
                jnp.where(pick, grad_gate_slot, 0.0), axis=0, keepdims=True
            )
            routed += dot(spread, (gate * result).astype(BF16))
            grad_in += dot(spread, grad_taken.astype(BF16))
        routed_ref[0] = routed.astype(BF16)
        gin_ref[0] = grad_in.astype(BF16)

    def per_source(*tail):
        return pl.BlockSpec((1,) + tail, lambda s: (s,) + (0,) * len(tail))

    def kept(width):
        return pl.BlockSpec((local, 1, CAP, width), lambda s: (0, s, 0, 0))

    def kept_shape(width):
        return jax.ShapeDtypeStruct((local, sources, CAP, width), BF16)

    return pl.pallas_call(
        kernel,
        grid=(sources,),
        out_shape=(
            jax.ShapeDtypeStruct((sources, rows, D), BF16),
            jax.ShapeDtypeStruct((sources, rows, D), BF16),
            jax.ShapeDtypeStruct((sources, local, rows), F32),
            kept_shape(D),
            kept_shape(FF),
            kept_shape(FF),
            kept_shape(FF),
            kept_shape(D),
        ),
        in_specs=[
            pl.BlockSpec(weights.shape, lambda s: (0, 0, 0), pipeline_mode=pl.Buffered(1)),
            per_source(rows, D),
            per_source(rows, D),
            per_source(local, rows),
            per_source(rows, local),
            per_source(local, rows),
        ],
        out_specs=(
            per_source(rows, D),
            per_source(rows, D),
            per_source(local, rows),
            kept(D),
            kept(FF),
            kept(FF),
            kept(FF),
            kept(D),
        ),
        compiler_params=pltpu.CompilerParams(vmem_limit_bytes=56 * MIB),
        cost_estimate=pl.CostEstimate(
            flops=sources * local * CAP * D * FF * 2 * 8,
            bytes_accessed=50 * MIB,
            transcendentals=sources * local * CAP * FF,
        ),
        name="experts_step",
    )(weights, act_all, cot_all, rank_row, rank_col, gates)


def local(
    tokens,
    cotangent,
    lengths,
    routes,
    dense_weights,
    dense_first,
    dense_second,
    dense_average,
    expert_weights,
    expert_first,
    expert_second,
    expert_average,
):
    ndp, nex = lax.axis_size("dp"), lax.axis_size("expert")
    dp, ex = lax.axis_index("dp"), lax.axis_index("expert")
    grid = Grid(ndp, nex)
    local_experts = EXPERTS // nex
    length = SEG * ndp
    rows_dev = D // grid.ndev
    shard_rows = 3 * D // ndp

    spot = jnp.arange(FF, dtype=jnp.int32)
    order = (FF // D) * (spot % D) + spot // D
    mix = (spot[:, None] == order[None, :]).astype(BF16)
    shard_row = dp * shard_rows + jnp.arange(shard_rows, dtype=jnp.int32)
    is_down = (shard_row >= 2 * D)[None, :, None]
    expert_low = expert_weights.astype(BF16).reshape(local_experts, shard_rows, FF)
    mixed_low = jnp.einsum(
        "erf,fg->erg", expert_low, mix, preferred_element_type=F32
    ).astype(BF16)
    expert_send = jnp.where(is_down, expert_low, mixed_low)
    expert_all = lax.all_gather(expert_send, "dp", axis=0, tiled=False)
    expert_all = expert_all.transpose(1, 0, 2, 3).reshape(local_experts, 3 * D, FF)

    table = dense_weights.astype(BF16).reshape(rows_dev, -1)
    after = 4 * D + EXPERTS
    shard = jnp.concatenate(
        [
            table[:, : 4 * D],
            table[:, after : after + 3 * FF],
            table[:, 4 * D : after],
            table[:, after + 3 * FF :],
            jnp.zeros((rows_dev, MISC - EXPERTS - 3), BF16),
        ],
        axis=1,
    )
    shard = jnp.pad(shard, ((0, ROW_PAD - rows_dev), (0, 0)))

    names = jnp.arange(EXPERTS, dtype=jnp.int32)
    routes_rows = routes.reshape(TOK_DEV, TOP)
    member = (routes_rows[:, :, None] == names[None, None, :]).any(axis=1)
    before = jnp.arange(TOK_DEV)
    earlier = (before[None, :] < before[:, None]).astype(BF16)
    count = jnp.dot(earlier, member.astype(BF16), preferred_element_type=F32)
    ranks = jnp.where(member, count.astype(jnp.int32), -1).T

    local_pos = dp * SEG + jnp.arange(SEG, dtype=jnp.int32)
    live = (local_pos[None, :] < lengths[:, None]).astype(F32)
    grad_out_low = (cotangent.astype(F32) * live[..., None]).astype(BF16).reshape(TOK_DEV, D)

    tok_all, dense_all, cot_all, rank_all = first_exchange(
        grid, tokens, shard, grad_out_low, ranks
    )

    dense_all = dense_all.reshape(grid.ndev * ROW_PAD, -1)
    row = jnp.arange(D, dtype=jnp.int32)
    row_from = (row // rows_dev) * ROW_PAD + row % rows_dev
    unpad = (row_from[:, None] == jnp.arange(grid.ndev * ROW_PAD)[None, :]).astype(BF16)
    qkv_rows = dot(dense_all[:, : 3 * D], unpad, 0, 1).astype(BF16)
    qkv_rows = qkv_rows.reshape(3, HEADS, HEAD_DIM, D)
    rest = dot(unpad, dense_all[:, 3 * D :]).astype(BF16)
    w_output = rest[:, :D]
    w_sgate = rest[:, D : D + FF]
    w_sup = rest[:, D + FF : D + 2 * FF]
    w_sdown = rest[:, D + 2 * FF : D + 3 * FF]
    w_misc = rest[:, D + 3 * FF :]
    gain_first = w_misc[:, EXPERTS + 1].astype(F32)
    gain_second = w_misc[:, EXPERTS + 2].astype(F32)

    unit = dp * grid.units + jnp.arange(HEADS, dtype=jnp.int32)
    working = (jnp.arange(HEADS) < grid.units) & (unit < UNITS_ALL)
    last = jnp.minimum(dp * grid.units + grid.units, UNITS_ALL) - 1
    series = jnp.clip(jnp.minimum(unit, last) // HEADS, 0, SERIES_DEV - 1)
    slot = jnp.clip(series - grid.first_series(dp), 0, grid.slots - 1)
    info = jnp.stack(
        [slot, unit % HEADS, lengths[series], working.astype(jnp.int32)]
    ).astype(jnp.int32)
    half = HEAD_DIM // 2
    inverse = rope_base ** (-jnp.arange(half, dtype=F32) * 2.0 / HEAD_DIM)
    angles = inverse[:, None] * jnp.arange(length, dtype=jnp.int32).astype(F32)[None, :]
    cosine, sine = jnp.cos(angles), jnp.sin(angles)
    heads, act_one, query, key, value, lse = attend(
        grid,
        info,
        tok_all.reshape(grid.slots, length, D),
        qkv_rows,
        gain_first[None, :],
        cosine,
        sine,
    )
    heads_here = heads_out(grid, heads).reshape(-1, HEAD_DIM, SEG)[:UNITS_ALL]
    attn_low = heads_here.reshape(SERIES_DEV, D, SEG).transpose(0, 2, 1).reshape(TOK_DEV, D)

    residual = tokens.astype(F32).reshape(TOK_DEV, D)
    mixed_rows = residual + dot(attn_low, w_output)
    scale_two = lax.rsqrt(jnp.mean(mixed_rows * mixed_rows, axis=-1, keepdims=True) + eps_norm)
    normed_two = mixed_rows * scale_two
    act_two = (normed_two * gain_second).astype(BF16)
    misc = dot(act_two, w_misc)
    router_probs = jax.nn.softmax(misc[:, :EXPERTS], axis=-1)
    shared_gate = jax.nn.sigmoid(misc[:, EXPERTS : EXPERTS + 1])

    act_all, gates_all = expert_gather(grid, act_two, router_probs.T)
    rank_row = lax.dynamic_slice_in_dim(rank_all, ex * local_experts, local_experts, 1)
    gate_row = lax.dynamic_slice_in_dim(gates_all, ex * local_experts, local_experts, 1)
    routed_parts, gin_parts, ggate, taken, grad_gate_lin, grad_up_lin, hidden, grad_result = (
        experts_step(
            expert_all, act_all, cot_all, rank_row, rank_row.transpose(0, 2, 1), gate_row
        )
    )
    gin_back = lax.all_to_all(gin_parts, "expert", split_axis=0, concat_axis=0, tiled=True)
    ggate_back = lax.all_to_all(ggate, "expert", split_axis=0, concat_axis=0, tiled=True)
    routed_back = lax.all_to_all(routed_parts, "expert", split_axis=0, concat_axis=0, tiled=True)

    def by_expert(rows):
        return rows.reshape(local_experts, nex * CAP, -1)

    taken, grad_gate_lin, grad_up_lin, hidden, grad_result = (
        by_expert(v) for v in (taken, grad_gate_lin, grad_up_lin, hidden, grad_result)
    )
    grad_e_gate = jnp.einsum("erd,erf->edf", taken, grad_gate_lin, preferred_element_type=F32)
    grad_e_up = jnp.einsum("erd,erf->edf", taken, grad_up_lin, preferred_element_type=F32)
    grad_e_down = [
        jnp.einsum(
            "erh,erd->ehd", hidden[..., at : at + D], grad_result, preferred_element_type=F32
        )
        for at in range(0, FF, D)
    ]
    expert_terms = jnp.concatenate(
        [
            grad_e_gate.astype(BF16),
            grad_e_up.astype(BF16),
            jnp.concatenate(grad_e_down, axis=2).astype(BF16),
        ],
        axis=1,
    )
    expert_terms = expert_terms.reshape(local_experts, ndp, shard_rows, FF).transpose(1, 0, 2, 3)
    expert_sum = lax.psum_scatter(expert_terms, "dp", scatter_dimension=0, tiled=False)
    unmixed = jnp.einsum("erg,fg->erf", expert_sum, mix, preferred_element_type=F32)
    expert_grad = jnp.where(is_down, expert_sum.astype(F32), unmixed)
    expert_grad = expert_grad.reshape(expert_weights.shape)

    sgate_lin = dot(act_two, w_sgate)
    sup_lin = dot(act_two, w_sup)
    sgate_sigmoid = jax.nn.sigmoid(sgate_lin)
    sgate_silu = sgate_lin * sgate_sigmoid
    shared_hidden = (sgate_silu * sup_lin).astype(BF16)
    shared_lin = dot(shared_hidden, w_sdown, 1, 1)
    grad_out = grad_out_low.astype(F32)
    grad_shared_lin = (grad_out * shared_gate).astype(BF16)
    grad_svec_logit = (
        shared_gate * (1.0 - shared_gate) * jnp.sum(grad_out * shared_lin, axis=-1, keepdims=True)
    ).astype(BF16)
    grad_shared_hidden = dot(grad_shared_lin, w_sdown)
    grad_sgate_lin = (
        grad_shared_hidden * sup_lin * sgate_sigmoid * (1.0 + sgate_lin * (1.0 - sgate_sigmoid))
    ).astype(BF16)
    grad_sup_lin = (grad_shared_hidden * sgate_silu).astype(BF16)

    routed = jnp.sum(routed_back.astype(F32), axis=0)
    output = (mixed_rows + routed + shared_gate * shared_lin).astype(BF16)
    grad_router_probs = ggate_back.reshape(EXPERTS, TOK_DEV).T
    grad_logits = (
        router_probs
        * (grad_router_probs - jnp.sum(router_probs * grad_router_probs, axis=-1, keepdims=True))
    ).astype(BF16)
    grad_misc = jnp.concatenate(
        [grad_logits, grad_svec_logit, jnp.zeros((TOK_DEV, MISC - EXPERTS - 1), BF16)], axis=1
    )
    grad_act_two = (
        jnp.sum(gin_back.astype(F32), axis=0)
        + dot(grad_sgate_lin, w_sgate, 1, 1)
        + dot(grad_sup_lin, w_sup, 1, 1)
        + dot(grad_misc, w_misc, 1, 1)
    )
    grad_gain_two = jnp.sum(grad_act_two * normed_two, axis=0)
    weighted_two = grad_act_two * gain_second
    grad_mixed = grad_out + scale_two * (
        weighted_two - normed_two * jnp.mean(weighted_two * normed_two, axis=-1, keepdims=True)
    )
    grad_attn_low = grad_mixed.astype(BF16)
    grad_heads = dot(grad_attn_low, w_output, 1, 1).astype(BF16)
    grad_heads = grad_heads.reshape(SERIES_DEV, SEG, D).transpose(0, 2, 1)
    grad_heads = grad_heads.reshape(UNITS_ALL, HEAD_DIM, SEG)
    grad_heads = jnp.pad(grad_heads, ((0, grid.units * ndp - UNITS_ALL), (0, 0), (0, 0)))
    grad_heads = heads_in(grid, grad_heads.reshape(ndp, grid.units, HEAD_DIM, SEG))

    back, qkv_grads = attend_back(
        grid, info, act_one, qkv_rows, query, key, value, lse, grad_heads, cosine, sine
    )
    back = rows_back(grid, back.reshape(grid.slots, ndp, SEG, D))
    grad_act_one = jnp.stack(
        [
            sum(
                back[owner, owned.index(s)].astype(F32)
                for owner, owned in enumerate(grid.owned)
                if s in owned
            )
            for s in range(SERIES_DEV)
        ]
    ).reshape(TOK_DEV, D)
    scale_one = lax.rsqrt(jnp.mean(residual * residual, axis=-1, keepdims=True) + eps_norm)
    normed_one = residual * scale_one
    grad_gain_one = jnp.sum(grad_act_one * normed_one, axis=0)
    weighted_one = grad_act_one * gain_first
    grad_tokens = grad_mixed + scale_one * (
        weighted_one - normed_one * jnp.mean(weighted_one * normed_one, axis=-1, keepdims=True)
    )

    row_dev = row // rows_dev
    row_to = ((row_dev % nex) * ndp + row_dev // nex) * ROW_PAD + row % rows_dev
    group = (jnp.arange(grid.ndev * ROW_PAD)[:, None] == row_to[None, :]).astype(BF16)

    def scatter_rows(padded):
        width = padded.shape[1]
        first = lax.all_to_all(
            padded.reshape(nex, ndp * ROW_PAD, width), "expert", split_axis=0, concat_axis=0,
            tiled=True,
        )
        first = jnp.sum(first.astype(F32), axis=0).astype(BF16)
        second = lax.all_to_all(
            first.reshape(ndp, ROW_PAD, width), "dp", split_axis=0, concat_axis=0, tiled=True
        )
        return jnp.sum(second.astype(F32), axis=0)[:rows_dev]

    def weight_grad(left, right):
        return dot(left, right, 0, 0).astype(BF16)

    g_misc = dot(act_two, grad_misc, 0, 0).astype(BF16)
    g_misc = jnp.where(
        jnp.arange(MISC)[None, :] == EXPERTS + 2, grad_gain_two[:, None].astype(BF16), g_misc
    )
    early = jnp.concatenate(
        [
            weight_grad(attn_low, grad_attn_low),
            weight_grad(act_two, grad_sgate_lin),
            weight_grad(act_two, grad_sup_lin),
            weight_grad(grad_shared_lin, shared_hidden),
            g_misc,
        ],
        axis=1,
    )
    early = scatter_rows(dot(group, early).astype(BF16))
    late = jnp.concatenate(
        [
            dot(group, qkv_grads.reshape(3 * D, D).astype(BF16), 1, 1).astype(BF16),
            dot(group, jnp.broadcast_to(grad_gain_one[:, None], (D, MISC)).astype(BF16)).astype(
                BF16
            ),
        ],
        axis=1,
    )
    late = scatter_rows(late)
    misc_at = D + 3 * FF
    dense_grad = jnp.concatenate(
        [
            late[:, : 3 * D],
            early[:, :D],
            early[:, misc_at : misc_at + EXPERTS],
            early[:, D:misc_at],
            early[:, misc_at + EXPERTS : misc_at + EXPERTS + 1],
            late[:, 3 * D : 3 * D + 1],
            early[:, misc_at + EXPERTS + 2 : misc_at + EXPERTS + 3],
        ],
        axis=1,
    ).reshape(-1)

    dense_first_new, dense_second_new, dense_new, dense_average_new = adamw_update(
        dense_weights, dense_grad, dense_first, dense_second, dense_average
    )
    expert_first_new, expert_second_new, expert_new, expert_average_new = adamw_update(
        expert_weights, expert_grad, expert_first, expert_second, expert_average
    )
    return (
        output.reshape(tokens.shape),
        grad_tokens.reshape(tokens.shape),
        dense_grad,
        dense_first_new,
        dense_second_new,
        dense_new,
        dense_average_new,
        expert_grad,
        expert_first_new,
        expert_second_new,
        expert_new,
        expert_average_new,
    )


def solution(mesh):
    rows = P("expert", "dp", None)
    dense = P(("dp", "expert"))
    experts = P("expert", "dp")
    return jax.shard_map(
        local,
        mesh=mesh,
        in_specs=(
            (rows, rows, P("expert"), P("dp", "expert", None, None)) + (dense,) * 4 + (experts,) * 4
        ),
        out_specs=(rows, rows) + (dense,) * 5 + (experts,) * 5,
        check_vma=False,
    )
```

time: 1430 us -> 681 us (0.48)
  waiting for transfers between devices: 767 us -> 127 us
  Pallas kernels: 0 us -> 319 us
  matrix products: 302 us -> 82.6 us
  local copies, waits for them, and re-layouts: 185 us -> 46.3 us
  other arithmetic: 126 us -> 48.2 us
  starting transfers between devices: 16.3 us -> 33.7 us
    unnamed x13 -> x2, waiting for transfers between devices: 615 us -> 0.03 us
    pallas_call x0 -> x8, Pallas kernels: none -> 319 us  [the longest x1 74.2 us: first_exchange(): pl.pallas_call(kernel, out_shape=(jax.ShapeDtypeStruct((grid.slots, ndp,...]
    dot_general x53 -> x29, matrix products: 302 us -> 82.6 us  [the longest x20 48.1 us: dot(): lax.dot_general(left, right, (((left_dim,), (right_dim,)), ((), ())), pre...]
    all_gather x3 -> x1, waiting for transfers between devices: 134 us -> 0.01 us  [local(): expert_all = lax.all_gather(expert_send, 'dp', axis=0, tiled=False)]
    all_to_all x4 -> x7, waiting for transfers between devices: 18.9 us -> 127 us  [the longest x2 63.2 us: scatter_rows(): lax.all_to_all(padded.reshape(nex, ndp * ROW_PAD, width), 'expert', split...]
    unnamed x164 -> x150, local copies, waits for them, and re-layouts: 68 us -> 17.1 us
    concatenate x3 -> x2, other arithmetic: 38 us -> 12 us  [the longest x1 10.9 us: local(): jnp.concatenate([grad_e_gate.astype(BF16), grad_e_up.astype(BF16), jnp.co...]
    reshape x4 -> x5, local copies, waits for them, and re-layouts: 27.2 us -> 4.94 us  [the longest x1 3.48 us: local(): expert_terms.reshape(local_experts, ndp, shard_rows, FF)]
  transfers between devices with their start and end apart: 12 -> 9, of which waited for: 8 -> 6; matrix products, arithmetic and copies ran while one was open for 26% -> 17% of each run, Pallas kernels for 0% -> 38%
where the time goes in v1:
time: 681 us; the launch traced here: 672 us
  Pallas kernels  319 us (47%)
  waiting for transfers between devices  127 us (19%)
  matrix products  82.6 us (12%)
  other arithmetic  48.2 us (7%)
  local copies, waits for them, and re-layouts  46.3 us (7%)
  starting transfers between devices  33.7 us (5%)
  between operations  15.5 us (2%)
    pallas_call x1, Pallas kernels, first_exchange(): pl.pallas_call(kernel, out_shape=(jax.ShapeDtypeStruct((grid.slots, ndp,...  74.2 us
    all_to_all x2, waiting for transfers between devices, scatter_rows(): lax.all_to_all(padded.reshape(nex, ndp * ROW_PAD, width), 'expert', split...  63.2 us
    pallas_call x1, Pallas kernels, experts_step(): pl.pallas_call(kernel, grid=(sources,), out_shape=(jax.ShapeDtypeStruct((...  60.2 us
    dot_general x20, matrix products, dot(): lax.dot_general(left, right, (((left_dim,), (right_dim,)), ((), ())), pre...  48.1 us
    pallas_call x1, Pallas kernels, rows_back(): pl.pallas_call(kernel, out_shape=jax.ShapeDtypeStruct((ndp, grid.slots) +...  45.2 us
    pallas_call x1, Pallas kernels, heads_out(): pl.pallas_call(kernel, out_shape=jax.ShapeDtypeStruct((ndp,) + values.sha...  41.8 us
    all_to_all x2, waiting for transfers between devices, scatter_rows(): lax.all_to_all(first.reshape(ndp, ROW_PAD, width), 'dp', split_axis=0, co...  34.4 us
    pallas_call x1, Pallas kernels, attend_back(): pl.pallas_call(kernel, out_shape=(jax.ShapeDtypeStruct((grid.slots, lengt...  29.9 us
  transfers between devices with their start and end apart: 9, of which 6 were waited for; matrix products, arithmetic and copies ran while one was open for 17% of the time, Pallas kernels for 38%

profile of v1, /device:TPU:0, one launch (start us, length us, event | category | flops | bytes accessed | tf_op | source)
XLA Modules:
  0.0 672.3 jit_solution(8049829436272210780)
XLA Ops:
  9.1 2.8 fusion.24
  16.0 74.2 %first_exchange.1 = (bf16[2,8,128,384]{3,2,1,0:T(8,128)(2,1)}, bf16[32,16,6272]{2,1,0:T(8,128)(2,1)}, bf16[4,768,384]{2,1,0:T(8,128)(2,1)}, s32[4,8,768]{2,1,0:T(8,128)}) custom-call(bf16[6,128,384]{2,1,0:T(8,128)(2,1)} %tok.1, bf16[16,6272]{1,0:T(8,128)(2,1)} %pad.4.shd, bf16[768,384]{1,0:T(8,128)(2,1)} %bitcast.145, s32[8,768]{1,0:T(8,128)} %fusion.59.rank_in), custom_call_target="tpu_custom_call" | custom-call | tf_op jit(solution)/shard_map/first_exchange/pallas_call | solution.py:264
  90.2 4.7 convolution_convert_fusion.1
  99.5 21.3 %attend.1 = (bf16[9,32,1024]{2,1,0:T(8,128)(2,1)S(1)}, bf16[2,1024,384]{2,1,0:T(8,128)(2,1)S(1)}, bf16[9,32,1024]{2,1,0:T(8,128)(2,1)S(1)}, bf16[9,32,1024]{2,1,...) custom-call(s32[4,12]{1,0:T(4,128)S(1)} %pad_add_fusion.info_ref, ...), custom_call_target="tpu_custom_call" | custom-call | flops 4831838208 | bytes 8388608 | tf_op jit(solution)/shard_map/attend/pallas_call | solution.py:557
  124.4 41.8 %heads_out.1 = bf16[8,9,32,128]{3,2,1,0:T(8,128)(2,1)} custom-call(bf16[9,32,1024]{2,1,0:T(8,128)(2,1)} %copy-done.2), custom_call_target="tpu_custom_call" | custom-call | tf_op jit(solution)/shard_map/heads_out/pallas_call | solution.py:312
  173.1 20.1 %expert_gather.1 = (bf16[4,768,384]{2,1,0:T(8,128)(2,1)}, f32[4,8,768]{2,1,0:T(8,128)}) custom-call(bf16[768,384]{1,0:T(8,128)(2,1)} %copy-done.11, f32[8,768]{1,0:T(8,128)} %fusion.126.gate), custom_call_target="tpu_custom_call" | custom-call | tf_op jit(solution)/shard_map/expert_gather/pallas_call | solution.py:482
  194.8 3.1 constant_dynamic-slice_fusion.1
  197.9 2.5 copy.87.rrow_ref
  200.4 2.8 fusion.68
  203.2 3.7 multiply_convert_fusion.2
  206.9 2.4 fusion.50
  213.9 3.0 fusion.156.rcol_ref
  217.5 7.0 %multiply_convert_fusion = (bf16[768,1536]{1,0:T(8,128)(2,1)}, bf16[768,1536]{1,0:T(8,128)(2,1)}) fusion(f32[768,1536]{1,0:T(8,128)} %copy-done.24, f32[768,1536]{1,0:T(8,128)} %get-tuple-element.85, bf16[384,5120]{1,0:T(8,128)(2,1)} %copy-done.41, bf16[768,384]{1,0:T(8,128)(2,1)S(1)} %bitcast.146, f32[768]{0:T(1024)S(1)} %reduce.7), kind=kOutput, calls=%fused_computation.10 | convolution fusion | flops 922189824 | bytes 15928320 | tf_op jit(solution)/shard_map/dot_general | solution.py:56
  224.5 6.4 copy.85
  231.0 60.2 %experts_step.1 = (bf16[4,768,384]{2,1,0:T(8,128)(2,1)}, bf16[4,768,384]{2,1,0:T(8,128)(2,1)}, f32[4,2,768]{2,1,0:T(2,128)}, bf16[2,4,384,384]{3,2,1,0:T(8,128)(...) custom-call(bf16[2,1152,1536]{2,1,0:T(8,128)(2,1)} %bitcast.149, ...), custom_call_target="tpu_custom_call" | custom-call | flops 28991029248 | bytes 52428800 | tf_op jit(solution)/shard_map/experts_step/pallas_call | solution.py:755
  291.2 4.0 fusion.37
  295.2 4.1 fusion.40
  299.3 4.1 fusion.43
  303.4 5.2 convolution_convert_fusion.3
  308.6 5.2 convolution_convert_fusion.2
  313.8 3.3 all-to-all-start.2
  317.1 4.6 fusion.46
  321.7 4.5 all-to-all-start.1
  326.3 10.9 %maximum_maximum_fusion = bf16[2,1152,1536]{2,1,0:T(8,128)(2,1)S(1)} fusion(bf16[2,384,384]{2,1,0:T(8,128)(2,1)} %fusion.46, bf16[2,384,384]{2,1,0:T(8,128)(2,1)} %fusion.43, bf16[2,384,384]{2,1,0:T(8,128)(2,1)} %fusion.40, bf16[2,384,384]{2,1,0:T(8,128)(2,1)S(1)} %fusion.37, bf16[2,384,1536]{2,1,0:T(8,128)(2,1)} %convolution_convert_fusion.2, ...), kind=kLoop, calls=%fused_computation.6 | loop fusion | flops 42467328 | bytes 14155776 | tf_op jit(solution)/shard_map/concatenate | solution.py:935
  337.2 3.5 copy.124
  341.5 13.4 %all-to-all-done.1 = bf16[4,768,384]{2,1,0:T(8,128)(2,1)} async-done(((bf16[4,768,384]{2,1,0:T(8,128)(2,1)}), bf16[4,768,384]{2,1,0:T(8,128)(2,1)}, u32[]{:S(2)}, u32[]{:S(2)}) %all-to-all-start.1) | async-done | bytes 2359328 | tf_op jit(solution)/shard_map/all_to_all | solution.py:917
  354.8 4.8 all-to-all-start
  363.0 2.8 convolution_add_fusion.3
  365.9 2.8 convolution_add_fusion.2
  368.7 3.0 multiply_reduce_fusion
  371.7 16.4 %all-to-all-done = bf16[4,768,384]{2,1,0:T(8,128)(2,1)} async-done(((bf16[4,768,384]{2,1,0:T(8,128)(2,1)}), bf16[4,768,384]{2,1,0:T(8,128)(2,1)}, u32[]{:S(2)}, u32[]{:S(2)}) %all-to-all-start) | async-done | bytes 2359328 | tf_op jit(solution)/shard_map/all_to_all | solution.py:919
  395.5 25.9 %heads_in.1.do_ref = bf16[9,32,1024]{2,1,0:T(8,128)(2,1)} custom-call(bf16[8,9,32,128]{3,2,1,0:T(8,128)(2,1)} %bitcast.158), custom_call_target="tpu_custom_call" | custom-call | tf_op jit(solution)/shard_map/heads_in/pallas_call | solution.py:345
  426.0 29.9 %attend_back.1 = (bf16[2,1024,384]{2,1,0:T(8,128)(2,1)S(1)}, f32[3,12,32,384]{3,2,1,0:T(8,128)S(1)}) custom-call(s32[4,12]{1,0:T(4,128)S(1)} %pad_add_fusion.info_ref, bf16[2,1024,384]{2,1,0:T(8,128)(2,1)S(1)} %copy-done.5, bf16[3,12,32,384]{3,2,1,0:T(8,128)(2,1)S(1)} %bitcast.141, bf16[9,32,1024]{2,1,0:T(8,128)(2,1)S(1)} %get-tuple-element.45.q_ref, ...), custom_call_target="tpu_custom_call" | custom-call | flops 12079595520 | bytes 12582912 | tf_op jit(solution)/shard_map/attend_back/pallas_call | solution.py:652
  458.5 45.2 %rows_back.1 = bf16[8,2,128,384]{3,2,1,0:T(8,128)(2,1)} custom-call(bf16[2,8,128,384]{3,2,1,0:T(8,128)(2,1)} %bitcast.138), custom_call_target="tpu_custom_call" | custom-call | tf_op jit(solution)/shard_map/rows_back/pallas_call | solution.py:396
  508.8 4.8 all-to-all-start.3
  513.7 2.9 fusion.11
  520.3 4.6 convolution_convert_fusion
  524.9 6.0 all-to-all-done.3
  530.9 5.1 all-to-all-start.5
  536.1 2.3 reduce_sum.151
  538.4 57.1 %all-to-all-done.5 = bf16[4,128,5120]{2,1,0:T(8,128)(2,1)} async-done(((bf16[4,128,5120]{2,1,0:T(8,128)(2,1)}), bf16[4,128,5120]{2,1,0:T(8,128)(2,1)}, u32[]{:S(2)}, u32[]{:S(2)}) %all-to-all-start.5) | async-done | bytes 5242912 | tf_op jit(solution)/shard_map/all_to_all | solution.py:1022
  595.5 6.7 all-to-all-start.4
  602.2 4.8 reduce_sum.154
  607.1 5.3 all-to-all-done.4
  612.3 4.4 all-to-all-start.6
  618.3 29.1 %all-to-all-done.6 = bf16[8,16,5120]{2,1,0:T(8,128)(2,1)} async-done(((bf16[8,16,5120]{2,1,0:T(8,128)(2,1)}), bf16[8,16,5120]{2,1,0:T(8,128)(2,1)}, u32[]{:S(2)}, u32[]{:S(2)}) %all-to-all-start.6) | async-done | bytes 1310752 | tf_op jit(solution)/shard_map/all_to_all | solution.py:1027
  650.7 3.6 fusion.15
  656.3 8.9 %multiply_add_fusion.1 = (f32[2,221184]{1,0:T(2,128)}, f32[2,221184]{1,0:T(2,128)}, f32[2,221184]{1,0:T(2,128)}, f32[2,221184]{1,0:T(2,128)}) fusion(f32[2,221184]{1,0:T(2,128)S(1)} %copy-done.35, f32[2,221184]{1,0:T(2,128)S(1)} %copy-done.26, f32[2,221184]{1,0:T(2,128)S(1)} %bitcast.150, f32[2,221184]{1,0:T(2,128)S(1)} %copy-done.36, ...), kind=kLoop, calls=%fused_computation.48 | loop fusion | flops 7520256 | bytes 15925248 | tf_op jit(solution)/shard_map/add | solution.py:51
  (246 shorter events, 61.3 us)
Async XLA Ops:
  7.2 217.4 %all-gather.3.cloned.1.call-start = ((), (), s32[]{:S(2)}) async-start(), calls=%async_computation.9 | async-start | bytes 7962624 | tf_op jit(solution)/shard_map/all_gather | solution.py:828
  7.2 4.7 copy-start.57
  9.1 2.9 copy-start.38
  12.0 3.1 copy-start.50
  95.0 4.5 copy-start.3
  124.4 43.9 %copy-start.17 = (bf16[6,128,384]{2,1,0:T(8,128)(2,1)S(1)}, bf16[6,128,384]{2,1,0:T(8,128)(2,1)}, u32[]{:S(2)}) copy-start(bf16[6,128,384]{2,1,0:T(8,128)(2,1)} %tok.1) | copy-start | bytes 1769476
  170.1 23.0 %copy-start.54 = (s32[4,8,768]{2,1,0:T(8,128)S(1)}, s32[4,8,768]{2,1,0:T(8,128)}, u32[]{:S(2)}) copy-start(s32[4,8,768]{2,1,0:T(8,128)} %get-tuple-element.39) | copy-start | bytes 294916
  170.3 2.7 copy-start.11
  194.8 5.6 copy-start.12
  200.4 2.8 copy-start.42
  203.2 3.7 copy-start.24
  203.2 3.7 copy-start.20
  206.9 6.8 %copy-start.18 = (bf16[6,128,384]{2,1,0:T(8,128)(2,1)S(1)}, bf16[6,128,384]{2,1,0:T(8,128)(2,1)}, u32[]{:S(2)}) copy-start(bf16[6,128,384]{2,1,0:T(8,128)(2,1)} %tok.1) | copy-start | bytes 1769476
  211.0 6.6 copy-start.21
  211.1 157.6 %copy-start.63 = (bf16[128]{0:T(256)(128)(2,1)}, bf16[128]{0:T(256)(128)(2,1)S(1)}, u32[]{:S(2)}) copy-start(bf16[128]{0:T(256)(128)(2,1)S(1)} %pad.15.clone) | copy-start | bytes 772
  291.2 4.0 copy-start.66
  295.2 8.2 %copy-start.65 = (bf16[2,4,384,1536]{3,2,1,0:T(8,128)(2,1)S(1)}, bf16[2,4,384,1536]{3,2,1,0:T(8,128)(2,1)}, u32[]{:S(2)}) copy-start(bf16[2,4,384,1536]{3,2,1,0:T(8,128)(2,1)} %get-tuple-element.52) | copy-start | bytes 28311556
  295.2 8.2 %copy-start.67 = (bf16[2,4,384,384]{3,2,1,0:T(8,128)(2,1)S(1)}, bf16[2,4,384,384]{3,2,1,0:T(8,128)(2,1)}, u32[]{:S(2)}) copy-start(bf16[2,4,384,384]{3,2,1,0:T(8,128)(2,1)} %get-tuple-element.51) | copy-start | bytes 7077892
  299.3 9.3 %slice-start = ((s8[9437184]{0:T(1024)(128)(4,1)}), s8[4194304]{0:T(1024)(128)(4,1)S(1)}, s32[]{:S(2)}) async-start(s8[9437184]{0:T(1024)(128)(4,1)} %bitcast.172), calls=%async_computation.10 | async-start | bytes 8388608
  303.4 5.2 slice-start.1
  303.4 5.2 slice-start.2
  313.8 7.9 %all-to-all-start.2 = ((f32[4,2,768]{2,1,0:T(2,128)}), f32[4,2,768]{2,1,0:T(2,128)S(1)}, u32[]{:S(2)}, u32[]{:S(2)}) async-start(f32[4,2,768]{2,1,0:T(2,128)} %get-tuple-element.43), calls=%async_computation.2 | async-start | bytes 49152 | tf_op jit(solution)/shard_map/all_to_all | solution.py:918
  321.7 33.1 %all-to-all-start.1 = ((bf16[4,768,384]{2,1,0:T(8,128)(2,1)}), bf16[4,768,384]{2,1,0:T(8,128)(2,1)}, u32[]{:S(2)}, u32[]{:S(2)}) async-start(bf16[4,768,384]{2,1,0:T(8,128)(2,1)} %get-tuple-element.42), calls=%async_computation.1 | async-start | bytes 4718592 | tf_op jit(solution)/shard_map/all_to_all | solution.py:917
  326.3 324.4 %reduce-scatter.2.cloned.1.call-start = ((), (), s32[]{:S(2)}) async-start(), calls=%async_computation.8 | async-start | bytes 7962624 | tf_op jit(solution)/shard_map/reduce_scatter | solution.py:944
  354.8 33.3 %all-to-all-start = ((bf16[4,768,384]{2,1,0:T(8,128)(2,1)}), bf16[4,768,384]{2,1,0:T(8,128)(2,1)}, u32[]{:S(2)}, u32[]{:S(2)}) async-start(bf16[4,768,384]{2,1,0:T(8,128)(2,1)} %get-tuple-element.41), calls=%async_computation | async-start | bytes 4718592 | tf_op jit(solution)/shard_map/all_to_all | solution.py:919
  360.5 8.2 %copy-start.47 = (bf16[768,8]{1,0:T(8,128)(2,1)}, bf16[768,8]{1,0:T(8,128)(2,1)S(1)}, u32[]{:S(2)}) copy-start(bf16[768,8]{1,0:T(8,128)(2,1)S(1)} %copy.88) | copy-start | bytes 36868
  363.0 2.8 copy-start.32
  365.9 2.8 copy-start.45
  371.7 18.7 %copy-start.22 = (bf16[6,128,384]{2,1,0:T(8,128)(2,1)S(1)}, bf16[6,128,384]{2,1,0:T(8,128)(2,1)}, u32[]{:S(2)}) copy-start(bf16[6,128,384]{2,1,0:T(8,128)(2,1)} %multiply_convert_fusion.4) | copy-start | bytes 1769476
  426.0 31.1 %copy-start.15 = (f32[768,384]{1,0:T(8,128)S(1)}, f32[768,384]{1,0:T(8,128)}, u32[]{:S(2)}) copy-start(f32[768,384]{1,0:T(8,128)} %copy-done.14) | copy-start | bytes 3538948
  426.0 31.1 %copy-start.27 = (bf16[6,384,128]{1,2,0:T(8,128)(2,1)S(1)}, bf16[6,384,128]{1,2,0:T(8,128)(2,1)}, u32[]{:S(2)}) copy-start(bf16[6,384,128]{1,2,0:T(8,128)(2,1)} %copy.84) | copy-start | bytes 1769476
  507.6 6.1 copy-start.13
  508.8 4.8 copy-start.43
  508.8 22.2 %all-to-all-start.3 = ((bf16[4,128,1280]{2,1,0:T(8,128)(2,1)}), bf16[4,128,1280]{2,1,0:T(8,128)(2,1)}, u32[]{:S(2)}, u32[]{:S(2)}) async-start(bf16[4,128,1280]{2,1,0:T(8,128)(2,1)} %bitcast.155), calls=%async_computation.3 | async-start | bytes 2621440 | tf_op jit(solution)/shard_map/all_to_all | solution.py:1022
  513.6 3.0 copy-start.33
  530.9 64.6 %all-to-all-start.5 = ((bf16[4,128,5120]{2,1,0:T(8,128)(2,1)}), bf16[4,128,5120]{2,1,0:T(8,128)(2,1)}, u32[]{:S(2)}, u32[]{:S(2)}) async-start(bf16[4,128,5120]{2,1,0:T(8,128)(2,1)} %bitcast.154), calls=%async_computation.5 | async-start | bytes 10485760 | tf_op jit(solution)/shard_map/all_to_all | solution.py:1022
  595.5 16.8 %all-to-all-start.4 = ((bf16[8,16,1280]{2,1,0:T(8,128)(2,1)}), bf16[8,16,1280]{2,1,0:T(8,128)(2,1)S(1)}, u32[]{:S(2)}, u32[]{:S(2)}) async-start(bf16[8,16,1280]{2,1,0:T(8,128)(2,1)} %bitcast.37), calls=%async_computation.4 | async-start | bytes 655360 | tf_op jit(solution)/shard_map/all_to_all | solution.py:1027
  607.1 9.7 %copy-start.56 = (f32[6,128]{1,0:T(8,128)S(1)}, f32[6,128]{1,0:T(8,128)}, u32[]{:S(2)}) copy-start(f32[6,128]{1,0:T(8,128)} %get-tuple-element.61) | copy-start | bytes 9220
  607.1 9.8 %copy-start.16 = (f32[768,384]{1,0:T(8,128)S(1)}, f32[768,384]{1,0:T(8,128)}, u32[]{:S(2)}) copy-start(f32[768,384]{1,0:T(8,128)} %copy-done.14) | copy-start | bytes 3538948
  612.3 35.0 %all-to-all-start.6 = ((bf16[8,16,5120]{2,1,0:T(8,128)(2,1)}), bf16[8,16,5120]{2,1,0:T(8,128)(2,1)}, u32[]{:S(2)}, u32[]{:S(2)}) async-start(bf16[8,16,5120]{2,1,0:T(8,128)(2,1)} %bitcast.156), calls=%async_computation.6 | async-start | bytes 2621440 | tf_op jit(solution)/shard_map/all_to_all | solution.py:1027
  618.2 31.2 %copy-start.39 = (f32[73860]{0:T(1024)S(1)}, f32[73860]{0:T(1024)}, u32[]{:S(2)}) copy-start(f32[73860]{0:T(1024)} %param.16) | copy-start | bytes 886324
  618.2 31.2 %copy-start.51 = (f32[73860]{0:T(1024)S(1)}, f32[73860]{0:T(1024)}, u32[]{:S(2)}) copy-start(f32[73860]{0:T(1024)} %param.19) | copy-start | bytes 886324
  618.2 31.3 %copy-start.52 = (f32[73860]{0:T(1024)S(1)}, f32[73860]{0:T(1024)}, u32[]{:S(2)}) copy-start(f32[73860]{0:T(1024)} %param.18) | copy-start | bytes 886324
  618.2 31.3 %copy-start.53 = (f32[73860]{0:T(1024)S(1)}, f32[73860]{0:T(1024)}, u32[]{:S(2)}) copy-start(f32[73860]{0:T(1024)} %param.17) | copy-start | bytes 886324
  649.5 4.9 copy-start.40
  650.7 5.0 copy-start.36
  650.7 5.0 copy-start.37
  655.7 9.5 %copy-start.25 = (f32[1,2,144,1536]{3,1,2,0:T(2,128)}, f32[1,2,144,1536]{3,1,2,0:T(2,128)S(1)}, u32[]{:S(2)}) copy-start(f32[1,2,144,1536]{3,1,2,0:T(2,128)S(1)} %copy.118) | copy-start | bytes 5308420
  (35 other events, 51.8 us)
Sparse Core Ops, SparseCore 0:
  12.1 155.1 all-gather.2
  340.8 166.7 reduce-scatter.1

commit v2 on v1

--- a/solution.py
+++ b/solution.py
@@ -320,10 +320,13 @@
     )(values)
 
 
-def heads_in(grid, values):
+def heads_in(grid, values, act, shared, attn, grads, hidden):
     ndp = grid.ndp
-
-    def kernel(src, dst, send, recv, loc):
+    grad_attn, grad_sgate, grad_sup, grad_misc = grads
+    tile = FF // 3
+
+    def kernel(src, act_ref, shared_ref, attn_ref, ga_ref, gs_ref, gu_ref, gm_ref, hid_ref,
+               dst, out_ref, send, recv, loc):
         dp, ex = lax.axis_index("dp"), lax.axis_index("expert")
         greet([(lax.rem(dp + d, ndp), ex) for d in range(1, ndp)])
         lanes = pl.ds(pl.multiple_of(dp * SEG, SEG), SEG)
@@ -337,75 +340,126 @@
             copies.append(copy)
         mine = pltpu.make_async_copy(src.at[dp], dst.at[:, :, lanes], loc)
         mine.start()
+        out_ref[:, :D] = dot(attn_ref[...], ga_ref[...]).astype(BF16)
+        out_ref[:, D + 3 * FF :] = dot(act_ref[...], gm_ref[...]).astype(BF16)
+
+        def column(step, carry):
+            at = pl.multiple_of(step * tile, tile)
+            for n, (left, right) in enumerate(
+                ((act_ref, gs_ref), (act_ref, gu_ref), (shared_ref, hid_ref))
+            ):
+                part = dot(left[...], right[:, pl.ds(at, tile)]).astype(BF16)
+                out_ref[:, pl.ds(pl.multiple_of(D + n * FF + at, MISC), tile)] = part
+            return carry
+
+        lax.fori_loop(0, FF // tile, column, 0)
         mine.wait()
         for copy in copies:
             copy.wait()
 
     dma = pltpu.SemaphoreType.DMA
+    vmem = pl.BlockSpec(memory_space=pltpu.VMEM)
     return pl.pallas_call(
         kernel,
-        out_shape=jax.ShapeDtypeStruct(values.shape[1:3] + (SEG * ndp,), values.dtype),
-        in_specs=[any_spec()],
-        out_specs=any_spec(),
+        out_shape=(
+            jax.ShapeDtypeStruct(values.shape[1:3] + (SEG * ndp,), values.dtype),
+            jax.ShapeDtypeStruct((D, D + 3 * FF + MISC), BF16),
+        ),
+        in_specs=[any_spec()] + [vmem] * 8,
+        out_specs=(any_spec(), vmem),
         scratch_shapes=[dma((ndp - 1,)), dma((ndp - 1,)), dma],
-        compiler_params=comm_params(2),
+        compiler_params=pltpu.CompilerParams(
+            collective_id=2, has_side_effects=True, vmem_limit_bytes=40 * MIB
+        ),
         name="heads_in",
-    )(values)
-
-
-def rows_back(grid, values):
-    ndp = grid.ndp
-
-    def kernel(src, dst, send, recv, loc):
-        dp, ex = lax.axis_index("dp"), lax.axis_index("expert")
-        greet([(lax.rem(dp + d, ndp), ex) for d in range(1, ndp)])
-
-        def block(d, slot):
-            target = lax.rem(dp + d, ndp)
-            return remote(
-                src.at[slot, target],
-                dst.at[dp, slot],
-                send.at[d - 1, slot],
-                recv.at[d - 1, slot],
-                (target, ex),
-            )
-
-        for slot in range(grid.slots):
-
-            @pl.when(grid.holds(dp, slot))
-            def _():
-                for d in far_first(ndp):
-                    block(d, slot).start()
-                mine = pltpu.make_async_copy(src.at[slot, dp], dst.at[dp, slot], loc.at[slot])
-                mine.start()
-                mine.wait()
-
-        for slot in range(grid.slots):
-            for d in range(1, ndp):
-
-                @pl.when(grid.holds(lax.rem(dp + ndp - d, ndp), slot))
-                def _():
-                    block(d, slot).wait_recv()
-
-            @pl.when(grid.holds(dp, slot))
-            def _():
-                for d in range(1, ndp):
-                    block(d, slot).wait_send()
-
-    dma = pltpu.SemaphoreType.DMA
-    return pl.pallas_call(
-        kernel,
-        out_shape=jax.ShapeDtypeStruct((ndp, grid.slots) + values.shape[2:], values.dtype),
-        in_specs=[any_spec()],
-        out_specs=any_spec(),
-        scratch_shapes=[
-            dma((ndp - 1, grid.slots)),
-            dma((ndp - 1, grid.slots)),
-            dma((grid.slots,)),
-        ],
-        compiler_params=comm_params(3),
-        name="rows_back",
-    )(values)
+    )(values, act, shared, attn, grad_attn, grad_sgate, grad_sup, grad_misc, hidden)
+
+
+class RowScatter:
+    def __init__(self, grid, width):
+        self.grid, self.width = grid, width
+        self.rows = D // grid.nex
+        self.rows_dev = D // grid.ndev
+
+    def scratch(self):
+        g, w = self.grid, self.width
+        dma = pltpu.SemaphoreType.DMA
+        return [
+            pltpu.VMEM((g.nx, self.rows, w), BF16),
+            pltpu.VMEM((g.nx, self.rows, w), BF16),
+            pltpu.VMEM((g.nx, self.rows, w), BF16),
+            pltpu.VMEM((g.ndp * ROW_PAD, w), BF16),
+            pltpu.VMEM((g.ndp, ROW_PAD, w), BF16),
+            dma((2, 2)),
+            dma((g.nx, 2)),
+            dma((g.ndp, 2)),
+        ]
+
+    def bind(self, source, refs):
+        self.source = source
+        (self.got_core, self.by_x, self.got_x, self.spread, self.got_dp,
+         self.sem_core, self.sem_x, self.sem_dp) = refs
+        g = self.grid
+        self.dp, self.ex = lax.axis_index("dp"), lax.axis_index("expert")
+        self.x, self.c = self.ex // g.nc, lax.rem(self.ex, g.nc)
+
+    def core_copy(self):
+        other = 1 - self.c
+        return remote(
+            self.source.at[:, other], self.got_core, self.sem_core.at[0, 0],
+            self.sem_core.at[0, 1], (self.dp, self.x * 2 + other),
+        )
+
+    def x_copy(self, d):
+        target = lax.rem(self.x + d, self.grid.nx)
+        return remote(
+            self.by_x.at[target], self.got_x.at[d], self.sem_x.at[d, 0], self.sem_x.at[d, 1],
+            (self.dp, target * self.grid.nc + self.c),
+        )
+
+    def dp_copy(self, d):
+        target = lax.rem(self.dp + d, self.grid.ndp)
+        rows = pl.ds(pl.multiple_of(target * ROW_PAD, ROW_PAD), ROW_PAD)
+        return remote(
+            self.spread.at[rows], self.got_dp.at[d], self.sem_dp.at[d, 0], self.sem_dp.at[d, 1],
+            (target, self.ex),
+        )
+
+    def start(self):
+        self.core_copy().start()
+
+    def along_x(self):
+        g = self.grid
+        self.core_copy().wait()
+        for n in range(g.nx):
+            mine = self.source[n, pl.ds(self.c, 1)][0]
+            self.by_x[n] = (mine.astype(F32) + self.got_core[n].astype(F32)).astype(BF16)
+        for d in range(1, g.nx):
+            self.x_copy(d).start()
+
+    def along_dp(self):
+        g = self.grid
+        for d in range(1, g.nx):
+            self.x_copy(d).wait()
+        total = self.by_x[pl.ds(self.x, 1)][0].astype(F32)
+        for d in range(1, g.nx):
+            total += self.got_x[d].astype(F32)
+        to = lax.broadcasted_iota(jnp.int32, (g.ndp * ROW_PAD, self.rows), 0)
+        of = lax.broadcasted_iota(jnp.int32, (g.ndp * ROW_PAD, self.rows), 1)
+        place = (of // self.rows_dev) * ROW_PAD + lax.rem(of, self.rows_dev)
+        move = (to == place).astype(F32).astype(BF16)
+        self.spread[...] = dot(move, total.astype(BF16)).astype(BF16)
+        for d in far_first(g.ndp):
+            self.dp_copy(d).start()
+
+    def finish(self, out):
+        g = self.grid
+        rows = pl.ds(pl.multiple_of(self.dp * ROW_PAD, ROW_PAD), ROW_PAD)
+        total = self.spread[rows].astype(F32)
+        for d in range(1, g.ndp):
+            self.dp_copy(d).wait()
+            total += self.got_dp[d].astype(F32)
+        out[...] = total
 
 
 def expert_gather(grid, rows, gates):
@@ -591,28 +645,65 @@
     )(info, tok, weights, gain, cosine, sine)
 
 
-def attend_back(grid, info, act, weights, query, key, value, lse, grad_heads, cosine, sine):
-    units, length = grid.units, act.shape[1]
+def attend_back(grid, lives, tok, act, weights, query, key, value, lse, grad_heads, cosine, sine,
+                group, early):
+    units, length, ndp, nex = grid.units, act.shape[1], grid.ndp, grid.nex
     blocks = length // QBLOCK
     scale = HEAD_DIM ** (-0.5)
-
-    def kernel(info_ref, act_ref, w_ref, q_ref, k_ref, v_ref, lse_ref, do_ref, cos_ref, sin_ref,
-               back_ref, grad_ref, acc, dq, dk, dv):
+    early_width, late_width = early.shape[1], 3 * D + MISC
+    early_sum, late_sum = RowScatter(grid, early_width), RowScatter(grid, late_width)
+    early = early.reshape(grid.nx, grid.nc, early_sum.rows, early_width)
+    n_early = len(early_sum.scratch())
+    steps = [min(n, units - 1) for n in (2, 5)]
+
+    def kernel(*refs):
+        (live_ref, tok_ref, act_ref, w_ref, q_ref, k_ref, v_ref, lse_ref, do_ref, cos_ref, sin_ref,
+         group_ref, early_ref, rows_out, early_out, late_out,
+         acc, back, dq, dk, dv, grads, gain, late_ref, b_send, b_recv, b_loc) = refs[:27]
+        early_sum.bind(early_ref, refs[27 : 27 + n_early])
+        late_sum.bind(late_ref, refs[27 + n_early :])
         i = pl.program_id(0)
-        live_unit = info_ref[3, i] == 1
-
-        @pl.when((i == 0) | (info_ref[0, i] != info_ref[0, jnp.maximum(i - 1, 0)]))
+        dp, ex = lax.axis_index("dp"), lax.axis_index("expert")
+        unit = dp * units + i
+        working = unit < UNITS_ALL
+        series, head = unit // HEADS, lax.rem(unit, HEADS)
+        slot = jnp.minimum(series - grid.first_series(dp), grid.slots - 1)
+
+        def back_copy(d, which):
+            target = lax.rem(dp + d, ndp)
+            return remote(
+                back.at[which, pl.ds(pl.multiple_of(target * SEG, SEG), SEG)],
+                rows_out.at[dp, which],
+                b_send.at[d - 1, which],
+                b_recv.at[d - 1, which],
+                (target, ex),
+            )
+
+        def back_local(which):
+            return pltpu.make_async_copy(
+                back.at[which, pl.ds(pl.multiple_of(dp * SEG, SEG), SEG)],
+                rows_out.at[dp, which],
+                b_loc.at[which],
+            )
+
+        @pl.when(i == 0)
+        def _():
+            greet(
+                [(lax.rem(dp + d, ndp), ex) for d in range(1, ndp)]
+                + [(dp, lax.rem(ex + d, nex)) for d in range(1, nex)]
+            )
+            early_sum.start()
+            grads[...] = jnp.zeros_like(grads)
+            gain[...] = jnp.zeros_like(gain)
+
+        @pl.when((i == 0) | (head == 0))
         def _():
             acc[...] = jnp.zeros_like(acc)
 
-        @pl.when(jnp.logical_not(live_unit))
+        @pl.when(working)
         def _():
-            grad_ref[...] = jnp.zeros_like(grad_ref)
-
-        @pl.when(live_unit)
-        def _():
-            live = info_ref[2, i]
-            query, key, value, grad = q_ref[0], k_ref[0], v_ref[0], do_ref[0]
+            live = live_ref[i]
+            query, key, value, grad = q_ref[i], k_ref[i], v_ref[i], do_ref[i]
             key_rows = key.astype(F32).T.astype(BF16)
             value_rows = value.astype(F32).T.astype(BF16)
             dk[...] = jnp.zeros_like(dk)
@@ -622,7 +713,7 @@
                 lanes = slice(QBLOCK * block, extent)
                 scores = dot(key_rows[:extent], query[:, lanes]) * scale
                 scores = jnp.where(allowed_mask(extent, block, live), scores, neg_fill)
-                probs = jnp.exp(scores - lse_ref[0, :, lanes])
+                probs = jnp.exp(scores - lse_ref[i, :, lanes])
                 grad_probs = dot(value_rows[:extent], grad[:, lanes])
                 delta = jnp.sum(probs * grad_probs, axis=0, keepdims=True)
                 grad_scores = (probs * (grad_probs - delta)).astype(BF16)
@@ -639,55 +730,113 @@
                 ],
                 axis=0,
             ).astype(BF16)
-            w_rows = w_ref[:, 0].reshape(3 * HEAD_DIM, D)
-            grad_ref[:, 0] = dot(stacked, act_ref[0]).reshape(3, HEAD_DIM, D)
-            acc[...] += dot(stacked, w_rows, 0, 0)
-            back_ref[0] = acc[...].astype(BF16)
-
-    def unit(i, n):
-        return (jnp.minimum(i, units - 1), 0, 0)
-
-    feature = pl.BlockSpec((1, HEAD_DIM, length), unit)
-    table = pl.BlockSpec((HEAD_DIM // 2, length), lambda i, n: (0, 0))
+            weight_grads = dot(stacked, act_ref[slot]).astype(BF16)
+            w_rows = []
+            for n in range(3):
+                at = pl.multiple_of(n * D + head * HEAD_DIM, HEAD_DIM)
+                part = slice(n * HEAD_DIM, (n + 1) * HEAD_DIM)
+                grads[pl.ds(at, HEAD_DIM)] = weight_grads[part]
+                w_rows.append(w_ref[pl.ds(at, HEAD_DIM)])
+            acc[...] += dot(stacked, jnp.concatenate(w_rows, axis=0), 0, 0)
+
+        @pl.when(working & ((head == HEADS - 1) | (i == units - 1)))
+        def _():
+            share = acc[...]
+            residual = tok_ref[slot].astype(F32)
+            normed = residual * lax.rsqrt(
+                jnp.mean(residual * residual, axis=-1, keepdims=True) + eps_norm
+            )
+            gain[...] += jnp.sum(share * normed, axis=0, keepdims=True)
+            back[slot] = share.astype(BF16)
+            for d in far_first(ndp):
+                back_copy(d, slot).start()
+            back_local(slot).start()
+
+        @pl.when(i == steps[0])
+        def _():
+            early_sum.along_x()
+
+        @pl.when(i == steps[1])
+        def _():
+            early_sum.along_dp()
+
+        @pl.when(i == units - 1)
+        def _():
+            grads[3 * D :] = jnp.broadcast_to(gain[...], (ROW_PAD, D)).astype(BF16)
+            late = dot(group_ref[...], grads[...], 1, 1).astype(BF16)
+            late = late.reshape(late_ref.shape[:3] + (late.shape[1],))
+            late_ref[:, :, :, : late.shape[3]] = late
+            late_ref[:, :, :, late.shape[3] :] = jnp.zeros(
+                late_ref.shape[:3] + (late_width - late.shape[3],), BF16
+            )
+            late_sum.start()
+            early_sum.finish(early_out)
+            late_sum.along_x()
+            late_sum.along_dp()
+            for which in range(grid.slots):
+                for d in range(1, ndp):
+
+                    @pl.when(grid.holds(lax.rem(dp + ndp - d, ndp), which))
+                    def _():
+                        back_copy(d, which).wait_recv()
+
+                @pl.when(grid.holds(dp, which))
+                def _():
+                    for d in range(1, ndp):
+                        back_copy(d, which).wait_send()
+                    back_local(which).wait()
+
+            late_sum.finish(late_out)
+
+    def whole(array):
+        return pl.BlockSpec(
+            array.shape, lambda i: (0,) * array.ndim, pipeline_mode=pl.Buffered(1)
+        )
+
+    def whole_out(shape):
+        return pl.BlockSpec(shape, lambda i: (0,) * len(shape))
+
+    dma = pltpu.SemaphoreType.DMA
+    inputs = (tok, act, weights, query, key, value, lse, grad_heads, cosine, sine, group, early)
     return pl.pallas_call(
         kernel,
+        grid=(units,),
         out_shape=(
-            jax.ShapeDtypeStruct((grid.slots, length, D), BF16),
-            jax.ShapeDtypeStruct((3, HEADS, HEAD_DIM, D), F32),
-        ),
-        grid_spec=pltpu.PrefetchScalarGridSpec(
-            num_scalar_prefetch=1,
-            grid=(HEADS,),
-            in_specs=[
-                pl.BlockSpec((1, length, D), lambda i, n: (n[0, i], 0, 0)),
-                pl.BlockSpec((3, 1, HEAD_DIM, D), lambda i, n: (0, n[1, i], 0, 0)),
-                feature,
-                feature,
-                feature,
-                pl.BlockSpec((1, 1, length), unit),
-                feature,
-                table,
-                table,
-            ],
-            out_specs=(
-                pl.BlockSpec((1, length, D), lambda i, n: (n[0, i], 0, 0)),
-                pl.BlockSpec((3, 1, HEAD_DIM, D), lambda i, n: (0, n[1, i], 0, 0)),
-            ),
-            scratch_shapes=[
-                pltpu.VMEM((length, D), F32),
-                pltpu.VMEM((HEAD_DIM, length), F32),
-                pltpu.VMEM((HEAD_DIM, length), F32),
-                pltpu.VMEM((HEAD_DIM, length), F32),
-            ],
-        ),
-        compiler_params=pltpu.CompilerParams(vmem_limit_bytes=40 * MIB),
+            jax.ShapeDtypeStruct((ndp, grid.slots, SEG, D), BF16),
+            jax.ShapeDtypeStruct((ROW_PAD, early_width), F32),
+            jax.ShapeDtypeStruct((ROW_PAD, late_width), F32),
+        ),
+        in_specs=[pl.BlockSpec(memory_space=pltpu.SMEM)] + [whole(v) for v in inputs],
+        out_specs=(
+            any_spec(),
+            whole_out((ROW_PAD, early_width)),
+            whole_out((ROW_PAD, late_width)),
+        ),
+        scratch_shapes=[
+            pltpu.VMEM((length, D), F32),
+            pltpu.VMEM((grid.slots, length, D), BF16),
+            pltpu.VMEM((HEAD_DIM, length), F32),
+            pltpu.VMEM((HEAD_DIM, length), F32),
+            pltpu.VMEM((HEAD_DIM, length), F32),
+            pltpu.VMEM((3 * D + ROW_PAD, D), BF16),
+            pltpu.VMEM((1, D), F32),
+            pltpu.VMEM((grid.nx, grid.nc, late_sum.rows, late_width), BF16),
+            dma((ndp - 1, grid.slots)),
+            dma((ndp - 1, grid.slots)),
+            dma((grid.slots,)),
+        ]
+        + early_sum.scratch()
+        + late_sum.scratch(),
+        compiler_params=pltpu.CompilerParams(
+            collective_id=3, has_side_effects=True, vmem_limit_bytes=56 * MIB
+        ),
         cost_estimate=pl.CostEstimate(
             flops=units * length * length * HEAD_DIM * 2 * 20,
             bytes_accessed=12 * MIB,
             transcendentals=units * length * length,
         ),
         name="attend_back",
-    )(info, act, weights, query, key, value, lse, grad_heads, cosine, sine)
+    )(lives, *inputs)
 
 
 def experts_step(weights, act_all, cot_all, rank_row, rank_col, gates):
@@ -858,6 +1007,8 @@
         grid, tokens, shard, grad_out_low, ranks
     )
 
+    tok_all = tok_all.reshape(grid.slots, length, D)
+
     dense_all = dense_all.reshape(grid.ndev * ROW_PAD, -1)
     row = jnp.arange(D, dtype=jnp.int32)
     row_from = (row // rows_dev) * ROW_PAD + row % rows_dev
@@ -888,7 +1039,7 @@
     heads, act_one, query, key, value, lse = attend(
         grid,
         info,
-        tok_all.reshape(grid.slots, length, D),
+        tok_all,
         qkv_rows,
         gain_first[None, :],
         cosine,
@@ -989,12 +1140,28 @@
     grad_heads = grad_heads.reshape(SERIES_DEV, SEG, D).transpose(0, 2, 1)
     grad_heads = grad_heads.reshape(UNITS_ALL, HEAD_DIM, SEG)
     grad_heads = jnp.pad(grad_heads, ((0, grid.units * ndp - UNITS_ALL), (0, 0), (0, 0)))
-    grad_heads = heads_in(grid, grad_heads.reshape(ndp, grid.units, HEAD_DIM, SEG))
-
-    back, qkv_grads = attend_back(
-        grid, info, act_one, qkv_rows, query, key, value, lse, grad_heads, cosine, sine
-    )
-    back = rows_back(grid, back.reshape(grid.slots, ndp, SEG, D))
+    row_dev = row // rows_dev
+    row_to = ((row_dev % nex) * ndp + row_dev // nex) * rows_dev + row % rows_dev
+    group = (row[:, None] == row_to[None, :]).astype(BF16)
+    attn_grouped = jnp.einsum(
+        "gf,sfp->gsp", group, heads_here.reshape(SERIES_DEV, D, SEG), preferred_element_type=F32
+    )
+    grad_heads, early = heads_in(
+        grid,
+        grad_heads.reshape(ndp, grid.units, HEAD_DIM, SEG),
+        dot(group, act_two, 1, 1).astype(BF16),
+        dot(group, grad_shared_lin, 1, 1).astype(BF16),
+        attn_grouped.astype(BF16).reshape(D, TOK_DEV),
+        (grad_attn_low, grad_sgate_lin, grad_sup_lin, grad_misc),
+        shared_hidden,
+    )
+    gain_two_grouped = dot(group, grad_gain_two.astype(BF16)[:, None]).astype(BF16)
+    early = early.at[:, D + 3 * FF + EXPERTS + 2].set(gain_two_grouped[:, 0])
+
+    back, early, late = attend_back(
+        grid, info[2], tok_all, act_one, qkv_rows.reshape(3 * D, D), query, key, value, lse,
+        grad_heads, cosine, sine, group, early,
+    )
     grad_act_one = jnp.stack(
         [
             sum(
@@ -1007,56 +1174,12 @@
     ).reshape(TOK_DEV, D)
     scale_one = lax.rsqrt(jnp.mean(residual * residual, axis=-1, keepdims=True) + eps_norm)
     normed_one = residual * scale_one
-    grad_gain_one = jnp.sum(grad_act_one * normed_one, axis=0)
     weighted_one = grad_act_one * gain_first
     grad_tokens = grad_mixed + scale_one * (
         weighted_one - normed_one * jnp.mean(weighted_one * normed_one, axis=-1, keepdims=True)
     )
 
-    row_dev = row // rows_dev
-    row_to = ((row_dev % nex) * ndp + row_dev // nex) * ROW_PAD + row % rows_dev
-    group = (jnp.arange(grid.ndev * ROW_PAD)[:, None] == row_to[None, :]).astype(BF16)
-
-    def scatter_rows(padded):
-        width = padded.shape[1]
-        first = lax.all_to_all(
-            padded.reshape(nex, ndp * ROW_PAD, width), "expert", split_axis=0, concat_axis=0,
-            tiled=True,
-        )
-        first = jnp.sum(first.astype(F32), axis=0).astype(BF16)
-        second = lax.all_to_all(
-            first.reshape(ndp, ROW_PAD, width), "dp", split_axis=0, concat_axis=0, tiled=True
-        )
-        return jnp.sum(second.astype(F32), axis=0)[:rows_dev]
-
-    def weight_grad(left, right):
-        return dot(left, right, 0, 0).astype(BF16)
-
-    g_misc = dot(act_two, grad_misc, 0, 0).astype(BF16)
-    g_misc = jnp.where(
-        jnp.arange(MISC)[None, :] == EXPERTS + 2, grad_gain_two[:, None].astype(BF16), g_misc
-    )
-    early = jnp.concatenate(
-        [
-            weight_grad(attn_low, grad_attn_low),
-            weight_grad(act_two, grad_sgate_lin),
-            weight_grad(act_two, grad_sup_lin),
-            weight_grad(grad_shared_lin, shared_hidden),
-            g_misc,
-        ],
-        axis=1,
-    )
-    early = scatter_rows(dot(group, early).astype(BF16))
-    late = jnp.concatenate(
-        [
-            dot(group, qkv_grads.reshape(3 * D, D).astype(BF16), 1, 1).astype(BF16),
-            dot(group, jnp.broadcast_to(grad_gain_one[:, None], (D, MISC)).astype(BF16)).astype(
-                BF16
-            ),
-        ],
-        axis=1,
-    )
-    late = scatter_rows(late)
+    early, late = early[:rows_dev], late[:rows_dev]
     misc_at = D + 3 * FF
     dense_grad = jnp.concatenate(
         [

time: 681 us -> 565 us (0.83)
  waiting for transfers between devices: 127 us -> 21.1 us
  starting transfers between devices: 33.7 us -> 13.1 us
  matrix products: 82.6 us -> 66 us
  Pallas kernels: 319 us -> 333 us
  other arithmetic: 48.2 us -> 61.8 us
    all_to_all x4 -> x0, waiting for transfers between devices: 97.6 us -> none  [the longest x2 63.2 us: scatter_rows(): lax.all_to_all(padded.reshape(nex, ndp * ROW_PAD, width), 'expert', split...]
    all_to_all x4 -> x0, starting transfers between devices: 21.1 us -> none  [the longest x2 11.1 us: scatter_rows(): lax.all_to_all(first.reshape(ndp, ROW_PAD, width), 'dp', split_axis=0, co...]
    concatenate x1, other arithmetic: 10.9 us -> 28.7 us  [local(): jnp.concatenate([grad_e_gate.astype(BF16), grad_e_up.astype(BF16), jnp.co...]
    all_to_all x1, waiting for transfers between devices: 16.4 us -> 0.01 us  [local(): lax.all_to_all(routed_parts, 'expert', split_axis=0, concat_axis=0, tiled...]
    pallas_call x3 -> x2, Pallas kernels: 101 us -> 116 us  [the longest x1 96.8 us: attend_back(): pl.pallas_call(kernel, grid=(units,), out_shape=(jax.ShapeDtypeStruct((nd...]
    dot_general x20 -> x15, matrix products: 48.1 us -> 34.3 us  [dot(): lax.dot_general(left, right, (((left_dim,), (right_dim,)), ((), ())), pre...]
    reduce_sum x5 -> x1, other arithmetic: 9.8 us -> 0.43 us  [local(): jnp.mean(weighted_one * normed_one, axis=-1, keepdims=True)]
    all_to_all x1, waiting for transfers between devices: 13.4 us -> 21.1 us  [local(): lax.all_to_all(gin_parts, 'expert', split_axis=0, concat_axis=0, tiled=True)]
  transfers between devices with their start and end apart: 9 -> 5, of which waited for: 6 -> 1; matrix products, arithmetic and copies ran while one was open for 17% -> 15% of each run, Pallas kernels for 38% -> 49%
where the time goes in v2:
time: 565 us; the launch traced here: 561 us
  Pallas kernels  333 us (59%)
  matrix products  66 us (12%)
  other arithmetic  61.8 us (11%)
  local copies, waits for them, and re-layouts  50.4 us (9%)
  waiting for transfers between devices  21.1 us (4%)
  between operations  15.5 us (3%)
  starting transfers between devices  13.1 us (2%)
    pallas_call x1, Pallas kernels, attend_back(): pl.pallas_call(kernel, grid=(units,), out_shape=(jax.ShapeDtypeStruct((nd...  96.8 us
    pallas_call x1, Pallas kernels, first_exchange(): pl.pallas_call(kernel, out_shape=(jax.ShapeDtypeStruct((grid.slots, ndp,...  74.2 us
    pallas_call x1, Pallas kernels, experts_step(): pl.pallas_call(kernel, grid=(sources,), out_shape=(jax.ShapeDtypeStruct((...  60.2 us
    pallas_call x1, Pallas kernels, heads_out(): pl.pallas_call(kernel, out_shape=jax.ShapeDtypeStruct((ndp,) + values.sha...  40.6 us
    dot_general x15, matrix products, dot(): lax.dot_general(left, right, (((left_dim,), (right_dim,)), ((), ())), pre...  34.3 us
    concatenate x1, other arithmetic, local(): jnp.concatenate([grad_e_gate.astype(BF16), grad_e_up.astype(BF16), jnp.co...  28.7 us
    pallas_call x1, Pallas kernels, attend(): pl.pallas_call(kernel, out_shape=(feature, jax.ShapeDtypeStruct((grid.slo...  21.2 us
    all_to_all x1, waiting for transfers between devices, local(): lax.all_to_all(gin_parts, 'expert', split_axis=0, concat_axis=0, tiled=True)  21.1 us
  transfers between devices with their start and end apart: 5, of which 1 were waited for; matrix products, arithmetic and copies ran while one was open for 15% of the time, Pallas kernels for 49%

profile of v2, /device:TPU:0, one launch (start us, length us, event | category | flops | bytes accessed | tf_op | source)
XLA Modules:
  0.0 560.6 jit_solution(14220733749106470568)
XLA Ops:
  7.3 1.8 convert_element_type.312
  9.1 2.8 fusion.21
  16.3 74.2 %first_exchange.1 = (bf16[2,8,128,384]{3,2,1,0:T(8,128)(2,1)}, bf16[32,16,6272]{2,1,0:T(8,128)(2,1)}, bf16[4,768,384]{2,1,0:T(8,128)(2,1)}, s32[4,8,768]{2,1,0:T(8,128)}) custom-call(bf16[6,128,384]{2,1,0:T(8,128)(2,1)} %tok.1, bf16[16,6272]{1,0:T(8,128)(2,1)} %pad.6.shd, bf16[768,384]{1,0:T(8,128)(2,1)} %bitcast.145, s32[8,768]{1,0:T(8,128)} %fusion.54.rank_in), custom_call_target="tpu_custom_call" | custom-call | tf_op jit(solution)/shard_map/first_exchange/pallas_call | solution.py:264
  90.5 4.7 convolution_convert_fusion
  95.5 1.6 copy-done.39
  97.5 2.2 convolution_convert_fusion.3.refs_3_
  99.8 21.2 %attend.1 = (bf16[9,32,1024]{2,1,0:T(8,128)(2,1)S(1)}, bf16[2,1024,384]{2,1,0:T(8,128)(2,1)S(1)}, bf16[9,32,1024]{2,1,0:T(8,128)(2,1)S(1)}, bf16[9,32,1024]{2,1,...) custom-call(s32[4,12]{1,0:T(4,128)S(1)} %pad_add_fusion.info_ref, ...), custom_call_target="tpu_custom_call" | custom-call | flops 4831838208 | bytes 8388608 | tf_op jit(solution)/shard_map/attend/pallas_call | solution.py:611
  126.0 40.6 %heads_out.1 = bf16[8,9,32,128]{3,2,1,0:T(8,128)(2,1)} custom-call(bf16[9,32,1024]{2,1,0:T(8,128)(2,1)} %copy-done.6), custom_call_target="tpu_custom_call" | custom-call | tf_op jit(solution)/shard_map/heads_out/pallas_call | solution.py:312
  168.0 1.8 multiply_reduce_fusion.4
  173.0 20.7 %expert_gather.1 = (bf16[4,768,384]{2,1,0:T(8,128)(2,1)}, f32[4,8,768]{2,1,0:T(8,128)}) custom-call(bf16[768,384]{1,0:T(8,128)(2,1)} %copy-done.21, f32[8,768]{1,0:T(8,128)} %copy.123.gate), custom_call_target="tpu_custom_call" | custom-call | tf_op jit(solution)/shard_map/expert_gather/pallas_call | solution.py:536
  194.2 1.6 constant_dynamic-slice_fusion.1
  195.9 2.5 copy.125.rrow_ref
  198.3 1.5 constant_dynamic-slice_fusion.gate_ref
  199.9 1.6 fusion.146.rcol_ref
  201.5 6.5 %copy.120 = bf16[8,2,144,1536]{3,2,0,1:T(8,128)(2,1)} copy(bf16[8,2,144,1536]{3,2,1,0:T(8,128)(2,1)} %bitcast.148) | data formatting | bytes 14155776 | tf_op jit(solution)/shard_map/all_gather | solution.py:977
  207.9 60.2 %experts_step.1 = (bf16[4,768,384]{2,1,0:T(8,128)(2,1)}, bf16[4,768,384]{2,1,0:T(8,128)(2,1)}, f32[4,2,768]{2,1,0:T(2,128)}, bf16[2,4,384,384]{3,2,1,0:T(8,128)(...) custom-call(bf16[2,1152,1536]{2,1,0:T(8,128)(2,1)} %bitcast.149, ...), custom_call_target="tpu_custom_call" | custom-call | flops 28991029248 | bytes 52428800 | tf_op jit(solution)/shard_map/experts_step/pallas_call | solution.py:904
  268.2 4.0 fusion.34
  272.2 4.0 fusion.37
  277.6 1.4 fusion.43
  279.3 7.8 %convolution_convert_fusion.2 = bf16[2,384,1536]{2,1,0:T(8,128)(2,1)S(1)} fusion(bf16[2,1536,384]{2,1,0:T(8,128)(2,1)S(1)} %bitcast.174, bf16[2,1536,1536]{2,1,0:T(8,128)(2,1)} %bitcast.169), kind=kOutput, calls=%fused_computation.19 | convolution fusion | flops 3625058304 | bytes 14155776 | tf_op jit(solution)/shard_map/erd,erf->edf/dot_general | solution.py:1078
  287.2 4.2 convolution_convert_fusion.1
  291.3 28.7 %maximum_maximum_fusion = bf16[2,1152,1536]{2,1,0:T(8,128)(2,1)S(1)} fusion(bf16[2,384,384]{2,1,0:T(8,128)(2,1)S(1)} %fusion.43, bf16[2,384,384]{2,1,0:T(8,128)(2,1)S(1)} %fusion.40, bf16[2,384,384]{2,1,0:T(8,128)(2,1)S(1)} %fusion.37, bf16[2,384,384]{2,1,0:T(8,128)(2,1)S(1)} %fusion.34, bf16[2,384,1536]{2,1,0:T(8,128)(2,1)S(1)} %convolution_convert_fusion.1, ...), kind=kLoop, calls=%fused_computation.5 | loop fusion | flops 42467328 | bytes 14155776 | tf_op jit(solution)/shard_map/concatenate | solution.py:1086
  320.0 3.5 copy.165
  325.5 1.6 fusion.69
  327.0 2.8 fusion.60
  331.3 5.2 multiply_convert_fusion
  336.4 3.9 all-to-all-start.2
  341.6 2.2 convert_element_type.332
  346.3 4.5 all-to-all-start.1
  350.9 3.9 fusion.47
  358.3 21.1 %all-to-all-done.1 = bf16[4,768,384]{2,1,0:T(8,128)(2,1)} async-done(((bf16[4,768,384]{2,1,0:T(8,128)(2,1)}), bf16[4,768,384]{2,1,0:T(8,128)(2,1)}, u32[]{:S(2)}, u32[]{:S(2)}) %all-to-all-start.1) | async-done | bytes 2359328 | tf_op jit(solution)/shard_map/all_to_all | solution.py:1068
  379.4 4.5 all-to-all-start
  383.9 2.4 convert_reduce_fusion
  386.4 2.9 convolution_add_fusion.3
  389.3 2.9 convolution_add_fusion.2
  392.2 1.5 multiply_reduce_fusion.1
  394.8 2.3 convolution_convert_fusion.6
  398.5 1.7 copy-done.1
  400.2 1.8 copy-done.3
  401.9 1.7 copy-done.5
  403.6 19.0 %heads_in.1 = (bf16[9,32,1024]{2,1,0:T(8,128)(2,1)S(1)}, bf16[384,5120]{1,0:T(8,128)(2,1)}) custom-call(bf16[8,9,32,128]{3,2,1,0:T(8,128)(2,1)S(1)} %bitcast.138, bf16[384,768]{1,0:T(8,128)(2,1)S(1)} %convolution_convert_fusion.5.act_ref, bf16[384,768]{1,0:T(8,128)(2,1)S(1)} %convolution_convert_fusion.4.shared_ref, bf16[384,768]{1,0:T(8,128)(2,1)S(1)} %copy.134.attn_ref, ...), custom_call_target="tpu_custom_call" | custom-call | tf_op jit(solution)/shard_map/heads_in/pallas_call | solution.py:362
  423.7 1.7 reshape_select_fusion
  425.3 1.8 scatter.4
  427.1 96.8 %attend_back.1 = (bf16[8,2,128,384]{3,2,1,0:T(8,128)(2,1)}, f32[16,5120]{1,0:T(8,128)}, f32[16,1280]{1,0:T(8,128)}) custom-call(s32[12]{0:T(128)} %copy-done.67, bf16[2,1024,384]{2,1,0:T(8,128)(2,1)} %bitcast.139, bf16[2,1024,384]{2,1,0:T(8,128)(2,1)} %copy-done.12, bf16[1152,384]{1,0:T(8,128)(2,1)} %copy-done.11, bf16[9,32,1024]{2,1,0:T(8,128)(2,1)} %copy-done.13, ...), custom_call_target="tpu_custom_call" | custom-call | flops 12079595520 | bytes 12582912 | tf_op jit(solution)/shard_map/attend_back/pallas_call | solution.py:801
  531.9 2.3 convert_reduce_fusion.1
  534.4 3.2 fusion.51
  538.9 3.6 fusion.12
  544.5 9.1 %multiply_add_fusion.1 = (f32[2,221184]{1,0:T(2,128)}, f32[2,221184]{1,0:T(2,128)}, f32[2,221184]{1,0:T(2,128)}, f32[2,221184]{1,0:T(2,128)}) fusion(f32[2,221184]{1,0:T(2,128)S(1)} %copy-done.41, f32[2,221184]{1,0:T(2,128)S(1)} %copy-done.35, f32[2,221184]{1,0:T(2,128)S(1)} %bitcast.150, f32[2,221184]{1,0:T(2,128)S(1)} %copy-done.42, ...), kind=kLoop, calls=%fused_computation.39 | loop fusion | flops 7520256 | bytes 15925248 | tf_op jit(solution)/shard_map/add | solution.py:51
  (238 shorter events, 41.9 us)
Async XLA Ops:
  7.2 194.3 %all-gather.3.cloned.1.call-start = ((), (), s32[]{:S(2)}) async-start(), calls=%async_computation.5 | async-start | bytes 7962624 | tf_op jit(solution)/shard_map/all_gather | solution.py:977
  7.2 4.7 copy-start.64
  9.1 3.1 copy-start.44
  12.0 3.3 copy-start.48
  12.0 526.9 %reduce-scatter.2.cloned.1.call-start = ((), (), s32[]{:S(2)}) async-start(), calls=%async_computation.4 | async-start | bytes 7962624 | tf_op jit(solution)/shard_map/reduce_scatter | solution.py:1095
  14.2 82.9 %copy-start.67 = (s32[12]{0:T(128)}, s32[12]{0:T(128)S(1)}, u32[]{:S(2)}) copy-start(s32[12]{0:T(128)S(1)} %gather_fusion) | copy-start | bytes 148
  95.2 4.6 copy-start.9
  97.1 23.9 %copy-start.53 = (f32[384]{0:T(512)}, f32[384]{0:T(512)S(1)}, u32[]{:S(2)}) copy-start(f32[384]{0:T(512)S(1)} %get-tuple-element.75) | copy-start | bytes 4612
  97.5 23.4 %copy-start.7 = (f32[16,1024]{1,0:T(8,128)}, f32[16,1024]{1,0:T(8,128)S(1)}, u32[]{:S(2)}) copy-start(f32[16,1024]{1,0:T(8,128)S(1)} %get-tuple-element.93.sin_ref.refs_10_) | copy-start | bytes 196612
  97.5 23.4 %copy-start.8 = (f32[16,1024]{1,0:T(8,128)}, f32[16,1024]{1,0:T(8,128)S(1)}, u32[]{:S(2)}) copy-start(f32[16,1024]{1,0:T(8,128)S(1)} %get-tuple-element.94.cos_ref.refs_9_) | copy-start | bytes 196612
  99.8 21.2 %copy-start.11 = (bf16[1152,384]{1,0:T(8,128)(2,1)}, bf16[1152,384]{1,0:T(8,128)(2,1)S(1)}, u32[]{:S(2)}) copy-start(bf16[1152,384]{1,0:T(8,128)(2,1)S(1)} %convolution_convert_fusion.3.refs_3_) | copy-start | bytes 2654212
  126.0 42.0 %copy-start.26 = (bf16[6,128,384]{2,1,0:T(8,128)(2,1)S(1)}, bf16[6,128,384]{2,1,0:T(8,128)(2,1)}, u32[]{:S(2)}) copy-start(bf16[6,128,384]{2,1,0:T(8,128)(2,1)} %tok.1) | copy-start | bytes 1769476
  170.0 3.0 copy-start.21
  170.0 23.7 %copy-start.52 = (s32[4,8,768]{2,1,0:T(8,128)S(1)}, s32[4,8,768]{2,1,0:T(8,128)}, u32[]{:S(2)}) copy-start(s32[4,8,768]{2,1,0:T(8,128)} %get-tuple-element.54) | copy-start | bytes 294916
  171.5 152.9 %copy-start.23 = (f32[768,128]{1,0:T(8,128)}, f32[768,128]{1,0:T(8,128)S(1)}, u32[]{:S(2)}) copy-start(f32[768,128]{1,0:T(8,128)S(1)} %fusion.92) | copy-start | bytes 1179652
  268.2 8.0 %copy-start.69 = (bf16[2,4,384,1536]{3,2,1,0:T(8,128)(2,1)S(1)}, bf16[2,4,384,1536]{3,2,1,0:T(8,128)(2,1)}, u32[]{:S(2)}) copy-start(bf16[2,4,384,1536]{3,2,1,0:T(8,128)(2,1)} %get-tuple-element.72) | copy-start | bytes 28311556
  272.2 4.0 copy-start.71
  277.6 9.5 %slice-start = ((s8[9437184]{0:T(1024)(128)(4,1)}), s8[4194304]{0:T(1024)(128)(4,1)S(1)}, s32[]{:S(2)}) async-start(s8[9437184]{0:T(1024)(128)(4,1)} %bitcast.166), calls=%async_computation.6 | async-start | bytes 8388608
  279.3 7.8 %slice-start.1 = ((s8[9437184]{0:T(1024)(128)(4,1)}), s8[4194304]{0:T(1024)(128)(4,1)S(1)}, s32[]{:S(2)}) async-start(s8[9437184]{0:T(1024)(128)(4,1)} %bitcast.166), calls=%async_computation.7 | async-start | bytes 8388608
  279.3 7.9 %slice-start.2 = ((s8[9437184]{0:T(1024)(128)(4,1)}), s8[1048576]{0:T(1024)(128)(4,1)S(1)}, s32[]{:S(2)}) async-start(s8[9437184]{0:T(1024)(128)(4,1)} %bitcast.166), calls=%async_computation.8 | async-start | bytes 2097152
  323.5 3.5 copy-start.22
  323.6 6.3 %copy-start.55 = (s32[384]{0:T(512)}, s32[384]{0:T(512)S(1)}, u32[]{:S(2)}) copy-start(s32[384]{0:T(512)S(1)} %fusion.112) | copy-start | bytes 4612
  324.7 6.6 %copy-start.58 = (f32[768]{0:T(1024)}, f32[768]{0:T(1024)S(1)}, u32[]{:S(2)}) copy-start(f32[768]{0:T(1024)S(1)} %fusion.94) | copy-start | bytes 9220
  327.0 2.8 copy-start.40
  336.4 14.4 %copy-start.4 = (bf16[768,1536]{1,0:T(8,128)(2,1)}, bf16[768,1536]{1,0:T(8,128)(2,1)S(1)}, u32[]{:S(2)}) copy-start(bf16[768,1536]{1,0:T(8,128)(2,1)S(1)} %get-tuple-element.88.hid_ref) | copy-start | bytes 7077892
  336.4 9.9 %all-to-all-start.2 = ((f32[4,2,768]{2,1,0:T(2,128)}), f32[4,2,768]{2,1,0:T(2,128)}, u32[]{:S(2)}, u32[]{:S(2)}) async-start(f32[4,2,768]{2,1,0:T(2,128)} %get-tuple-element.58), calls=%async_computation.2 | async-start | bytes 49152 | tf_op jit(solution)/shard_map/all_to_all | solution.py:1069
  346.3 33.1 %all-to-all-start.1 = ((bf16[4,768,384]{2,1,0:T(8,128)(2,1)}), bf16[4,768,384]{2,1,0:T(8,128)(2,1)}, u32[]{:S(2)}, u32[]{:S(2)}) async-start(bf16[4,768,384]{2,1,0:T(8,128)(2,1)} %get-tuple-element.57), calls=%async_computation.1 | async-start | bytes 4718592 | tf_op jit(solution)/shard_map/all_to_all | solution.py:1068
  350.9 4.0 copy-start.24
  350.9 4.2 copy-start.56
  354.8 2.6 copy-start.25
  379.4 152.4 %all-to-all-start = ((bf16[4,768,384]{2,1,0:T(8,128)(2,1)}), bf16[4,768,384]{2,1,0:T(8,128)(2,1)}, u32[]{:S(2)}, u32[]{:S(2)}) async-start(bf16[4,768,384]{2,1,0:T(8,128)(2,1)} %get-tuple-element.56), calls=%async_computation | async-start | bytes 4718592 | tf_op jit(solution)/shard_map/all_to_all | solution.py:1070
  383.9 2.5 copy-start.2
  386.4 2.9 copy-start
  389.3 2.9 copy-start.19
  403.6 19.8 %copy-start.57 = (s32[384]{0:T(512)S(1)}, s32[384]{0:T(512)}, u32[]{:S(2)}) copy-start(s32[384]{0:T(512)} %copy-done.55) | copy-start | bytes 4612
  524.0 6.1 %copy-start.47 = (bf16[8,2,128,384]{3,2,1,0:T(8,128)(2,1)S(1)}, bf16[8,2,128,384]{3,2,1,0:T(8,128)(2,1)}, u32[]{:S(2)}) copy-start(bf16[8,2,128,384]{3,2,1,0:T(8,128)(2,1)} %get-tuple-element.66) | copy-start | bytes 4718596
  531.8 2.5 copy-start.33
  531.9 2.5 copy-start.60
  531.9 2.5 copy-start.61
  531.9 2.5 copy-start.62
  534.3 3.3 copy-start.45
  534.3 3.3 copy-start.46
  534.4 3.3 copy-start.49
  534.4 3.3 copy-start.50
  534.4 3.3 copy-start.51
  538.9 5.0 copy-start.42
  538.9 5.0 copy-start.43
  543.9 9.7 %copy-start.34 = (f32[1,2,144,1536]{3,1,2,0:T(2,128)}, f32[1,2,144,1536]{3,1,2,0:T(2,128)S(1)}, u32[]{:S(2)}) copy-start(f32[1,2,144,1536]{3,1,2,0:T(2,128)S(1)} %copy.159) | copy-start | bytes 5308420
  (34 other events, 50.3 us)
Sparse Core Ops, SparseCore 0:
  12.1 154.8 all-gather.2
  323.7 130.4 reduce-scatter.1

commit v3 on v2

v3 whole, which is shorter than its diff:
```python
import functools
import math

import jax
import jax.numpy as jnp
from jax import lax
from jax.experimental import pallas as pl
from jax.experimental.pallas import tpu as pltpu
from jax.sharding import PartitionSpec as P

D = 384
HEADS = 12
HEAD_DIM = 32
FF = 1536
EXPERTS = 8
TOP = 2
SEG = 128
SERIES_DEV = 6
STEP = 8
TOK_DEV = 768
CAP = 384
ROW_PAD = 16
MISC = 128
UNITS_ALL = SERIES_DEV * HEADS
QBLOCK = 256
MIB = 1 << 20

eps_norm = 1e-06
beta_one = 0.5
beta_two = 0.5
learn_rate = 0.02
weight_decay = 0.1
eps_adam = 1e-08
average_keep = 0.9
rope_base = 10000.0
neg_fill = -1e30

MESH = pl.DeviceIdType.MESH
F32 = jnp.float32
BF16 = jnp.bfloat16


def adamw_update(weights, grads, first, second, average):
    first_new = beta_one * first + (1.0 - beta_one) * grads
    second_new = beta_two * second + (1.0 - beta_two) * grads * grads
    first_hat = first_new / (1.0 - beta_one**STEP)
    second_hat = second_new / (1.0 - beta_two**STEP)
    weights_new = weights - learn_rate * (
        first_hat / (jnp.sqrt(second_hat) + eps_adam) + weight_decay * weights
    )
    average_new = average_keep * average + (1.0 - average_keep) * weights_new
    return (first_new, second_new, weights_new, average_new)


def dot(left, right, left_dim=1, right_dim=0):
    return lax.dot_general(
        left, right, (((left_dim,), (right_dim,)), ((), ())), preferred_element_type=F32
    )


class Grid:
    def __init__(self, ndp, nex):
        self.ndp, self.nex = ndp, nex
        self.nz = math.gcd(ndp, 4)
        self.ny = ndp // self.nz
        self.nc = math.gcd(nex, 2)
        self.nx = nex // self.nc
        self.ndev = ndp * nex
        self.units = -(-UNITS_ALL // ndp)
        spans = [
            [u // HEADS for u in range(self.units * o, min(self.units * (o + 1), UNITS_ALL))]
            for o in range(ndp)
        ]
        self.owned = [sorted(set(s)) for s in spans]
        self.slots = max(len(s) for s in self.owned)

    def first_series(self, owner):
        return (owner * self.units) // HEADS

    def holds(self, owner, slot):
        begin = owner * self.units
        end = jnp.minimum(begin + self.units, UNITS_ALL)
        return (begin // HEADS + slot) * HEADS < end


def remote(src, dst, send, recv, target):
    return pltpu.make_async_remote_copy(
        src_ref=src,
        dst_ref=dst,
        send_sem=send,
        recv_sem=recv,
        device_id=target,
        device_id_type=MESH,
    )


def greet(peers):
    barrier = pltpu.get_barrier_semaphore()
    for peer in peers:
        pl.semaphore_signal(barrier, inc=1, device_id=peer, device_id_type=MESH)
    pl.semaphore_wait(barrier, len(peers))


def any_spec():
    return pl.BlockSpec(memory_space=pl.ANY)


def far_first(n):
    return sorted(range(1, n), key=lambda d: -min(d, n - d))


def comm_params(number):
    return pltpu.CompilerParams(collective_id=number, has_side_effects=True)


class DenseGather:
    def __init__(self, grid):
        self.grid = grid

    def scratch(self):
        dma = pltpu.SemaphoreType.DMA
        return [dma((self.grid.ndev,)), dma((self.grid.ndev,)), dma]

    def bind(self, shard, out, refs):
        g = self.grid
        self.shard, self.out = shard, out
        self.send, self.recv, self.loc = refs
        dp, ex = lax.axis_index("dp"), lax.axis_index("expert")
        self.z, self.y = dp // g.ny, lax.rem(dp, g.ny)
        self.x, self.c = ex // g.nc, lax.rem(ex, g.nc)
        self.zs = [0] + far_first(g.nz)[::-1]
        self.count = 0
        self.ends = []

    def place(self, dz, dy, dx, dc):
        g = self.grid
        return (
            lax.rem(self.z + dz, g.nz) * g.ny + lax.rem(self.y + dy, g.ny),
            lax.rem(self.x + dx, g.nx) * g.nc + lax.rem(self.c + dc, g.nc),
        )

    def slot(self, dz, dy, dx, dc):
        g = self.grid
        dp, ex = self.place(g.nz - dz, g.ny - dy, g.nx - dx, g.nc - dc)
        return dp * g.nex + ex

    def copy(self, ref, slot, number, target):
        return remote(ref, self.out.at[slot], self.send.at[number], self.recv.at[slot], target)

    def go(self, slot, target):
        ref = self.out.at[slot]
        if self.count < self.own_sends():
            ref = self.shard
        self.copy(ref, slot, self.count, target).start()
        self.count += 1

    def own_sends(self):
        g = self.grid
        return g.nz + g.ny + g.nx + g.nc - 4

    def wait(self, slot):
        self.copy(self.shard, slot, 0, self.place(0, 0, 0, 0)).wait_recv()

    def onward(self, slot, axes):
        g = self.grid
        if "y" in axes:
            for dy in range(1, g.ny):
                self.go(slot, self.place(0, dy, 0, 0))
        if "x" in axes:
            for dx in range(1, g.nx):
                self.go(slot, self.place(0, 0, dx, 0))
        for dc in range(1, g.nc):
            self.go(slot, self.place(0, 0, 0, dc))

    def own(self):
        return pltpu.make_async_copy(self.shard, self.out.at[self.slot(0, 0, 0, 0)], self.loc)

    def start(self):
        own = self.slot(0, 0, 0, 0)
        for dz in far_first(self.grid.nz):
            self.go(own, self.place(dz, 0, 0, 0))
        self.onward(own, "yx")
        self.own().start()

    def pass_z(self):
        for dz in self.zs[1:]:
            slot = self.slot(dz, 0, 0, 0)
            self.wait(slot)
            self.onward(slot, "yx")

    def pass_y(self):
        for dy in range(1, self.grid.ny):
            for dz in self.zs:
                slot = self.slot(dz, dy, 0, 0)
                self.wait(slot)
                self.onward(slot, "x")

    def pass_x(self):
        g = self.grid
        for dx in range(1, g.nx):
            for dy in range(g.ny):
                for dz in self.zs:
                    slot = self.slot(dz, dy, dx, 0)
                    self.wait(slot)
                    self.onward(slot, "")

    def finish(self):
        g = self.grid
        for dc in range(1, g.nc):
            for dx in range(g.nx):
                for dy in range(g.ny):
                    for dz in self.zs:
                        self.wait(self.slot(dz, dy, dx, dc))
        for number in range(g.ndev - 1):
            self.copy(self.shard, 0, number, self.place(0, 0, 0, 0)).wait_send()
        self.own().wait()


class RowGather:
    parts = 3

    def __init__(self, grid):
        self.grid = grid

    def scratch(self):
        g, n = self.grid, self.parts
        dma = pltpu.SemaphoreType.DMA
        return [dma((g.nx + g.nc, n)), dma((g.nex, n)), dma((g.nx, n)), dma]

    def bind(self, src, dst, refs):
        g = self.grid
        self.src, self.dst = src, dst
        self.send, self.recv, self.fsend, self.loc = refs
        self.dp, self.ex = lax.axis_index("dp"), lax.axis_index("expert")
        self.x, self.c = self.ex // g.nc, lax.rem(self.ex, g.nc)
        self.sends = []

    def rows(self, part):
        extent = TOK_DEV // self.parts
        return pl.ds(part * extent, extent)

    def slot_at(self, owner, target):
        return lax.rem(owner - target - 1 + 2 * self.grid.nex, self.grid.nex)

    def go(self, ref, owner, part, sem, target):
        slot = self.slot_at(owner, target)
        copy = remote(
            ref, self.dst.at[slot, self.rows(part)], sem, self.recv.at[slot, part],
            (self.dp, target),
        )
        copy.start()
        self.sends.append(copy)

    def arrived(self, owner, part):
        slot = self.slot_at(owner, self.ex)
        remote(
            self.src.at[self.rows(part)], self.dst.at[slot, self.rows(part)], self.send.at[0, 0],
            self.recv.at[slot, part], (self.dp, self.ex),
        ).wait_recv()

    def beside(self, dc):
        g = self.grid
        return self.x * g.nc + lax.rem(self.c + dc, g.nc)

    def start(self):
        g = self.grid
        for part in range(self.parts):
            for dx in range(1, g.nx):
                target = lax.rem(self.x + dx, g.nx) * g.nc + self.c
                ref = self.src.at[self.rows(part)]
                self.go(ref, self.ex, part, self.send.at[dx - 1, part], target)
        for part in range(self.parts):
            for dc in range(1, g.nc):
                ref = self.src.at[self.rows(part)]
                self.go(ref, self.ex, part, self.send.at[g.nx + dc - 2, part], self.beside(dc))
        self.own = pltpu.make_async_copy(self.src, self.dst.at[g.nex - 1], self.loc)
        self.own.start()

    def pass_on(self, part):
        g = self.grid
        for dx in range(1, g.nx):
            owner = lax.rem(self.x + g.nx - dx, g.nx) * g.nc + self.c
            self.arrived(owner, part)
            for dc in range(1, g.nc):
                ref = self.dst.at[self.slot_at(owner, self.ex), self.rows(part)]
                self.go(ref, owner, part, self.fsend.at[dx - 1, part], self.beside(dc))

    def finish(self):
        g = self.grid
        for part in range(self.parts):
            for dc in range(1, g.nc):
                for dx in range(g.nx):
                    owner = lax.rem(self.x + g.nx - dx, g.nx) * g.nc
                    self.arrived(owner + lax.rem(self.c + g.nc - dc, g.nc), part)
        for copy in self.sends:
            copy.wait_send()
        self.own.wait()


def first_exchange(grid, tokens, shard, cot, ranks):
    ndp, nex = grid.ndp, grid.nex

    def kernel(tok, shd, cot_in, rank_in, tok_out, dense_out, cot_out, rank_out,
               t_send, t_recv, e_send, e_recv, loc, *more_refs):
        dp, ex = lax.axis_index("dp"), lax.axis_index("expert")

        def off(value, by, n):
            return lax.rem(value + by, n)

        peers = [(off(dp, d, ndp), ex) for d in range(1, ndp)]
        peers += [(dp, off(ex, d, nex)) for d in range(1, nex)]
        greet(peers)
        dense = DenseGather(grid)
        dense.bind(shd, dense_out, more_refs[4:])
        dense.start()

        def token_copy(d, slot, src_series, sender, target):
            return remote(
                tok.at[src_series],
                tok_out.at[slot, sender],
                t_send.at[d - 1, slot],
                t_recv.at[d - 1, slot],
                (target, ex),
            )

        for d in far_first(ndp):
            target = off(dp, d, ndp)
            for slot in range(grid.slots):

                @pl.when(grid.holds(target, slot))
                def _():
                    token_copy(d, slot, grid.first_series(target) + slot, dp, target).start()

        rows = RowGather(grid)
        rows.bind(cot_in, cot_out, more_refs[:4])
        rows.start()
        e_sends = []
        for d in range(1, nex):
            target = off(ex, d, nex)
            copy = remote(
                rank_in.at[target], rank_out.at[nex - 1 - d], e_send.at[d - 1], e_recv.at[d - 1],
                (dp, target),
            )
            copy.start()
            e_sends.append(copy)
        copy = pltpu.make_async_copy(rank_in.at[ex], rank_out.at[nex - 1], loc.at[0])
        copy.start()
        e_sends.append(copy)

        for slot in range(grid.slots):

            @pl.when(grid.holds(dp, slot))
            def _():
                copy = pltpu.make_async_copy(
                    tok.at[grid.first_series(dp) + slot], tok_out.at[slot, dp], loc.at[1 + slot]
                )
                copy.start()
                copy.wait()

        dense.pass_z()
        rows.pass_on(0)
        dense.pass_y()
        for part in range(1, rows.parts):
            rows.pass_on(part)
        dense.pass_x()
        dense.finish()
        rows.finish()
        for d in range(1, ndp):
            for slot in range(grid.slots):

                @pl.when(grid.holds(dp, slot))
                def _():
                    token_copy(d, slot, 0, dp, off(dp, d, ndp)).wait_recv()

                @pl.when(grid.holds(off(dp, d, ndp), slot))
                def _():
                    token_copy(d, slot, 0, dp, off(dp, d, ndp)).wait_send()

        for copy in e_sends:
            copy.wait()

    seg, width = tokens.shape[1:]
    dma = pltpu.SemaphoreType.DMA
    return pl.pallas_call(
        kernel,
        out_shape=(
            jax.ShapeDtypeStruct((grid.slots, ndp, seg, width), tokens.dtype),
            jax.ShapeDtypeStruct((grid.ndev,) + shard.shape, shard.dtype),
            jax.ShapeDtypeStruct((nex,) + cot.shape, cot.dtype),
            jax.ShapeDtypeStruct(ranks.shape, ranks.dtype),
        ),
        in_specs=[any_spec()] * 4,
        out_specs=(any_spec(),) * 4,
        scratch_shapes=[
            dma((ndp - 1, grid.slots)),
            dma((ndp - 1, grid.slots)),
            dma((nex - 1,)),
            dma((nex - 1,)),
            dma((1 + grid.slots,)),
        ]
        + RowGather(grid).scratch()
        + DenseGather(grid).scratch(),
        compiler_params=comm_params(0),
        name="first_exchange",
    )(tokens, shard, cot, ranks)


def heads_in(grid, values, act, attn, grad_attn, grad_misc):
    ndp = grid.ndp

    def kernel(src, act_ref, attn_ref, ga_ref, gm_ref, dst, out_ref, send, recv, loc):
        dp, ex = lax.axis_index("dp"), lax.axis_index("expert")
        greet([(lax.rem(dp + d, ndp), ex) for d in range(1, ndp)])
        lanes = pl.ds(pl.multiple_of(dp * SEG, SEG), SEG)
        copies = []
        for d in far_first(ndp):
            target = lax.rem(dp + d, ndp)
            copy = remote(
                src.at[target], dst.at[:, :, lanes], send.at[d - 1], recv.at[d - 1], (target, ex)
            )
            copy.start()
            copies.append(copy)
        mine = pltpu.make_async_copy(src.at[dp], dst.at[:, :, lanes], loc)
        mine.start()
        out_ref[:, :D] = dot(attn_ref[...], ga_ref[...]).astype(BF16)
        out_ref[:, D:] = dot(act_ref[...], gm_ref[...]).astype(BF16)
        mine.wait()
        for copy in copies:
            copy.wait()

    dma = pltpu.SemaphoreType.DMA
    vmem = pl.BlockSpec(memory_space=pltpu.VMEM)
    return pl.pallas_call(
        kernel,
        out_shape=(
            jax.ShapeDtypeStruct(values.shape[1:3] + (SEG * ndp,), values.dtype),
            jax.ShapeDtypeStruct((D, D + MISC), BF16),
        ),
        in_specs=[any_spec()] + [vmem] * 4,
        out_specs=(any_spec(), vmem),
        scratch_shapes=[dma((ndp - 1,)), dma((ndp - 1,)), dma],
        compiler_params=pltpu.CompilerParams(
            collective_id=2, has_side_effects=True, vmem_limit_bytes=40 * MIB
        ),
        name="heads_in",
    )(values, act, attn, grad_attn, grad_misc)


class RowScatter:
    def __init__(self, grid, width):
        self.grid, self.width = grid, width
        self.rows = D // grid.nex
        self.rows_dev = D // grid.ndev

    def scratch_x(self):
        g = self.grid
        dma = pltpu.SemaphoreType.DMA
        blocks = pltpu.VMEM((g.nx, self.rows, self.width), BF16)
        return [blocks, blocks, blocks, dma((2, 2)), dma((g.nx, 2))]

    def scratch_dp(self):
        g = self.grid
        return [
            pltpu.VMEM((g.ndp, ROW_PAD, self.width), BF16),
            pltpu.SemaphoreType.DMA((g.ndp, 2)),
        ]

    def spread_shape(self):
        return (self.grid.ndp * ROW_PAD, self.width)

    def bind(self, spread):
        g = self.grid
        self.spread = spread
        self.dp, self.ex = lax.axis_index("dp"), lax.axis_index("expert")
        self.x, self.c = self.ex // g.nc, lax.rem(self.ex, g.nc)

    def bind_x(self, source, refs):
        self.source = source
        self.got_core, self.by_x, self.got_x, self.sem_core, self.sem_x = refs

    def bind_dp(self, refs):
        self.got_dp, self.sem_dp = refs

    def core_copy(self):
        other = 1 - self.c
        return remote(
            self.source.at[:, other], self.got_core, self.sem_core.at[0, 0],
            self.sem_core.at[0, 1], (self.dp, self.x * 2 + other),
        )

    def x_copy(self, d):
        target = lax.rem(self.x + d, self.grid.nx)
        return remote(
            self.by_x.at[target], self.got_x.at[d], self.sem_x.at[d, 0], self.sem_x.at[d, 1],
            (self.dp, target * self.grid.nc + self.c),
        )

    def dp_copy(self, d):
        target = lax.rem(self.dp + d, self.grid.ndp)
        rows = pl.ds(pl.multiple_of(target * ROW_PAD, ROW_PAD), ROW_PAD)
        return remote(
            self.spread.at[rows], self.got_dp.at[d], self.sem_dp.at[d, 0], self.sem_dp.at[d, 1],
            (target, self.ex),
        )

    def start(self):
        self.core_copy().start()

    def along_x(self):
        g = self.grid
        self.core_copy().wait()
        for n in range(g.nx):
            mine = self.source[n, pl.ds(self.c, 1)][0]
            self.by_x[n] = (mine.astype(F32) + self.got_core[n].astype(F32)).astype(BF16)
        for d in range(1, g.nx):
            self.x_copy(d).start()

    def after_x(self):
        g = self.grid
        for d in range(1, g.nx):
            self.x_copy(d).wait()
        total = self.by_x[pl.ds(self.x, 1)][0].astype(F32)
        for d in range(1, g.nx):
            total += self.got_x[d].astype(F32)
        to = lax.broadcasted_iota(jnp.int32, (g.ndp * ROW_PAD, self.rows), 0)
        of = lax.broadcasted_iota(jnp.int32, (g.ndp * ROW_PAD, self.rows), 1)
        place = (of // self.rows_dev) * ROW_PAD + lax.rem(of, self.rows_dev)
        move = (to == place).astype(F32).astype(BF16)
        self.spread[...] = dot(move, total.astype(BF16)).astype(BF16)

    def along_dp(self):
        for d in far_first(self.grid.ndp):
            self.dp_copy(d).start()

    def finish(self, out):
        g = self.grid
        rows = pl.ds(pl.multiple_of(self.dp * ROW_PAD, ROW_PAD), ROW_PAD)
        total = self.spread[rows].astype(F32)
        for d in range(1, g.ndp):
            self.dp_copy(d).wait()
            total += self.got_dp[d].astype(F32)
        out[...] = total


class ShardScatter:
    def __init__(self, grid, rows, width):
        self.grid, self.rows, self.width = grid, rows, width

    def scratch(self):
        g = self.grid
        block = (self.rows, self.width)
        dma = pltpu.SemaphoreType.DMA
        return [
            pltpu.VMEM((g.nz,) + block, BF16),
            pltpu.VMEM((max(g.ny - 1, 1), g.nz) + block, BF16),
            pltpu.VMEM((max(g.nz - 1, 1),) + block, BF16),
            dma((g.ny, g.nz, 2)),
            dma((g.nz, 2)),
            dma((g.nz,)),
        ]

    def bind(self, source, refs):
        self.source = source
        self.mine, self.got_y, self.got_z, self.sem_y, self.sem_z, self.loc = refs
        g = self.grid
        self.dp, self.ex = lax.axis_index("dp"), lax.axis_index("expert")
        self.z, self.y = self.dp // g.ny, lax.rem(self.dp, g.ny)
        self.order = far_first(g.nz) + [0]

    def place(self, dz, dy):
        g = self.grid
        return lax.rem(self.z + dz, g.nz) * g.ny + lax.rem(self.y + dy, g.ny)

    def y_copy(self, dy, dz):
        return remote(
            self.source.at[self.place(dz, dy)], self.got_y.at[dy - 1, dz],
            self.sem_y.at[dy, dz, 0], self.sem_y.at[dy, dz, 1], (self.place(0, dy), self.ex),
        )

    def z_copy(self, dz):
        return remote(
            self.mine.at[dz], self.got_z.at[dz - 1], self.sem_z.at[dz, 0], self.sem_z.at[dz, 1],
            (self.place(dz, 0), self.ex),
        )

    def own(self, dz):
        return pltpu.make_async_copy(
            self.source.at[self.place(dz, 0)], self.mine.at[dz], self.loc.at[dz]
        )

    def start(self):
        for dz in self.order:
            for dy in range(1, self.grid.ny):
                self.y_copy(dy, dz).start()
            self.own(dz).start()

    def along_z(self, which):
        g = self.grid
        for dz in which:
            self.own(dz).wait()
            for dy in range(1, g.ny):
                self.y_copy(dy, dz).wait()
            if g.ny > 1:
                total = self.mine[dz].astype(F32)
                for dy in range(1, g.ny):
                    total += self.got_y[dy - 1, dz].astype(F32)
                self.mine[dz] = total.astype(BF16)
            if dz:
                self.z_copy(dz).start()

    def finish(self, out):
        total = self.mine[0].astype(F32)
        for dz in range(1, self.grid.nz):
            self.z_copy(dz).wait()
            total += self.got_z[dz - 1].astype(F32)
        out[...] = total.astype(BF16)


def gather_shared(grid, rows, gates, shared_gate, grad_out, weights, group):
    nex = grid.nex

    def kernel(src, gate, sg_ref, go_ref, w_ref, group_ref,
               dst, gate_dst, lin_ref, gact_ref, early_ref, g_send, g_recv, loc, *row_refs):
        dp, ex = lax.axis_index("dp"), lax.axis_index("expert")
        greet([(dp, lax.rem(ex + d, nex)) for d in range(1, nex)])
        gather = RowGather(grid)
        gather.bind(src, dst, row_refs)
        gather.start()
        gate_copies = []
        for d in range(1, nex):
            target = lax.rem(ex + d, nex)
            copy = remote(
                gate.at[target], gate_dst.at[nex - 1 - d], g_send.at[d - 1], g_recv.at[d - 1],
                (dp, target),
            )
            copy.start()
            gate_copies.append(copy)
        copy = pltpu.make_async_copy(gate.at[ex], gate_dst.at[nex - 1], loc)
        copy.start()
        gate_copies.append(copy)

        act = src[...]
        grad_lin = (go_ref[...].astype(F32) * sg_ref[...]).astype(BF16)
        act_across = dot(group_ref[...], act, 1, 1).astype(BF16)
        grad_across = dot(group_ref[...], grad_lin, 1, 1).astype(BF16)
        wide = 2 * D
        for n in range(FF // wide):
            gate_w, up_w, down_w = (
                w_ref[:, m * FF + n * wide : m * FF + (n + 1) * wide] for m in range(3)
            )
            gate_lin, up_lin = dot(act, gate_w), dot(act, up_w)
            sig = 0.5 * jnp.tanh(0.5 * gate_lin) + 0.5
            silu = gate_lin * sig
            hidden = (silu * up_lin).astype(BF16)
            grad_hidden = dot(grad_lin, down_w)
            grad_gate = (grad_hidden * up_lin * (sig + silu * (1.0 - sig))).astype(BF16)
            grad_up = (grad_hidden * silu).astype(BF16)
            lin = dot(hidden, down_w, 1, 1)
            gact = dot(grad_gate, gate_w, 1, 1) + dot(grad_up, up_w, 1, 1)
            if n:
                lin_ref[...] += lin
                gact_ref[...] += gact
            else:
                lin_ref[...] = lin
                gact_ref[...] = gact
            if n == 0:
                gather.pass_on(0)
            for m, (left, right) in enumerate(
                ((act_across, grad_gate), (act_across, grad_up), (grad_across, hidden))
            ):
                lanes = slice(m * FF + n * wide, m * FF + (n + 1) * wide)
                early_ref[:, lanes] = dot(left, right).astype(BF16)
            if n == 0:
                gather.pass_on(1)
        for part in range(2, gather.parts):
            gather.pass_on(part)
        gather.finish()
        for copy in gate_copies:
            copy.wait()

    dma = pltpu.SemaphoreType.DMA
    vmem = pl.BlockSpec(memory_space=pltpu.VMEM)
    return pl.pallas_call(
        kernel,
        out_shape=(
            jax.ShapeDtypeStruct((nex,) + rows.shape, rows.dtype),
            jax.ShapeDtypeStruct(gates.shape, gates.dtype),
            jax.ShapeDtypeStruct((TOK_DEV, D), F32),
            jax.ShapeDtypeStruct((TOK_DEV, D), F32),
            jax.ShapeDtypeStruct((D, 3 * FF), BF16),
        ),
        in_specs=[vmem] * 6,
        out_specs=(any_spec(), any_spec(), vmem, vmem, vmem),
        scratch_shapes=[dma((nex - 1,)), dma((nex - 1,)), dma] + RowGather(grid).scratch(),
        compiler_params=pltpu.CompilerParams(
            collective_id=4, has_side_effects=True, vmem_limit_bytes=40 * MIB
        ),
        name="gather_shared",
    )(rows, gates, shared_gate, grad_out, weights, group)


def turn(values, cosine, sine):
    first, second = values[: HEAD_DIM // 2], values[HEAD_DIM // 2 :]
    return jnp.concatenate(
        [first * cosine - second * sine, second * cosine + first * sine], axis=0
    )


def allowed_mask(extent, block, length):
    keys = lax.broadcasted_iota(jnp.int32, (extent, QBLOCK), 0)
    queries = lax.broadcasted_iota(jnp.int32, (extent, QBLOCK), 1) + block * QBLOCK
    return (keys <= queries) & (keys < length)


def attend(grid, lives, tok, weights, gain, cosine, sine, shard):
    units, length, ndp, nex = grid.units, tok.shape[1], grid.ndp, grid.nex
    blocks = length // QBLOCK
    chunk = 1
    ends = sorted(set(range(chunk - 1, units, chunk)) | {units - 1})

    def kernel(live_ref, tok_ref, w_ref, gain_ref, cos_ref, sin_ref, shard_ref,
               heads_ref, dense_ref, act_ref, q_ref, k_ref, v_ref, lse_ref,
               buf, h_send, h_recv, h_loc, *dense_refs):
        i = pl.program_id(0)
        dp, ex = lax.axis_index("dp"), lax.axis_index("expert")
        unit = jnp.minimum(dp * units + i, UNITS_ALL - 1)
        head = lax.rem(unit, HEADS)
        slot = jnp.minimum(unit // HEADS - grid.first_series(dp), grid.slots - 1)
        slot = jnp.maximum(slot, 0)
        dense = DenseGather(grid)
        dense.bind(shard_ref, dense_ref, dense_refs)

        def heads_copy(d, n):
            begin = ends[n - 1] + 1 if n else 0
            count = ends[n] + 1 - begin
            target = lax.rem(dp + d, ndp)
            lanes = pl.ds(pl.multiple_of(target * SEG, SEG), SEG)
            return remote(
                buf.at[pl.ds(begin, count), :, lanes],
                heads_ref.at[dp, pl.ds(begin, count)],
                h_send.at[d - 1, n],
                h_recv.at[d - 1, n],
                (target, ex),
            )

        @pl.when(i == 0)
        def _():
            greet(
                [(lax.rem(dp + d, ndp), ex) for d in range(1, ndp)]
                + [(dp, lax.rem(ex + d, nex)) for d in range(1, nex)]
            )
            dense.start()

        @pl.when((i == 0) | (head == 0))
        def _():
            residual = tok_ref[slot].astype(F32)
            scale = lax.rsqrt(jnp.mean(residual * residual, axis=-1, keepdims=True) + eps_norm)
            act_ref[slot] = (residual * scale * gain_ref[...]).astype(BF16)

        cos, sin = cos_ref[...], sin_ref[...]
        w_rows = [
            w_ref[pl.ds(pl.multiple_of(n * D + head * HEAD_DIM, HEAD_DIM), HEAD_DIM)]
            for n in range(3)
        ]
        qkv = dot(jnp.concatenate(w_rows, axis=0), act_ref[slot], 1, 1)
        query = turn(qkv[:HEAD_DIM], cos, sin).astype(BF16)
        key_wide = turn(qkv[HEAD_DIM : 2 * HEAD_DIM], cos, sin)
        value = qkv[2 * HEAD_DIM :].astype(BF16)
        key_rows = key_wide.T.astype(BF16)
        q_ref[0], k_ref[0], v_ref[0] = query, key_wide.astype(BF16), value
        live = live_ref[i]
        for block in range(blocks):
            extent = QBLOCK * (block + 1)
            lanes = slice(QBLOCK * block, extent)
            scores = dot(key_rows[:extent], query[:, lanes]) * HEAD_DIM ** (-0.5)
            scores = jnp.where(allowed_mask(extent, block, live), scores, neg_fill)
            top = jnp.max(scores, axis=0, keepdims=True)
            probs = jnp.exp(scores - top)
            total = jnp.sum(probs, axis=0, keepdims=True)
            result = dot(value[:, :extent], probs.astype(BF16))
            buf[i, :, lanes] = (result * (1.0 / total)).astype(BF16)
            lse_ref[0, :, lanes] = top + jnp.log(total)

        for n, end in enumerate(ends):

            @pl.when(i == end)
            def _():
                for d in far_first(ndp):
                    heads_copy(d, n).start()

        pl.when(i == min(3, units - 1))(dense.pass_z)
        pl.when(i == min(5, units - 1))(dense.pass_y)

        @pl.when(i == units - 1)
        def _():
            mine = pltpu.make_async_copy(
                buf.at[:, :, pl.ds(pl.multiple_of(dp * SEG, SEG), SEG)], heads_ref.at[dp], h_loc
            )
            mine.start()
            dense.pass_x()
            dense.finish()
            for n in range(len(ends)):
                for d in range(1, ndp):
                    heads_copy(d, n).wait()
            mine.wait()

    def whole(array):
        return pl.BlockSpec(
            array.shape, lambda i: (0,) * array.ndim, pipeline_mode=pl.Buffered(1)
        )

    def per_unit(*tail):
        return pl.BlockSpec((1,) + tail, lambda i: (i, 0, 0))

    feature = jax.ShapeDtypeStruct((units, HEAD_DIM, length), BF16)
    inputs = (tok, weights, gain, cosine, sine)
    dma = pltpu.SemaphoreType.DMA
    return pl.pallas_call(
        kernel,
        grid=(units,),
        out_shape=(
            jax.ShapeDtypeStruct((ndp, units, HEAD_DIM, SEG), BF16),
            jax.ShapeDtypeStruct((grid.ndev,) + shard.shape, BF16),
            jax.ShapeDtypeStruct((grid.slots, length, D), BF16),
            feature,
            feature,
            feature,
            jax.ShapeDtypeStruct((units, 1, length), F32),
        ),
        in_specs=[pl.BlockSpec(memory_space=pltpu.SMEM)]
        + [whole(v) for v in inputs]
        + [any_spec()],
        out_specs=(
            any_spec(),
            any_spec(),
            pl.BlockSpec((grid.slots, length, D), lambda i: (0, 0, 0)),
            per_unit(HEAD_DIM, length),
            per_unit(HEAD_DIM, length),
            per_unit(HEAD_DIM, length),
            per_unit(1, length),
        ),
        scratch_shapes=[
            pltpu.VMEM((units, HEAD_DIM, length), BF16),
            dma((ndp - 1, len(ends))),
            dma((ndp - 1, len(ends))),
            dma,
        ]
        + DenseGather(grid).scratch(),
        compiler_params=pltpu.CompilerParams(
            collective_id=1, has_side_effects=True, vmem_limit_bytes=40 * MIB
        ),
        cost_estimate=pl.CostEstimate(
            flops=units * length * length * HEAD_DIM * 2 * 8,
            bytes_accessed=8 * MIB,
            transcendentals=units * length * length,
        ),
        name="attend",
    )(lives, *inputs, shard)


def attend_back(grid, lives, tok, act, weights, query, key, value, lse, grad_heads, cosine, sine,
                group, early, routed):
    units, length, ndp, nex = grid.units, act.shape[1], grid.ndp, grid.nex
    blocks = length // QBLOCK
    scale = HEAD_DIM ** (-0.5)
    early_width, late_width = early.shape[1], 3 * D + MISC
    early_sum, late_sum = RowScatter(grid, early_width), RowScatter(grid, late_width)
    early = early.reshape(grid.nx, grid.nc, early_sum.rows, early_width)
    steps = [min(n, units - 1) for n in (0, 3)]

    def kernel(*refs):
        (live_ref, tok_ref, act_ref, w_ref, q_ref, k_ref, v_ref, lse_ref, do_ref, cos_ref, sin_ref,
         group_ref, early_ref, routed_ref, rows_out, early_out, late_out, routed_out,
         acc, back, dq, dk, dv, grads, gain, late_ref, b_send, b_recv, b_loc,
         early_spread, late_spread, r_send, r_recv) = refs[:33]
        at = 33
        for work, source, spread in (
            (early_sum, early_ref, early_spread),
            (late_sum, late_ref, late_spread),
        ):
            work.bind(spread)
            work.bind_x(source, refs[at : at + 5])
            work.bind_dp(refs[at + 5 : at + 7])
            at += 7

        def routed_copy(step):
            return remote(
                routed_ref.at[step], routed_out.at[step], r_send.at[step], r_recv.at[step],
                (dp, lax.rem(ex + 1 + step, nex)),
            )

        i = pl.program_id(0)
        dp, ex = lax.axis_index("dp"), lax.axis_index("expert")
        unit = dp * units + i
        working = unit < UNITS_ALL
        series, head = unit // HEADS, lax.rem(unit, HEADS)
        slot = jnp.minimum(series - grid.first_series(dp), grid.slots - 1)

        def back_copy(d, which):
            target = lax.rem(dp + d, ndp)
            return remote(
                back.at[which, pl.ds(pl.multiple_of(target * SEG, SEG), SEG)],
                rows_out.at[dp, which],
                b_send.at[d - 1, which],
                b_recv.at[d - 1, which],
                (target, ex),
            )

        def back_local(which):
            return pltpu.make_async_copy(
                back.at[which, pl.ds(pl.multiple_of(dp * SEG, SEG), SEG)],
                rows_out.at[dp, which],
                b_loc.at[which],
            )

        @pl.when(i == 0)
        def _():
            greet(
                [(lax.rem(dp + d, ndp), ex) for d in range(1, ndp)]
                + [(dp, lax.rem(ex + d, nex)) for d in range(1, nex)]
            )
            early_sum.start()
            grads[...] = jnp.zeros_like(grads)
            gain[...] = jnp.zeros_like(gain)

        @pl.when((i == 0) | (head == 0))
        def _():
            acc[...] = jnp.zeros_like(acc)

        @pl.when(working)
        def _():
            live = live_ref[i]
            query, key, value, grad = q_ref[i], k_ref[i], v_ref[i], do_ref[i]
            key_rows = key.astype(F32).T.astype(BF16)
            value_rows = value.astype(F32).T.astype(BF16)
            dk[...] = jnp.zeros_like(dk)
            dv[...] = jnp.zeros_like(dv)
            for block in range(blocks):
                extent = QBLOCK * (block + 1)
                lanes = slice(QBLOCK * block, extent)
                scores = dot(key_rows[:extent], query[:, lanes]) * scale
                scores = jnp.where(allowed_mask(extent, block, live), scores, neg_fill)
                probs = jnp.exp(scores - lse_ref[i, :, lanes])
                grad_probs = dot(value_rows[:extent], grad[:, lanes])
                delta = jnp.sum(probs * grad_probs, axis=0, keepdims=True)
                grad_scores = (probs * (grad_probs - delta)).astype(BF16)
                probs_low = probs.astype(BF16)
                dq[:, lanes] = dot(key[:, :extent], grad_scores)
                dk[:, :extent] += dot(query[:, lanes], grad_scores, 1, 1)
                dv[:, :extent] += dot(grad[:, lanes], probs_low, 1, 1)
            cos, sin = cos_ref[...], -sin_ref[...]
            stacked = jnp.concatenate(
                [
                    turn(dq[...] * scale, cos, sin),
                    turn(dk[...] * scale, cos, sin),
                    dv[...],
                ],
                axis=0,
            ).astype(BF16)
            weight_grads = dot(stacked, act_ref[slot]).astype(BF16)
            w_rows = []
            for n in range(3):
                at = pl.multiple_of(n * D + head * HEAD_DIM, HEAD_DIM)
                part = slice(n * HEAD_DIM, (n + 1) * HEAD_DIM)
                grads[pl.ds(at, HEAD_DIM)] = weight_grads[part]
                w_rows.append(w_ref[pl.ds(at, HEAD_DIM)])
            acc[...] += dot(stacked, jnp.concatenate(w_rows, axis=0), 0, 0)

        @pl.when(working & ((head == HEADS - 1) | (i == units - 1)))
        def _():
            share = acc[...]
            residual = tok_ref[slot].astype(F32)
            normed = residual * lax.rsqrt(
                jnp.mean(residual * residual, axis=-1, keepdims=True) + eps_norm
            )
            gain[...] += jnp.sum(share * normed, axis=0, keepdims=True)
            back[slot] = share.astype(BF16)
            for d in far_first(ndp):
                back_copy(d, slot).start()
            back_local(slot).start()

        @pl.when(i == steps[0])
        def _():
            early_sum.along_x()
            for step in range(nex - 1):
                routed_copy(step).start()

        @pl.when(i == steps[1])
        def _():
            early_sum.after_x()
            early_sum.along_dp()

        @pl.when(i == units - 1)
        def _():
            grads[3 * D :] = jnp.broadcast_to(gain[...], (ROW_PAD, D)).astype(BF16)
            late = dot(group_ref[...], grads[...], 1, 1).astype(BF16)
            late = late.reshape(late_ref.shape[:3] + (late.shape[1],))
            late_ref[:, :, :, : late.shape[3]] = late
            late_ref[:, :, :, late.shape[3] :] = jnp.zeros(
                late_ref.shape[:3] + (late_width - late.shape[3],), BF16
            )
            late_sum.start()
            early_sum.finish(early_out)
            late_sum.along_x()
            late_sum.after_x()
            late_sum.along_dp()
            for which in range(grid.slots):
                for d in range(1, ndp):

                    @pl.when(grid.holds(lax.rem(dp + ndp - d, ndp), which))
                    def _():
                        back_copy(d, which).wait_recv()

                @pl.when(grid.holds(dp, which))
                def _():
                    for d in range(1, ndp):
                        back_copy(d, which).wait_send()
                    back_local(which).wait()

            late_sum.finish(late_out)
            for step in range(nex - 1):
                routed_copy(step).wait()

    def whole(array):
        return pl.BlockSpec(
            array.shape, lambda i: (0,) * array.ndim, pipeline_mode=pl.Buffered(1)
        )

    def whole_out(shape):
        return pl.BlockSpec(shape, lambda i: (0,) * len(shape))

    dma = pltpu.SemaphoreType.DMA
    inputs = (tok, act, weights, query, key, value, lse, grad_heads, cosine, sine, group, early)
    return pl.pallas_call(
        kernel,
        grid=(units,),
        out_shape=(
            jax.ShapeDtypeStruct((ndp, grid.slots, SEG, D), BF16),
            jax.ShapeDtypeStruct((ROW_PAD, early_width), F32),
            jax.ShapeDtypeStruct((ROW_PAD, late_width), F32),
            jax.ShapeDtypeStruct((nex - 1,) + routed.shape[1:], BF16),
        ),
        in_specs=[pl.BlockSpec(memory_space=pltpu.SMEM)] + [whole(v) for v in inputs] + [any_spec()],
        out_specs=(
            any_spec(),
            whole_out((ROW_PAD, early_width)),
            whole_out((ROW_PAD, late_width)),
            any_spec(),
        ),
        scratch_shapes=[
            pltpu.VMEM((length, D), F32),
            pltpu.VMEM((grid.slots, length, D), BF16),
            pltpu.VMEM((HEAD_DIM, length), F32),
            pltpu.VMEM((HEAD_DIM, length), F32),
            pltpu.VMEM((HEAD_DIM, length), F32),
            pltpu.VMEM((3 * D + ROW_PAD, D), BF16),
            pltpu.VMEM((1, D), F32),
            pltpu.VMEM((grid.nx, grid.nc, late_sum.rows, late_width), BF16),
            dma((ndp - 1, grid.slots)),
            dma((ndp - 1, grid.slots)),
            dma((grid.slots,)),
            pltpu.VMEM(early_sum.spread_shape(), BF16),
            pltpu.VMEM(late_sum.spread_shape(), BF16),
            dma((nex - 1,)),
            dma((nex - 1,)),
        ]
        + early_sum.scratch_x()
        + early_sum.scratch_dp()
        + late_sum.scratch_x()
        + late_sum.scratch_dp(),
        compiler_params=pltpu.CompilerParams(
            collective_id=3, has_side_effects=True, vmem_limit_bytes=56 * MIB
        ),
        cost_estimate=pl.CostEstimate(
            flops=units * length * length * HEAD_DIM * 2 * 20,
            bytes_accessed=12 * MIB,
            transcendentals=units * length * length,
        ),
        name="attend_back",
    )(lives, *inputs, routed)


def experts_step(grid, number, weights, act_all, cot_all, ranks, gates, before, early, done=None):
    nex, nc, ndp = grid.nex, grid.nc, grid.ndp
    rows = act_all.shape[1]
    local = EXPERTS // nex
    parts, wide = FF // D, 2 * D
    first, last = number == 0, number == local - 1
    batch = math.gcd(nex, 4)
    flushes = nex // batch
    scatter = RowScatter(grid, 3 * FF) if first or last else None
    talks = first or last
    settle = None if done is None else ShardScatter(grid, *done.shape[1:])
    if first:
        early = early.reshape(grid.nx, nc, scatter.rows, 3 * FF)

    def kernel(*refs):
        refs = list(refs)

        def take(count):
            taken = refs[:count]
            del refs[:count]
            return taken

        w_ref, act_ref, cot_ref, rank_ref, gate_ref = take(5)
        prev = take(3) if before is not None else None
        early_ref = take(1)[0] if talks else None
        done_ref = take(1)[0] if settle is not None else None
        if last:
            gin_out, ggate_out = take(2)
            routed_ref, grad_ref = take(2)
        else:
            gin_ref, ggate_ref = take(2)
            routed_ref, grad_ref = take(2)
        early_out = take(1)[0] if talks else None
        done_out = take(1)[0] if settle is not None else None
        xt_ref, dyt_ref, dg_ref, du_ref, hid_ref, down_ref = take(6)
        acc_ref = take(1)[0] if flushes > 1 else None
        if last:
            gin_buf, ggate_buf, send, recv, loc = take(5)
        if first:
            scatter.bind_x(early_ref, take(len(scatter.scratch_x())))
        if last:
            scatter.bind_dp(take(len(scatter.scratch_dp())))
        if talks:
            spread_ref = early_out if not last else take(1)[0] if first else early_ref
            scatter.bind(spread_ref)
        if settle is not None:
            settle.bind(done_ref, take(len(settle.scratch())))
        s = pl.program_id(0)
        dp, ex = lax.axis_index("dp"), lax.axis_index("expert")

        def copies(step):
            target = lax.rem(ex + 1 + step, nex)
            pairs = (
                (gin_buf.at[step], gin_out.at[step]),
                (ggate_buf.at[step], ggate_out.at[ex]),
            )
            return [
                remote(src, dst, send.at[step, n], recv.at[step, n], (dp, target))
                for n, (src, dst) in enumerate(pairs)
            ]

        if talks:

            @pl.when(s == 0)
            def _():
                peers = [(dp, lax.rem(ex + d, nex)) for d in range(1, nex)]
                if last:
                    peers += [(lax.rem(dp + d, ndp), ex) for d in range(1, ndp)]
                greet(peers)
                if settle is not None:
                    settle.start()
                if first:
                    scatter.start()
                else:
                    scatter.along_dp()

        @pl.when(s == 0)
        def _():
            for part in range(parts):
                lanes = slice(part * D, (part + 1) * D)
                down_ref[lanes] = w_ref[2 * D : 3 * D, lanes]

        rank = rank_ref[0, number : number + 1, :]
        rank_column = jnp.broadcast_to(rank, (8, rows)).T[:, :1]
        slot_down = lax.broadcasted_iota(jnp.int32, (CAP, rows), 0).astype(F32)
        slot_across = lax.broadcasted_iota(jnp.int32, (rows, CAP), 1).astype(F32)
        pick = slot_down == rank
        pick_low = pick.astype(F32).astype(BF16)
        spread = (slot_across == rank_column).astype(F32).astype(BF16)
        picked = dot(pick_low, jnp.concatenate([act_ref[0], cot_ref[0]], axis=1))
        taken_wide, grad_rows = picked[:, :D], picked[:, D:]
        taken = taken_wide.astype(BF16)
        gate_row = gate_ref[0, number : number + 1, :]
        gate = jnp.sum(jnp.where(pick, gate_row, 0.0), axis=1, keepdims=True)
        grad_wide = gate * grad_rows
        grad_result = grad_wide.astype(BF16)
        block = pl.ds(pl.multiple_of(lax.rem(s, batch) * CAP, CAP), CAP)
        xt_ref[:, block] = taken_wide.T.astype(BF16)
        dyt_ref[:, block] = grad_wide.T.astype(BF16)
        result = jnp.zeros((CAP, D), F32)
        grad_taken = jnp.zeros((CAP, D), F32)
        for part in range(0, FF, wide):
            lanes = slice(part, part + wide)
            w_gate = w_ref[0:D, lanes]
            w_up = w_ref[D : 2 * D, lanes]
            w_down = down_ref[lanes]
            gate_lin = dot(taken, w_gate)
            up_lin = dot(taken, w_up)
            sig = 0.5 * jnp.tanh(0.5 * gate_lin) + 0.5
            silu = gate_lin * sig
            hidden = (silu * up_lin).astype(BF16)
            result += dot(hidden, w_down)
            grad_hidden = dot(grad_result, w_down, 1, 1)
            grad_gate = (grad_hidden * up_lin * (sig + silu * (1.0 - sig))).astype(BF16)
            grad_up = (grad_hidden * silu).astype(BF16)
            hid_ref[block, lanes] = hidden
            dg_ref[block, lanes] = grad_gate
            du_ref[block, lanes] = grad_up
            grad_taken += dot(grad_gate, w_gate, 1, 1) + dot(grad_up, w_up, 1, 1)
        result = result.astype(BF16).astype(F32)
        grad_gate_slot = jnp.sum(grad_rows * result, axis=1, keepdims=True)
        grad_gate_row = jnp.sum(jnp.where(pick, grad_gate_slot, 0.0), axis=0, keepdims=True)
        both = jnp.concatenate([gate * result, grad_taken], axis=1).astype(BF16)
        both = dot(spread, both)
        routed, grad_in = both[:, :D], both[:, D:]
        if prev is not None:
            grad_in += prev[0][0]
            routed += prev[2][0]
        if last:
            routed_ref[0] = routed.astype(BF16)
            gin_buf[s] = grad_in.astype(BF16)
            if prev is not None:
                ggate_buf[s, 0:number] = prev[1][0]
            ggate_buf[s, number : number + 1] = grad_gate_row

            @pl.when(s < nex - 1)
            def _():
                for copy in copies(s):
                    copy.start()
        else:
            routed_ref[0] = routed
            gin_ref[0] = grad_in
            if prev is not None:
                ggate_ref[0, 0:number] = prev[1][0]
            ggate_ref[0, number : number + 1] = grad_gate_row

        if first:

            @pl.when(s == 0)
            def _():
                scatter.along_x()

            @pl.when(s == min(2, nex - 1))
            def _():
                scatter.after_x()
                if last:
                    scatter.along_dp()

        if settle is not None:
            for n, which in enumerate(settle.order):

                @pl.when(s == min(n, nex - 2))
                def _():
                    settle.along_z([which])

        own = []
        if last:
            own = [
                pltpu.make_async_copy(src, dst, loc.at[n])
                for n, (src, dst) in enumerate(
                    (
                        (gin_buf.at[nex - 1], gin_out.at[nex - 1]),
                        (ggate_buf.at[nex - 1], ggate_out.at[ex]),
                    )
                )
            ]

        @pl.when(s == nex - 1)
        def _():
            for copy in own:
                copy.start()

        def weight_grads(flush):
            def put(at, lanes, value):
                if flush:
                    value += acc_ref[at : at + D, lanes]
                if flush < flushes - 1:
                    acc_ref[at : at + D, lanes] = value
                else:
                    grad_ref[at : at + D, lanes] = value.astype(BF16)

            def columns(part, carry):
                begin = pl.multiple_of(part * wide, wide)
                lanes = pl.ds(begin, wide)
                put(0, lanes, dot(xt_ref[...], dg_ref[:, lanes]))
                put(D, lanes, dot(xt_ref[...], du_ref[:, lanes]))
                down = dot(dyt_ref[...], hid_ref[:, lanes])
                for n in range(0, wide, D):
                    put(2 * D, pl.ds(begin + n, D), down[:, n : n + D].T)
                return carry

            lax.fori_loop(0, FF // wide, columns, 0)

        for flush in range(flushes):
            pl.when(s == (flush + 1) * batch - 1)(functools.partial(weight_grads, flush))

        @pl.when(s == nex - 1)
        def _():
            if settle is not None:
                settle.finish(done_out)
            if last:
                scatter.finish(early_out)
                for step in range(nex - 1):
                    for copy in copies(step):
                        copy.wait()
                for copy in own:
                    copy.wait()

    def per_source(*tail):
        return pl.BlockSpec((1,) + tail, lambda s: (s,) + (0,) * len(tail))

    def whole(shape):
        return pl.BlockSpec(shape, lambda s: (0,) * len(shape), pipeline_mode=pl.Buffered(1))

    def whole_out(shape):
        return pl.BlockSpec(shape, lambda s: (0,) * len(shape))

    inputs = [weights, act_all, cot_all, ranks, gates]
    in_specs = [
        whole(weights.shape),
        per_source(rows, D),
        per_source(rows, D),
        per_source(local, rows),
        per_source(local, rows),
    ]
    if before is not None:
        inputs += list(before)
        in_specs += [per_source(rows, D), per_source(number, rows), per_source(rows, D)]
    if talks:
        inputs.append(early)
        in_specs.append(whole(early.shape))
    if settle is not None:
        inputs.append(done)
        in_specs.append(any_spec())
    dma = pltpu.SemaphoreType.DMA
    kind = BF16 if last else F32
    out_shape = [
        jax.ShapeDtypeStruct((nex, rows, D), kind),
        jax.ShapeDtypeStruct((nex, number + 1, rows), F32),
        jax.ShapeDtypeStruct((nex, rows, D), kind),
        jax.ShapeDtypeStruct(weights.shape, BF16),
    ]
    if last:
        out_specs = [any_spec()] * 2
    else:
        out_specs = [per_source(rows, D), per_source(number + 1, rows)]
    out_specs += [per_source(rows, D), whole_out(weights.shape)]
    if talks:
        shape = (ROW_PAD, 3 * FF) if last else scatter.spread_shape()
        out_shape.append(jax.ShapeDtypeStruct(shape, F32 if last else BF16))
        out_specs.append(whole_out(shape))
    if settle is not None:
        out_shape.append(jax.ShapeDtypeStruct(done.shape[1:], BF16))
        out_specs.append(whole_out(done.shape[1:]))
    scratch = [
        pltpu.VMEM((D, batch * CAP), BF16),
        pltpu.VMEM((D, batch * CAP), BF16),
        pltpu.VMEM((batch * CAP, FF), BF16),
        pltpu.VMEM((batch * CAP, FF), BF16),
        pltpu.VMEM((batch * CAP, FF), BF16),
        pltpu.VMEM((FF, D), BF16),
    ]
    if flushes > 1:
        scratch.append(pltpu.VMEM(weights.shape, F32))
    if last:
        scratch += [
            pltpu.VMEM((nex, rows, D), BF16),
            pltpu.VMEM((nex, local, rows), F32),
            dma((nex - 1, 2)),
            dma((nex - 1, 2)),
            dma((2,)),
        ]
    if first:
        scratch += scatter.scratch_x()
    if last:
        scratch += scatter.scratch_dp()
    if first and last:
        scratch.append(pltpu.VMEM(scatter.spread_shape(), BF16))
    if settle is not None:
        scratch += settle.scratch()
    return pl.pallas_call(
        kernel,
        grid=(nex,),
        out_shape=tuple(out_shape),
        in_specs=in_specs,
        out_specs=tuple(out_specs),
        scratch_shapes=scratch,
        compiler_params=pltpu.CompilerParams(
            vmem_limit_bytes=60 * MIB,
            collective_id=5 + number if talks else None,
            has_side_effects=talks,
        ),
        cost_estimate=pl.CostEstimate(
            flops=nex * CAP * D * FF * 2 * 11,
            bytes_accessed=25 * MIB,
            transcendentals=nex * CAP * FF,
        ),
        name="experts_step",
    )(*inputs)


def local(
    tokens,
    cotangent,
    lengths,
    routes,
    dense_weights,
    dense_first,
    dense_second,
    dense_average,
    expert_weights,
    expert_first,
    expert_second,
    expert_average,
):
    ndp, nex = lax.axis_size("dp"), lax.axis_size("expert")
    dp, ex = lax.axis_index("dp"), lax.axis_index("expert")
    grid = Grid(ndp, nex)
    local_experts = EXPERTS // nex
    length = SEG * ndp
    rows_dev = D // grid.ndev
    shard_rows = 3 * D // ndp

    spot = jnp.arange(FF, dtype=jnp.int32)
    order = (FF // D) * (spot % D) + spot // D
    mix = (spot[:, None] == order[None, :]).astype(BF16)
    shard_row = dp * shard_rows + jnp.arange(shard_rows, dtype=jnp.int32)
    is_down = (shard_row >= 2 * D)[None, :, None]
    expert_low = expert_weights.astype(BF16).reshape(local_experts, shard_rows, FF)
    mixed_low = jnp.einsum(
        "erf,fg->erg", expert_low, mix, preferred_element_type=F32
    ).astype(BF16)
    expert_send = jnp.where(is_down, expert_low, mixed_low)
    table = dense_weights.astype(BF16).reshape(rows_dev, -1)
    after = 4 * D + EXPERTS

    def padded(*columns):
        return jnp.pad(jnp.concatenate(columns, axis=1), ((0, ROW_PAD - rows_dev), (0, 0)))

    shard_first = padded(
        table[:, : 3 * D],
        table[:, 4 * D : after],
        table[:, after + 3 * FF :],
        jnp.zeros((rows_dev, MISC - EXPERTS - 3), BF16),
        table[:, 3 * D : 4 * D],
    )
    shard_rest = padded(table[:, after : after + 3 * FF])

    names = jnp.arange(EXPERTS, dtype=jnp.int32)
    routes_rows = routes.reshape(TOK_DEV, TOP)
    member = (routes_rows[:, :, None] == names[None, None, :]).any(axis=1)
    before = jnp.arange(TOK_DEV)
    earlier = (before[None, :] < before[:, None]).astype(BF16)
    count = jnp.dot(earlier, member.astype(BF16), preferred_element_type=F32)
    ranks = jnp.where(member, count, -1.0).T.reshape(nex, local_experts, TOK_DEV)

    local_pos = dp * SEG + jnp.arange(SEG, dtype=jnp.int32)
    live = (local_pos[None, :] < lengths[:, None]).astype(F32)
    grad_out_low = (cotangent.astype(F32) * live[..., None]).astype(BF16).reshape(TOK_DEV, D)

    tok_all, dense_all, cot_all, rank_all = first_exchange(
        grid, tokens, shard_first, grad_out_low, ranks
    )
    tok_all, expert_send = lax.optimization_barrier((tok_all, expert_send))
    expert_all = [
        lax.all_gather(expert_send[e], "dp", axis=0, tiled=True) for e in range(local_experts)
    ]
    tok_all = tok_all.reshape(grid.slots, length, D)

    dense_all = dense_all.reshape(grid.ndev * ROW_PAD, -1)
    row = jnp.arange(D, dtype=jnp.int32)
    row_from = (row // rows_dev) * ROW_PAD + row % rows_dev
    unpad = (row_from[:, None] == jnp.arange(grid.ndev * ROW_PAD)[None, :]).astype(BF16)
    qkv_rows = dot(dense_all[:, : 3 * D], unpad, 0, 1).astype(BF16)
    w_misc = dot(unpad, dense_all[:, 3 * D :]).astype(BF16)
    w_misc, w_output = w_misc[:, :MISC], w_misc[:, MISC:]
    gain_first = w_misc[:, EXPERTS + 1].astype(F32)
    gain_second = w_misc[:, EXPERTS + 2].astype(F32)

    unit = jnp.minimum(dp * grid.units + jnp.arange(grid.units, dtype=jnp.int32), UNITS_ALL - 1)
    lives = lengths[unit // HEADS]
    half = HEAD_DIM // 2
    inverse = rope_base ** (-jnp.arange(half, dtype=F32) * 2.0 / HEAD_DIM)
    angles = inverse[:, None] * jnp.arange(length, dtype=jnp.int32).astype(F32)[None, :]
    cosine, sine = jnp.cos(angles), jnp.sin(angles)
    heads_here, rest, act_one, query, key, value, lse = attend(
        grid, lives, tok_all, qkv_rows, gain_first[None, :], cosine, sine, shard_rest
    )
    w_shared = dot(unpad, rest.reshape(grid.ndev * ROW_PAD, -1)).astype(BF16)
    heads_here = heads_here.reshape(-1, HEAD_DIM, SEG)[:UNITS_ALL]
    attn_low = heads_here.reshape(SERIES_DEV, D, SEG).transpose(0, 2, 1).reshape(TOK_DEV, D)

    residual = tokens.astype(F32).reshape(TOK_DEV, D)
    mixed_rows = residual + dot(attn_low, w_output)
    scale_two = lax.rsqrt(jnp.mean(mixed_rows * mixed_rows, axis=-1, keepdims=True) + eps_norm)
    normed_two = mixed_rows * scale_two
    act_two = (normed_two * gain_second).astype(BF16)
    misc = dot(act_two, w_misc)
    router_probs = jax.nn.softmax(misc[:, :EXPERTS], axis=-1)
    shared_gate = jax.nn.sigmoid(misc[:, EXPERTS : EXPERTS + 1])

    row_dev = row // rows_dev
    row_to = ((row_dev % nex) * ndp + row_dev // nex) * rows_dev + row % rows_dev
    group = (row[:, None] == row_to[None, :]).astype(BF16)
    act_all, gates_all, shared_lin, grad_act_shared, early = gather_shared(
        grid,
        act_two,
        router_probs.T.reshape(nex, local_experts, TOK_DEV),
        shared_gate,
        grad_out_low,
        w_shared,
        group,
    )
    before, terms, expert_sums = None, None, []
    for e in range(local_experts):
        results = experts_step(
            grid, e, expert_all[e], act_all, cot_all, rank_all, gates_all, before, early, terms
        )
        before, terms, early = results[:3], results[3], results[4]
        expert_sums += results[5:]
        if e + 1 < local_experts:
            terms = terms.reshape(ndp, shard_rows, FF)
    expert_sums.append(lax.psum_scatter(terms, "dp", scatter_dimension=0, tiled=True))
    gin_back, ggate_back, routed_parts = before

    grad_out = grad_out_low.astype(F32)
    grad_svec_logit = (
        shared_gate * (1.0 - shared_gate) * jnp.sum(grad_out * shared_lin, axis=-1, keepdims=True)
    ).astype(BF16)
    grad_router_probs = ggate_back.reshape(EXPERTS, TOK_DEV).T
    grad_logits = (
        router_probs
        * (grad_router_probs - jnp.sum(router_probs * grad_router_probs, axis=-1, keepdims=True))
    ).astype(BF16)
    grad_misc = jnp.concatenate(
        [grad_logits, grad_svec_logit, jnp.zeros((TOK_DEV, MISC - EXPERTS - 1), BF16)], axis=1
    )
    grad_act_two = (
        jnp.sum(gin_back.astype(F32), axis=0)
        + grad_act_shared
        + dot(grad_misc, w_misc, 1, 1)
    )
    grad_gain_two = jnp.sum(grad_act_two * normed_two, axis=0)
    weighted_two = grad_act_two * gain_second
    grad_mixed = grad_out + scale_two * (
        weighted_two - normed_two * jnp.mean(weighted_two * normed_two, axis=-1, keepdims=True)
    )
    grad_attn_low = grad_mixed.astype(BF16)
    grad_heads = dot(grad_attn_low, w_output, 1, 1).astype(BF16)
    grad_heads = grad_heads.reshape(SERIES_DEV, SEG, D).transpose(0, 2, 1)
    grad_heads = grad_heads.reshape(UNITS_ALL, HEAD_DIM, SEG)
    grad_heads = jnp.pad(grad_heads, ((0, grid.units * ndp - UNITS_ALL), (0, 0), (0, 0)))
    attn_grouped = jnp.einsum(
        "gf,sfp->gsp", group, heads_here.reshape(SERIES_DEV, D, SEG), preferred_element_type=F32
    )
    grad_heads, middle = heads_in(
        grid,
        grad_heads.reshape(ndp, grid.units, HEAD_DIM, SEG),
        dot(group, act_two, 1, 1).astype(BF16),
        attn_grouped.astype(BF16).reshape(D, TOK_DEV),
        grad_attn_low,
        grad_misc,
    )
    gain_two_grouped = dot(group, grad_gain_two.astype(BF16)[:, None]).astype(BF16)
    middle = middle.at[:, D + EXPERTS + 2].set(gain_two_grouped[:, 0])

    back, middle, late, routed_back = attend_back(
        grid, lives, tok_all, act_one, qkv_rows, query, key, value, lse,
        grad_heads, cosine, sine, group, middle, routed_parts,
    )
    routed = jnp.sum(routed_back.astype(F32), axis=0) + routed_parts[nex - 1].astype(F32)
    output = (mixed_rows + routed + shared_gate * shared_lin).astype(BF16)
    grad_act_one = jnp.stack(
        [
            sum(
                back[owner, owned.index(s)].astype(F32)
                for owner, owned in enumerate(grid.owned)
                if s in owned
            )
            for s in range(SERIES_DEV)
        ]
    ).reshape(TOK_DEV, D)
    scale_one = lax.rsqrt(jnp.mean(residual * residual, axis=-1, keepdims=True) + eps_norm)
    normed_one = residual * scale_one
    weighted_one = grad_act_one * gain_first
    grad_tokens = grad_mixed + scale_one * (
        weighted_one - normed_one * jnp.mean(weighted_one * normed_one, axis=-1, keepdims=True)
    )

    early, middle, late = early[:rows_dev], middle[:rows_dev], late[:rows_dev]
    dense_grad = jnp.concatenate(
        [
            late[:, : 3 * D],
            middle[:, : D + EXPERTS],
            early,
            middle[:, D + EXPERTS : D + EXPERTS + 1],
            late[:, 3 * D : 3 * D + 1],
            middle[:, D + EXPERTS + 2 : D + EXPERTS + 3],
        ],
        axis=1,
    ).reshape(-1)

    expert_sums = jnp.stack(expert_sums)
    unmixed = jnp.einsum("erg,fg->erf", expert_sums, mix, preferred_element_type=F32)
    expert_grad = jnp.where(is_down, expert_sums.astype(F32), unmixed)
    expert_grad = expert_grad.reshape(expert_weights.shape)

    dense_first_new, dense_second_new, dense_new, dense_average_new = adamw_update(
        dense_weights, dense_grad, dense_first, dense_second, dense_average
    )
    expert_first_new, expert_second_new, expert_new, expert_average_new = adamw_update(
        expert_weights, expert_grad, expert_first, expert_second, expert_average
    )
    return (
        output.reshape(tokens.shape),
        grad_tokens.reshape(tokens.shape),
        dense_grad,
        dense_first_new,
        dense_second_new,
        dense_new,
        dense_average_new,
        expert_grad,
        expert_first_new,
        expert_second_new,
        expert_new,
        expert_average_new,
    )


def solution(mesh):
    rows = P("expert", "dp", None)
    dense = P(("dp", "expert"))
    experts = P("expert", "dp")
    return jax.shard_map(
        local,
        mesh=mesh,
        in_specs=(
            (rows, rows, P("expert"), P("dp", "expert", None, None)) + (dense,) * 4 + (experts,) * 4
        ),
        out_specs=(rows, rows) + (dense,) * 5 + (experts,) * 5,
        check_vma=False,
    )
```

time: 565 us -> 460 us (0.81)
  matrix products: 66 us -> 22 us
  other arithmetic: 61.8 us -> 32 us
  waiting for transfers between devices: 21.1 us -> 0.77 us
  Pallas kernels: 333 us -> 353 us
  local copies, waits for them, and re-layouts: 50.4 us -> 32.9 us
  starting transfers between devices: 13.1 us -> 0.29 us
    pallas_call x4, Pallas kernels: 143 us -> 202 us  [the longest x2 118 us: experts_step(): pl.pallas_call(kernel, grid=(nex,), out_shape=tuple(out_shape), in_specs=...]
    pallas_call x1, Pallas kernels: 74.2 us -> 45 us  [first_exchange(): pl.pallas_call(kernel, out_shape=(jax.ShapeDtypeStruct((grid.slots, ndp,...]
    concatenate x1 -> x0, other arithmetic: 28.7 us -> none  [local(): jnp.concatenate([grad_e_gate.astype(BF16), grad_e_up.astype(BF16), jnp.co...]
    dot_general x7 -> x1, matrix products: 26.4 us -> 3.41 us  [local(): jnp.einsum('erg,fg->erf', expert_sums, mix, preferred_element_type=F32)]
    all_to_all x3 -> x0, waiting for transfers between devices: 21.1 us -> none  [the longest x1 21.1 us: local(): lax.all_to_all(gin_parts, 'expert', split_axis=0, concat_axis=0, tiled=True)]
    dot_general x15 -> x9, matrix products: 34.3 us -> 15.8 us  [dot(): lax.dot_general(left, right, (((left_dim,), (right_dim,)), ((), ())), pre...]
    pallas_call x1, Pallas kernels: 96.8 us -> 79.1 us  [attend_back(): pl.pallas_call(kernel, grid=(units,), out_shape=(jax.ShapeDtypeStruct((nd...]
    all_to_all x3 -> x0, starting transfers between devices: 12.9 us -> none  [the longest x1 4.51 us: local(): lax.all_to_all(gin_parts, 'expert', split_axis=0, concat_axis=0, tiled=True)]
  transfers between devices with their start and end apart: 5 -> 3, of which waited for: 1 -> 0; matrix products, arithmetic and copies ran while one was open for 15% -> 9% of each run, Pallas kernels for 49% -> 52%
where the time goes in v3:
time: 460 us; the launch traced here: 456 us
  Pallas kernels  353 us (77%)
  local copies, waits for them, and re-layouts  32.9 us (7%)
  other arithmetic  32 us (7%)
  matrix products  22 us (5%)
  between operations  15.1 us (3%)
    pallas_call x2, Pallas kernels, experts_step(): pl.pallas_call(kernel, grid=(nex,), out_shape=tuple(out_shape), in_specs=...  118 us
    pallas_call x1, Pallas kernels, attend_back(): pl.pallas_call(kernel, grid=(units,), out_shape=(jax.ShapeDtypeStruct((nd...  79.1 us
    pallas_call x1, Pallas kernels, attend(): pl.pallas_call(kernel, grid=(units,), out_shape=(jax.ShapeDtypeStruct((nd...  64.6 us
    pallas_call x1, Pallas kernels, first_exchange(): pl.pallas_call(kernel, out_shape=(jax.ShapeDtypeStruct((grid.slots, ndp,...  45 us
    pallas_call x1, Pallas kernels, heads_in(): pl.pallas_call(kernel, out_shape=(jax.ShapeDtypeStruct(values.shape[1:3]...  27 us
    unnamed x135, local copies, waits for them, and re-layouts  19 us
    pallas_call x1, Pallas kernels, gather_shared(): pl.pallas_call(kernel, out_shape=(jax.ShapeDtypeStruct((nex,) + rows.shap...  18.8 us
    dot_general x9, matrix products, dot(): lax.dot_general(left, right, (((left_dim,), (right_dim,)), ((), ())), pre...  15.8 us
  transfers between devices with their start and end apart: 3, of which 0 were waited for; matrix products, arithmetic and copies ran while one was open for 9% of the time, Pallas kernels for 52%

profile of v3, /device:TPU:0, one launch (start us, length us, event | category | flops | bytes accessed | tf_op | source)
XLA Modules:
  0.0 455.8 jit_solution(4455050116396071333)
XLA Ops:
  7.2 1.1 convert_element_type.278
  12.2 1.0 multiply_convert_fusion.1
  13.2 1.9 fusion.19
  15.1 45.0 %first_exchange.1 = (bf16[2,8,128,384]{3,2,1,0:T(8,128)(2,1)}, bf16[32,16,1664]{2,1,0:T(8,128)(2,1)}, bf16[4,768,384]{2,1,0:T(8,128)(2,1)}, f32[4,2,768]{2,1,0:T(2,128)}) custom-call(bf16[6,128,384]{2,1,0:T(8,128)(2,1)} %tok.1, bf16[16,1664]{1,0:T(8,128)(2,1)} %pad.10.shd, bf16[768,384]{1,0:T(8,128)(2,1)} %bitcast.118, f32[4,2,768]{2,1,0:T(2,128)} %reshape.533.rank_in), custom_call_target="tpu_custom_call" | custom-call | tf_op jit(solution)/shard_map/first_exchange/pallas_call | solution.py:384
  60.1 1.0 fusion.96
  62.1 2.2 convolution_convert_fusion.1.w_ref.refs_3_
  64.3 1.8 convolution_convert_fusion.4
  67.6 64.6 %attend.1 = (bf16[8,9,32,128]{3,2,1,0:T(8,128)(2,1)S(1)}, bf16[32,16,4608]{2,1,0:T(8,128)(2,1)S(1)}, bf16[2,1024,384]{2,1,0:T(8,128)(2,1)S(1)}, bf16[9,32,1024]{...) custom-call(s32[9]{0:T(128)S(1)} %gather_fusion, ...), custom_call_target="tpu_custom_call" | custom-call | flops 4831838208 | bytes 8388608 | tf_op jit(solution)/shard_map/attend/pallas_call | solution.py:818
  132.3 2.1 copy-done.15
  134.4 1.1 copy-done.17
  135.5 0.8 copy-done.18
  136.4 0.8 copy-done.19
  137.2 0.8 copy-done.20
  140.5 1.3 fusion.62
  144.5 0.9 fusion.94
  145.4 4.4 convolution_convert_fusion.w_ref
  149.9 18.8 %gather_shared.1 = (bf16[4,768,384]{2,1,0:T(8,128)(2,1)S(1)}, f32[4,2,768]{2,1,0:T(2,128)S(1)}, f32[768,384]{1,0:T(8,128)S(1)}, f32[768,384]{1,0:T(8,128)S(1)}, bf16[384,4608]{1,0:T(8,128)(2,1)S(1)}) custom-call(bf16[768,384]{1,0:T(8,128)(2,1)S(1)} %multiply_convert_fusion.src, f32[4,2,768]{2,1,0:T(2,128)S(1)} %reshape.538.gate, ...), custom_call_target="tpu_custom_call" | custom-call | tf_op jit(solution)/shard_map/gather_shared/pallas_call | solution.py:683
  168.7 1.8 copy-done.10
  170.4 1.4 copy-done.11
  171.8 0.8 compare_reduce_fusion
  173.7 0.8 fusion.43
  175.1 46.8 %experts_step.2 = (f32[4,768,384]{2,1,0:T(8,128)}, f32[4,1,768]{2,1,0:T(1,128)}, f32[4,768,384]{2,1,0:T(8,128)}, bf16[1152,1536]{1,0:T(8,128)(2,1)}, bf16[128,4608]{1,0:T(8,128)(2,1)}) custom-call(bf16[1152,1536]{1,0:T(8,128)(2,1)} %bitcast.142, bf16[4,768,384]{2,1,0:T(8,128)(2,1)} %copy-done.11, bf16[4,768,384]{2,1,0:T(8,128)(2,1)} %get-tuple-element.71.refs_2_, ...), custom_call_target="tpu_custom_call" | custom-call | flops 19931332608 | bytes 26214400 | tf_op jit(solution)/shard_map/experts_step/pallas_call | solution.py:1373
  221.9 71.6 %experts_step.3 = (bf16[4,768,384]{2,1,0:T(8,128)(2,1)}, f32[4,2,768]{2,1,0:T(2,128)}, bf16[4,768,384]{2,1,0:T(8,128)(2,1)}, bf16[1152,1536]{1,0:T(8,128)(2,1)},...) custom-call(bf16[1152,1536]{1,0:T(8,128)(2,1)} %bitcast.141, bf16[4,768,384]{2,1,0:T(8,128)(2,1)} %copy-done.11, ...), custom_call_target="tpu_custom_call" | custom-call | flops 19931332608 | bytes 26214400 | tf_op jit(solution)/shard_map/experts_step/pallas_call | solution.py:1373
  294.2 0.9 copy.60
  295.1 1.4 fusion.47
  296.5 1.4 fusion.49
  297.9 3.1 convert_reduce_fusion
  301.0 0.9 copy-done.44
  302.1 3.3 multiply_reduce_fusion.2
  306.7 1.3 convolution_convert_fusion.3
  308.1 2.1 copy.63
  310.2 1.1 copy-done.1
  311.3 0.9 copy-done.3
  312.2 27.0 %heads_in.1 = (bf16[9,32,1024]{2,1,0:T(8,128)(2,1)S(1)}, bf16[384,512]{1,0:T(8,128)(2,1)S(1)}) custom-call(bf16[8,9,32,128]{3,2,1,0:T(8,128)(2,1)S(1)} %bitcast.120, bf16[384,768]{1,0:T(8,128)(2,1)S(1)} %convolution_convert_fusion.2.act_ref, bf16[384,768]{1,0:T(8,128)(2,1)S(1)} %copy.65.attn_ref, bf16[768,384]{1,0:T(8,128)(2,1)S(1)} %fusion.91.ga_ref, ...), custom_call_target="tpu_custom_call" | custom-call | tf_op jit(solution)/shard_map/heads_in/pallas_call | solution.py:433
  339.2 0.8 copy-done.13
  340.8 0.8 reshape_select_fusion
  341.6 1.8 scatter.4
  343.4 79.1 %attend_back.1 = (bf16[8,2,128,384]{3,2,1,0:T(8,128)(2,1)}, f32[16,512]{1,0:T(8,128)}, f32[16,1280]{1,0:T(8,128)}, bf16[3,768,384]{2,1,0:T(8,128)(2,1)}) custom-call(s32[9]{0:T(128)} %copy-done.9, bf16[2,1024,384]{2,1,0:T(8,128)(2,1)} %bitcast.124, bf16[2,1024,384]{2,1,0:T(8,128)(2,1)} %copy-done.17, bf16[1152,384]{1,0:T(8,128)(2,1)} %copy-done.16, ...), custom_call_target="tpu_custom_call" | custom-call | flops 12079595520 | bytes 12582912 | tf_op jit(solution)/shard_map/attend_back/pallas_call | solution.py:1034
  422.5 0.9 slice.157
  424.1 0.9 fusion.97
  424.9 1.0 concatenate.13
  426.1 2.0 convert_reduce_fusion.1
  428.4 0.8 copy-done.30
  430.0 3.0 fusion.31
  433.1 1.2 multiply_add_fusion.3
  434.4 3.4 fusion.10
  437.8 1.4 copy.69
  439.8 9.2 %multiply_add_fusion.1 = (f32[2,221184]{1,0:T(2,128)}, f32[2,221184]{1,0:T(2,128)}, f32[2,221184]{1,0:T(2,128)}, f32[2,221184]{1,0:T(2,128)}) fusion(f32[2,221184]{1,0:T(2,128)S(1)} %copy-done.38, f32[2,221184]{1,0:T(2,128)S(1)} %copy-done.35, f32[2,221184]{1,0:T(2,128)S(1)} %bitcast.128, f32[2,221184]{1,0:T(2,128)S(1)} %copy-done.39, ...), kind=kLoop, calls=%fused_computation.21 | loop fusion | flops 7520256 | bytes 15925248 | tf_op jit(solution)/shard_map/add | solution.py:51
  (194 shorter events, 18.2 us)
Async XLA Ops:
  7.2 3.9 copy-start.34
  7.2 167.9 %all-gather.7.cloned.1.call-start = ((), (), s32[]{:S(2)}) async-start(), calls=%async_computation.3 | async-start | bytes 3981312 | tf_op jit(solution)/shard_map/all_gather | solution.py:1458
  8.7 4.5 copy-start.58
  11.8 3.3 copy-start.65
  61.1 160.8 %all-gather.5.cloned.1.call-start = ((), (), s32[]{:S(2)}) async-start(), calls=%async_computation.2 | async-start | bytes 3981312 | tf_op jit(solution)/shard_map/all_gather | solution.py:1458
  61.8 372.5 %reduce-scatter.2.cloned.1.call-start = ((), (), s32[]{:S(2)}) async-start(), calls=%async_computation.1 | async-start | bytes 3981312 | tf_op jit(solution)/shard_map/reduce_scatter | solution.py:1515
  62.1 2.2 copy-start.61
  64.3 3.3 copy-start.16
  64.3 3.3 copy-start.12
  66.1 72.8 %copy-start.36 = (bf16[384,512]{1,0:T(8,128)(2,1)}, bf16[384,512]{1,0:T(8,128)(2,1)S(1)}, u32[]{:S(2)}) copy-start(bf16[384,512]{1,0:T(8,128)(2,1)S(1)} %convolution_convert_fusion.4) | copy-start | bytes 1179652
  67.0 65.2 %copy-start.9 = (s32[9]{0:T(128)}, s32[9]{0:T(128)S(1)}, u32[]{:S(2)}) copy-start(s32[9]{0:T(128)S(1)} %gather_fusion) | copy-start | bytes 112
  67.2 65.0 %copy-start.53 = (f32[384]{0:T(512)}, f32[384]{0:T(512)S(1)}, u32[]{:S(2)}) copy-start(f32[384]{0:T(512)S(1)} %get-tuple-element.97) | copy-start | bytes 4612
  67.6 64.7 %copy-start.6 = (f32[16,1024]{1,0:T(8,128)}, f32[16,1024]{1,0:T(8,128)S(1)}, u32[]{:S(2)}) copy-start(f32[16,1024]{1,0:T(8,128)S(1)} %get-tuple-element.114.sin_ref.refs_10_) | copy-start | bytes 196612
  67.6 64.7 %copy-start.7 = (f32[16,1024]{1,0:T(8,128)}, f32[16,1024]{1,0:T(8,128)S(1)}, u32[]{:S(2)}) copy-start(f32[16,1024]{1,0:T(8,128)S(1)} %get-tuple-element.115.cos_ref.refs_9_) | copy-start | bytes 196612
  132.3 2.1 copy-start.15
  140.3 1.6 copy-start.23
  141.9 2.6 copy-start.26
  142.9 1.5 copy-start.50
  143.5 1.9 copy-start.62
  144.5 5.4 %copy-start.5 = (bf16[384,384]{1,0:T(8,128)(2,1)}, bf16[384,384]{1,0:T(8,128)(2,1)S(1)}, u32[]{:S(2)}) copy-start(bf16[384,384]{1,0:T(8,128)(2,1)S(1)} %fusion.40.group_ref.refs_11_) | copy-start | bytes 884740
  145.4 4.5 copy-start
  149.8 22.8 %copy-start.29 = (bf16[6,128,384]{2,1,0:T(8,128)(2,1)S(1)}, bf16[6,128,384]{2,1,0:T(8,128)(2,1)}, u32[]{:S(2)}) copy-start(bf16[6,128,384]{2,1,0:T(8,128)(2,1)} %tok.1) | copy-start | bytes 1769476
  168.7 1.8 copy-start.10
  170.4 1.4 copy-start.11
  171.8 1.3 copy-start.14
  172.8 1.8 copy-start.51
  221.9 73.3 %copy-start.27 = (f32[768,128]{1,0:T(8,128)S(1)}, f32[768,128]{1,0:T(8,128)}, u32[]{:S(2)}) copy-start(f32[768,128]{1,0:T(8,128)} %copy-done.26) | copy-start | bytes 1179652
  302.1 3.3 copy-start.2
  302.1 3.3 copy-start.24
  305.4 1.3 copy-start.37
  306.7 3.5 copy-start.60
  312.2 27.9 %copy-start.52 = (s32[384]{0:T(512)S(1)}, s32[384]{0:T(512)}, u32[]{:S(2)}) copy-start(s32[384]{0:T(512)} %copy-done.50) | copy-start | bytes 4612
  343.4 81.6 %copy-start.49 = (f32[16,4608]{1,0:T(8,128)S(1)}, f32[16,4608]{1,0:T(8,128)}, u32[]{:S(2)}) copy-start(f32[16,4608]{1,0:T(8,128)} %get-tuple-element.91) | copy-start | bytes 884740
  426.1 7.0 %copy-start.42 = (f32[73860]{0:T(1024)}, f32[73860]{0:T(1024)S(1)}, u32[]{:S(2)}) copy-start(f32[73860]{0:T(1024)S(1)} %reshape.550) | copy-start | bytes 886324
  426.1 2.1 copy-start.43
  428.3 1.4 copy-start.32
  428.3 1.7 copy-start.25
  428.4 1.6 copy-start.55
  428.4 1.6 copy-start.56
  430.0 3.1 copy-start.41
  430.0 3.1 copy-start.46
  430.0 3.1 copy-start.47
  430.0 3.1 copy-start.48
  434.4 4.9 %copy-start.39 = (f32[2,221184]{1,0:T(2,128)S(1)}, f32[2,221184]{1,0:T(2,128)}, u32[]{:S(2)}) copy-start(f32[2,221184]{1,0:T(2,128)} %param.24) | copy-start | bytes 5308420
  434.4 4.9 %copy-start.40 = (f32[2,221184]{1,0:T(2,128)S(1)}, f32[2,221184]{1,0:T(2,128)}, u32[]{:S(2)}) copy-start(f32[2,221184]{1,0:T(2,128)} %param.23) | copy-start | bytes 5308420
  437.8 1.5 copy-start.35
  437.8 2.0 copy-start.38
  439.2 9.8 %copy-start.33 = (f32[1,2,144,1536]{3,1,2,0:T(2,128)}, f32[1,2,144,1536]{3,1,2,0:T(2,128)S(1)}, u32[]{:S(2)}) copy-start(f32[1,2,144,1536]{3,1,2,0:T(2,128)S(1)} %copy.69) | copy-start | bytes 5308420
  (22 other events, 21.6 us)
Sparse Core Ops, SparseCore 0:
  61.2 86.3 all-gather.6
  149.8 63.4 all-gather.4
  301.2 112.3 reduce-scatter.1

commit v4 on v3

--- a/solution.py
+++ b/solution.py
@@ -111,6 +111,23 @@
 
 def comm_params(number):
     return pltpu.CompilerParams(collective_id=number, has_side_effects=True)
+
+
+def unpad_matrix(grid):
+    shape = (D, grid.ndev * ROW_PAD)
+    rows_dev = D // grid.ndev
+    row = lax.broadcasted_iota(jnp.int32, shape, 0)
+    at = (row // rows_dev) * ROW_PAD + lax.rem(row, rows_dev)
+    return (lax.broadcasted_iota(jnp.int32, shape, 1) == at).astype(F32).astype(BF16)
+
+
+def group_matrix(grid):
+    rows_dev = D // grid.ndev
+    row = lax.broadcasted_iota(jnp.int32, (D, D), 1)
+    owner = row // rows_dev
+    at = (lax.rem(owner, grid.nex) * grid.ndp + owner // grid.nex) * rows_dev
+    at = at + lax.rem(row, rows_dev)
+    return (lax.broadcasted_iota(jnp.int32, (D, D), 0) == at).astype(F32).astype(BF16)
 
 
 class DenseGather:
@@ -405,47 +422,6 @@
     )(tokens, shard, cot, ranks)
 
 
-def heads_in(grid, values, act, attn, grad_attn, grad_misc):
-    ndp = grid.ndp
-
-    def kernel(src, act_ref, attn_ref, ga_ref, gm_ref, dst, out_ref, send, recv, loc):
-        dp, ex = lax.axis_index("dp"), lax.axis_index("expert")
-        greet([(lax.rem(dp + d, ndp), ex) for d in range(1, ndp)])
-        lanes = pl.ds(pl.multiple_of(dp * SEG, SEG), SEG)
-        copies = []
-        for d in far_first(ndp):
-            target = lax.rem(dp + d, ndp)
-            copy = remote(
-                src.at[target], dst.at[:, :, lanes], send.at[d - 1], recv.at[d - 1], (target, ex)
-            )
-            copy.start()
-            copies.append(copy)
-        mine = pltpu.make_async_copy(src.at[dp], dst.at[:, :, lanes], loc)
-        mine.start()
-        out_ref[:, :D] = dot(attn_ref[...], ga_ref[...]).astype(BF16)
-        out_ref[:, D:] = dot(act_ref[...], gm_ref[...]).astype(BF16)
-        mine.wait()
-        for copy in copies:
-            copy.wait()
-
-    dma = pltpu.SemaphoreType.DMA
-    vmem = pl.BlockSpec(memory_space=pltpu.VMEM)
-    return pl.pallas_call(
-        kernel,
-        out_shape=(
-            jax.ShapeDtypeStruct(values.shape[1:3] + (SEG * ndp,), values.dtype),
-            jax.ShapeDtypeStruct((D, D + MISC), BF16),
-        ),
-        in_specs=[any_spec()] + [vmem] * 4,
-        out_specs=(any_spec(), vmem),
-        scratch_shapes=[dma((ndp - 1,)), dma((ndp - 1,)), dma],
-        compiler_params=pltpu.CompilerParams(
-            collective_id=2, has_side_effects=True, vmem_limit_bytes=40 * MIB
-        ),
-        name="heads_in",
-    )(values, act, attn, grad_attn, grad_misc)
-
-
 class RowScatter:
     def __init__(self, grid, width):
         self.grid, self.width = grid, width
@@ -546,26 +522,36 @@
     def __init__(self, grid, rows, width):
         self.grid, self.rows, self.width = grid, rows, width
 
-    def scratch(self):
+    def scratch_y(self):
         g = self.grid
         block = (self.rows, self.width)
         dma = pltpu.SemaphoreType.DMA
         return [
             pltpu.VMEM((g.nz,) + block, BF16),
             pltpu.VMEM((max(g.ny - 1, 1), g.nz) + block, BF16),
-            pltpu.VMEM((max(g.nz - 1, 1),) + block, BF16),
             dma((g.ny, g.nz, 2)),
-            dma((g.nz, 2)),
             dma((g.nz,)),
         ]
 
-    def bind(self, source, refs):
+    def scratch_z(self):
+        g = self.grid
+        block = (self.rows, self.width)
+        dma = pltpu.SemaphoreType.DMA
+        return [pltpu.VMEM(block, BF16), pltpu.VMEM((g.nz,) + block, BF16), dma((g.nz, 2)), dma]
+
+    def bind(self, source):
         self.source = source
-        self.mine, self.got_y, self.got_z, self.sem_y, self.sem_z, self.loc = refs
         g = self.grid
         self.dp, self.ex = lax.axis_index("dp"), lax.axis_index("expert")
         self.z, self.y = self.dp // g.ny, lax.rem(self.dp, g.ny)
         self.order = far_first(g.nz) + [0]
+
+    def bind_y(self, out, refs):
+        self.out = out
+        self.mine, self.got_y, self.sem_y, self.loc = refs
+
+    def bind_z(self, refs):
+        self.own, self.got_z, self.sem_z, self.loc = refs
 
     def place(self, dz, dy):
         g = self.grid
@@ -577,27 +563,24 @@
             self.sem_y.at[dy, dz, 0], self.sem_y.at[dy, dz, 1], (self.place(0, dy), self.ex),
         )
 
-    def z_copy(self, dz):
-        return remote(
-            self.mine.at[dz], self.got_z.at[dz - 1], self.sem_z.at[dz, 0], self.sem_z.at[dz, 1],
-            (self.place(dz, 0), self.ex),
-        )
-
-    def own(self, dz):
+    def load(self, dz):
         return pltpu.make_async_copy(
             self.source.at[self.place(dz, 0)], self.mine.at[dz], self.loc.at[dz]
         )
 
-    def start(self):
+    def store(self, dz):
+        return pltpu.make_async_copy(self.mine.at[dz], self.out.at[dz], self.loc.at[dz])
+
+    def start_y(self):
         for dz in self.order:
             for dy in range(1, self.grid.ny):
                 self.y_copy(dy, dz).start()
-            self.own(dz).start()
-
-    def along_z(self, which):
-        g = self.grid
-        for dz in which:
-            self.own(dz).wait()
+            self.load(dz).start()
+
+    def finish_y(self):
+        g = self.grid
+        for dz in self.order:
+            self.load(dz).wait()
             for dy in range(1, g.ny):
                 self.y_copy(dy, dz).wait()
             if g.ny > 1:
@@ -605,48 +588,99 @@
                 for dy in range(1, g.ny):
                     total += self.got_y[dy - 1, dz].astype(F32)
                 self.mine[dz] = total.astype(BF16)
-            if dz:
-                self.z_copy(dz).start()
-
-    def finish(self, out):
-        total = self.mine[0].astype(F32)
+            self.store(dz).start()
+        for dz in self.order:
+            self.store(dz).wait()
+
+    def z_copy(self, dz):
+        return remote(
+            self.source.at[dz], self.got_z.at[dz], self.sem_z.at[dz, 0], self.sem_z.at[dz, 1],
+            (self.place(dz, 0), self.ex),
+        )
+
+    def own_copy(self):
+        return pltpu.make_async_copy(self.source.at[0], self.own, self.loc)
+
+    def start_z(self):
+        for dz in far_first(self.grid.nz):
+            self.z_copy(dz).start()
+        self.own_copy().start()
+
+    def finish_z(self, out):
+        self.own_copy().wait()
+        total = self.own[...].astype(F32)
         for dz in range(1, self.grid.nz):
             self.z_copy(dz).wait()
-            total += self.got_z[dz - 1].astype(F32)
+            total += self.got_z[dz].astype(F32)
         out[...] = total.astype(BF16)
 
 
-def gather_shared(grid, rows, gates, shared_gate, grad_out, weights, group):
+def route_rows(grid, heads, tokens, table, grad_out, weights):
     nex = grid.nex
-
-    def kernel(src, gate, sg_ref, go_ref, w_ref, group_ref,
-               dst, gate_dst, lin_ref, gact_ref, early_ref, g_send, g_recv, loc, *row_refs):
+    local = EXPERTS // nex
+    count = len(OUTS_ROUTE)
+
+    def kernel(heads_ref, tok_ref, table_ref, go_ref, w_ref, dst, gate_dst, *refs):
+        outs, bufs = refs[:count], refs[count : 2 * count]
+        mixed_buf, probs_buf, lin_ref, gact_ref, early_ref, across_ref, small_ref, gain_ref = bufs
+        act_buf, gate_buf, g_send, g_recv, loc, out_sem = refs[2 * count : 2 * count + 6]
+        row_refs = refs[2 * count + 6 :]
         dp, ex = lax.axis_index("dp"), lax.axis_index("expert")
         greet([(dp, lax.rem(ex + d, nex)) for d in range(1, nex)])
+
+        def keep(n):
+            return pltpu.make_async_copy(bufs[n], outs[n], out_sem.at[n])
+
+        unpad, group = unpad_matrix(grid), group_matrix(grid)
+        small_ref[...] = dot(unpad, table_ref[:, 3 * D :]).astype(BF16)
+        gain_ref[...] = dot(table_ref[:, 3 * D : 3 * D + MISC], unpad, 0, 1)[
+            EXPERTS : EXPERTS + 8
+        ]
+        for s in range(SERIES_DEV):
+            attn = heads_ref[s * HEADS : (s + 1) * HEADS].reshape(D, SEG)
+            rows = slice(s * SEG, (s + 1) * SEG)
+            mixed_buf[rows] = tok_ref[s].astype(F32) + dot(attn, small_ref[:, MISC:], 0, 0)
+        mixed = mixed_buf[...]
+        scale = lax.rsqrt(jnp.mean(mixed * mixed, axis=-1, keepdims=True) + eps_norm)
+        act = (mixed * scale * gain_ref[2:3]).astype(BF16)
+        act_buf[...] = act
         gather = RowGather(grid)
-        gather.bind(src, dst, row_refs)
+        gather.bind(act_buf, dst, row_refs)
         gather.start()
+        misc = dot(act, small_ref[:, :MISC])
+        lane = lax.broadcasted_iota(jnp.int32, misc.shape, 1)
+        logits = jnp.where(lane < EXPERTS, misc, neg_fill)
+        powers = jnp.exp(logits - jnp.max(logits, axis=1, keepdims=True))
+        probs = powers / jnp.sum(powers, axis=1, keepdims=True)
+        shared_gate = 0.5 * jnp.tanh(0.5 * misc[:, EXPERTS : EXPERTS + 1]) + 0.5
+        probs_buf[...] = jnp.where(lane == EXPERTS, shared_gate, probs)
+        flipped = probs.T
+        for n in range(nex):
+            gate_buf[n] = flipped[n * local : (n + 1) * local]
         gate_copies = []
         for d in range(1, nex):
             target = lax.rem(ex + d, nex)
             copy = remote(
-                gate.at[target], gate_dst.at[nex - 1 - d], g_send.at[d - 1], g_recv.at[d - 1],
+                gate_buf.at[target], gate_dst.at[nex - 1 - d], g_send.at[d - 1], g_recv.at[d - 1],
                 (dp, target),
             )
             copy.start()
             gate_copies.append(copy)
-        copy = pltpu.make_async_copy(gate.at[ex], gate_dst.at[nex - 1], loc)
+        copy = pltpu.make_async_copy(gate_buf.at[ex], gate_dst.at[nex - 1], loc)
         copy.start()
         gate_copies.append(copy)
-
-        act = src[...]
-        grad_lin = (go_ref[...].astype(F32) * sg_ref[...]).astype(BF16)
-        act_across = dot(group_ref[...], act, 1, 1).astype(BF16)
-        grad_across = dot(group_ref[...], grad_lin, 1, 1).astype(BF16)
+        for n in (0, 1, 6, 7):
+            keep(n).start()
+
+        grad_lin = (go_ref[...].astype(F32) * shared_gate).astype(BF16)
+        across_ref[...] = dot(group, act, 1, 1).astype(BF16)
+        keep(5).start()
+        grad_across = dot(group, grad_lin, 1, 1).astype(BF16)
         wide = 2 * D
         for n in range(FF // wide):
             gate_w, up_w, down_w = (
-                w_ref[:, m * FF + n * wide : m * FF + (n + 1) * wide] for m in range(3)
+                dot(unpad, w_ref[:, m * FF + n * wide : m * FF + (n + 1) * wide]).astype(BF16)
+                for m in range(3)
             )
             gate_lin, up_lin = dot(act, gate_w), dot(act, up_w)
             sig = 0.5 * jnp.tanh(0.5 * gate_lin) + 0.5
@@ -665,38 +699,65 @@
                 gact_ref[...] = gact
             if n == 0:
                 gather.pass_on(0)
+            else:
+                keep(2).start()
+                keep(3).start()
             for m, (left, right) in enumerate(
-                ((act_across, grad_gate), (act_across, grad_up), (grad_across, hidden))
+                ((across_ref[...], grad_gate), (across_ref[...], grad_up), (grad_across, hidden))
             ):
                 lanes = slice(m * FF + n * wide, m * FF + (n + 1) * wide)
                 early_ref[:, lanes] = dot(left, right).astype(BF16)
             if n == 0:
                 gather.pass_on(1)
+        keep(4).start()
         for part in range(2, gather.parts):
             gather.pass_on(part)
         gather.finish()
         for copy in gate_copies:
             copy.wait()
+        for n in range(count):
+            keep(n).wait()
 
     dma = pltpu.SemaphoreType.DMA
     vmem = pl.BlockSpec(memory_space=pltpu.VMEM)
+    hbm = pl.BlockSpec(memory_space=pltpu.HBM)
+    inputs = (heads, tokens, table, grad_out, weights)
     return pl.pallas_call(
         kernel,
         out_shape=(
-            jax.ShapeDtypeStruct((nex,) + rows.shape, rows.dtype),
-            jax.ShapeDtypeStruct(gates.shape, gates.dtype),
-            jax.ShapeDtypeStruct((TOK_DEV, D), F32),
-            jax.ShapeDtypeStruct((TOK_DEV, D), F32),
-            jax.ShapeDtypeStruct((D, 3 * FF), BF16),
+            jax.ShapeDtypeStruct((nex, TOK_DEV, D), BF16),
+            jax.ShapeDtypeStruct((nex, local, TOK_DEV), F32),
+        )
+        + tuple(jax.ShapeDtypeStruct(shape, kind) for shape, kind in OUTS_ROUTE),
+        in_specs=[vmem] * len(inputs),
+        out_specs=(hbm,) * (2 + count),
+        scratch_shapes=[pltpu.VMEM(shape, kind) for shape, kind in OUTS_ROUTE]
+        + [
+            pltpu.VMEM((TOK_DEV, D), BF16),
+            pltpu.VMEM((nex, local, TOK_DEV), F32),
+            dma((nex - 1,)),
+            dma((nex - 1,)),
+            dma,
+            dma((count,)),
+        ]
+        + RowGather(grid).scratch(),
+        compiler_params=pltpu.CompilerParams(
+            collective_id=4, has_side_effects=True, vmem_limit_bytes=60 * MIB
         ),
-        in_specs=[vmem] * 6,
-        out_specs=(any_spec(), any_spec(), vmem, vmem, vmem),
-        scratch_shapes=[dma((nex - 1,)), dma((nex - 1,)), dma] + RowGather(grid).scratch(),
-        compiler_params=pltpu.CompilerParams(
-            collective_id=4, has_side_effects=True, vmem_limit_bytes=40 * MIB
-        ),
-        name="gather_shared",
-    )(rows, gates, shared_gate, grad_out, weights, group)
+        name="route_rows",
+    )(*inputs)
+
+
+OUTS_ROUTE = (
+    ((TOK_DEV, D), F32),
+    ((TOK_DEV, MISC), F32),
+    ((TOK_DEV, D), F32),
+    ((TOK_DEV, D), F32),
+    ((D, 3 * FF), BF16),
+    ((D, TOK_DEV), BF16),
+    ((D, MISC + D), BF16),
+    ((8, D), F32),
+)
 
 
 def turn(values, cosine, sine):
@@ -712,14 +773,15 @@
     return (keys <= queries) & (keys < length)
 
 
-def attend(grid, lives, tok, weights, gain, cosine, sine, shard):
+def attend(grid, lengths, tok, table, cosine, sine, shard):
     units, length, ndp, nex = grid.units, tok.shape[1], grid.ndp, grid.nex
     blocks = length // QBLOCK
     chunk = 1
     ends = sorted(set(range(chunk - 1, units, chunk)) | {units - 1})
 
-    def kernel(live_ref, tok_ref, w_ref, gain_ref, cos_ref, sin_ref, shard_ref,
-               heads_ref, dense_ref, act_ref, q_ref, k_ref, v_ref, lse_ref,
+    def kernel(len_ref, tok_ref, table_ref, cos_ref, sin_ref, shard_ref,
+               heads_ref, dense_ref, act_out, q_out, k_out, v_out, lse_out, w_out,
+               act_ref, q_ref, k_ref, v_ref, lse_ref, w_ref, k_sem,
                buf, h_send, h_recv, h_loc, *dense_refs):
         i = pl.program_id(0)
         dp, ex = lax.axis_index("dp"), lax.axis_index("expert")
@@ -729,6 +791,15 @@
         slot = jnp.maximum(slot, 0)
         dense = DenseGather(grid)
         dense.bind(shard_ref, dense_ref, dense_refs)
+
+        def keep():
+            pairs = (
+                (act_ref, act_out), (q_ref, q_out), (k_ref, k_out), (v_ref, v_out),
+                (lse_ref, lse_out), (w_ref, w_out),
+            )
+            return [
+                pltpu.make_async_copy(src, dst, k_sem.at[n]) for n, (src, dst) in enumerate(pairs)
+            ]
 
         def heads_copy(d, n):
             begin = ends[n - 1] + 1 if n else 0
@@ -750,12 +821,14 @@
                 + [(dp, lax.rem(ex + d, nex)) for d in range(1, nex)]
             )
             dense.start()
+            w_ref[...] = dot(table_ref[:, : 3 * D + MISC], unpad_matrix(grid), 0, 1).astype(BF16)
 
         @pl.when((i == 0) | (head == 0))
         def _():
             residual = tok_ref[slot].astype(F32)
             scale = lax.rsqrt(jnp.mean(residual * residual, axis=-1, keepdims=True) + eps_norm)
-            act_ref[slot] = (residual * scale * gain_ref[...]).astype(BF16)
+            gain = w_ref[3 * D : 3 * D + ROW_PAD].astype(F32)[EXPERTS + 1 : EXPERTS + 2]
+            act_ref[slot] = (residual * scale * gain).astype(BF16)
 
         cos, sin = cos_ref[...], sin_ref[...]
         w_rows = [
@@ -767,8 +840,8 @@
         key_wide = turn(qkv[HEAD_DIM : 2 * HEAD_DIM], cos, sin)
         value = qkv[2 * HEAD_DIM :].astype(BF16)
         key_rows = key_wide.T.astype(BF16)
-        q_ref[0], k_ref[0], v_ref[0] = query, key_wide.astype(BF16), value
-        live = live_ref[i]
+        q_ref[i], k_ref[i], v_ref[i] = query, key_wide.astype(BF16), value
+        live = len_ref[unit // HEADS]
         for block in range(blocks):
             extent = QBLOCK * (block + 1)
             lanes = slice(QBLOCK * block, extent)
@@ -779,7 +852,7 @@
             total = jnp.sum(probs, axis=0, keepdims=True)
             result = dot(value[:, :extent], probs.astype(BF16))
             buf[i, :, lanes] = (result * (1.0 / total)).astype(BF16)
-            lse_ref[0, :, lanes] = top + jnp.log(total)
+            lse_ref[i, :, lanes] = top + jnp.log(total)
 
         for n, end in enumerate(ends):
 
@@ -797,23 +870,24 @@
                 buf.at[:, :, pl.ds(pl.multiple_of(dp * SEG, SEG), SEG)], heads_ref.at[dp], h_loc
             )
             mine.start()
+            for copy in keep():
+                copy.start()
             dense.pass_x()
             dense.finish()
             for n in range(len(ends)):
                 for d in range(1, ndp):
                     heads_copy(d, n).wait()
             mine.wait()
+            for copy in keep():
+                copy.wait()
 
     def whole(array):
         return pl.BlockSpec(
             array.shape, lambda i: (0,) * array.ndim, pipeline_mode=pl.Buffered(1)
         )
 
-    def per_unit(*tail):
-        return pl.BlockSpec((1,) + tail, lambda i: (i, 0, 0))
-
     feature = jax.ShapeDtypeStruct((units, HEAD_DIM, length), BF16)
-    inputs = (tok, weights, gain, cosine, sine)
+    inputs = (tok, table, cosine, sine)
     dma = pltpu.SemaphoreType.DMA
     return pl.pallas_call(
         kernel,
@@ -826,6 +900,7 @@
             feature,
             feature,
             jax.ShapeDtypeStruct((units, 1, length), F32),
+            jax.ShapeDtypeStruct((3 * D + MISC, D), BF16),
         ),
         in_specs=[pl.BlockSpec(memory_space=pltpu.SMEM)]
         + [whole(v) for v in inputs]
@@ -833,13 +908,16 @@
         out_specs=(
             any_spec(),
             any_spec(),
-            pl.BlockSpec((grid.slots, length, D), lambda i: (0, 0, 0)),
-            per_unit(HEAD_DIM, length),
-            per_unit(HEAD_DIM, length),
-            per_unit(HEAD_DIM, length),
-            per_unit(1, length),
-        ),
+        )
+        + (pl.BlockSpec(memory_space=pltpu.HBM),) * 6,
         scratch_shapes=[
+            pltpu.VMEM((grid.slots, length, D), BF16),
+            pltpu.VMEM(feature.shape, BF16),
+            pltpu.VMEM(feature.shape, BF16),
+            pltpu.VMEM(feature.shape, BF16),
+            pltpu.VMEM((units, 1, length), F32),
+            pltpu.VMEM((3 * D + MISC, D), BF16),
+            dma((6,)),
             pltpu.VMEM((units, HEAD_DIM, length), BF16),
             dma((ndp - 1, len(ends))),
             dma((ndp - 1, len(ends))),
@@ -847,7 +925,7 @@
         ]
         + DenseGather(grid).scratch(),
         compiler_params=pltpu.CompilerParams(
-            collective_id=1, has_side_effects=True, vmem_limit_bytes=40 * MIB
+            collective_id=1, has_side_effects=True, vmem_limit_bytes=60 * MIB
         ),
         cost_estimate=pl.CostEstimate(
             flops=units * length * length * HEAD_DIM * 2 * 8,
@@ -855,11 +933,11 @@
             transcendentals=units * length * length,
         ),
         name="attend",
-    )(lives, *inputs, shard)
-
-
-def attend_back(grid, lives, tok, act, weights, query, key, value, lse, grad_heads, cosine, sine,
-                group, early, routed):
+    )(lengths, *inputs, shard)
+
+
+def attend_back(grid, lengths, tok, act, weights, query, key, value, lse, grad_heads, cosine, sine,
+                early, routed, partial, tokens, mixed, grad_mixed, probs, lin, gains, shared):
     units, length, ndp, nex = grid.units, act.shape[1], grid.ndp, grid.nex
     blocks = length // QBLOCK
     scale = HEAD_DIM ** (-0.5)
@@ -867,13 +945,17 @@
     early_sum, late_sum = RowScatter(grid, early_width), RowScatter(grid, late_width)
     early = early.reshape(grid.nx, grid.nc, early_sum.rows, early_width)
     steps = [min(n, units - 1) for n in (0, 3)]
+    settle = ShardScatter(grid, *partial.shape[1:])
 
     def kernel(*refs):
-        (live_ref, tok_ref, act_ref, w_ref, q_ref, k_ref, v_ref, lse_ref, do_ref, cos_ref, sin_ref,
-         group_ref, early_ref, routed_ref, rows_out, early_out, late_out, routed_out,
+        (len_ref, tok_ref, act_ref, w_ref, q_ref, k_ref, v_ref, lse_ref, do_ref, cos_ref, sin_ref,
+         early_ref, tokens_ref, mixed_ref, grad_mixed_ref, probs_ref, lin_ref, gains_ref, shared_ref,
+         routed_ref, partial_ref,
+         output_ref, grad_tokens_ref, table_ref, settle_out,
+         rows_out, early_out, late_out, routed_out,
          acc, back, dq, dk, dv, grads, gain, late_ref, b_send, b_recv, b_loc,
-         early_spread, late_spread, r_send, r_recv) = refs[:33]
-        at = 33
+         early_spread, late_spread, r_send, r_recv) = refs[:44]
+        at = 44
         for work, source, spread in (
             (early_sum, early_ref, early_spread),
             (late_sum, late_ref, late_spread),
@@ -882,6 +964,8 @@
             work.bind_x(source, refs[at : at + 5])
             work.bind_dp(refs[at + 5 : at + 7])
             at += 7
+        settle.bind(partial_ref)
+        settle.bind_z(refs[at:])
 
         def routed_copy(step):
             return remote(
@@ -919,6 +1003,7 @@
                 [(lax.rem(dp + d, ndp), ex) for d in range(1, ndp)]
                 + [(dp, lax.rem(ex + d, nex)) for d in range(1, nex)]
             )
+            settle.start_z()
             early_sum.start()
             grads[...] = jnp.zeros_like(grads)
             gain[...] = jnp.zeros_like(gain)
@@ -929,7 +1014,7 @@
 
         @pl.when(working)
         def _():
-            live = live_ref[i]
+            live = len_ref[series]
             query, key, value, grad = q_ref[i], k_ref[i], v_ref[i], do_ref[i]
             key_rows = key.astype(F32).T.astype(BF16)
             value_rows = value.astype(F32).T.astype(BF16)
@@ -993,7 +1078,7 @@
         @pl.when(i == units - 1)
         def _():
             grads[3 * D :] = jnp.broadcast_to(gain[...], (ROW_PAD, D)).astype(BF16)
-            late = dot(group_ref[...], grads[...], 1, 1).astype(BF16)
+            late = dot(group_matrix(grid), grads[...], 1, 1).astype(BF16)
             late = late.reshape(late_ref.shape[:3] + (late.shape[1],))
             late_ref[:, :, :, : late.shape[3]] = late
             late_ref[:, :, :, late.shape[3] :] = jnp.zeros(
@@ -1002,6 +1087,13 @@
             late_sum.start()
             early_sum.finish(early_out)
             late_sum.along_x()
+            for step in range(nex - 1):
+                routed_copy(step).wait()
+            total = routed_ref[nex - 1].astype(F32)
+            for step in range(nex - 1):
+                total += routed_out[step].astype(F32)
+            shared_gate = probs_ref[:, EXPERTS : EXPERTS + 1]
+            output_ref[...] = (mixed_ref[...] + total + shared_gate * lin_ref[...]).astype(BF16)
             late_sum.after_x()
             late_sum.along_dp()
             for which in range(grid.slots):
@@ -1017,9 +1109,39 @@
                         back_copy(d, which).wait_send()
                     back_local(which).wait()
 
+            for n in range(SERIES_DEV):
+                rows = slice(n * SEG, (n + 1) * SEG)
+                grad_act = sum(
+                    rows_out[owner, owned.index(n)].astype(F32)
+                    for owner, owned in enumerate(grid.owned)
+                    if n in owned
+                )
+                residual = tokens_ref[n].astype(F32)
+                scale_one = lax.rsqrt(
+                    jnp.mean(residual * residual, axis=-1, keepdims=True) + eps_norm
+                )
+                normed = residual * scale_one
+                weighted = grad_act * gains_ref[1:2]
+                inner = jnp.mean(weighted * normed, axis=-1, keepdims=True)
+                grad_tokens_ref[rows] = grad_mixed_ref[rows] + scale_one * (
+                    weighted - normed * inner
+                )
             late_sum.finish(late_out)
-            for step in range(nex - 1):
-                routed_copy(step).wait()
+            late, mid = late_out[...], early_out[...]
+            misc = mid[:, D:]
+            lane = lax.broadcasted_iota(jnp.int32, misc.shape, 1)
+            wide = jnp.concatenate([shared_ref[...], jnp.zeros_like(misc)], axis=1)
+            wide = pltpu.roll(wide, EXPERTS, 1)
+            table_ref[:, : 3 * D] = late[:, : 3 * D]
+            table_ref[:, 3 * D : 4 * D] = mid[:, :D]
+            table_ref[:, 4 * D : 4 * D + MISC] = wide[:, :MISC] + jnp.where(
+                lane < EXPERTS, misc, 0.0
+            )
+            table_ref[:, 4 * D + MISC : 4 * D + 3 * FF] = wide[:, MISC : 3 * FF]
+            ends = jnp.where(lane == EXPERTS + 1, late[:, 3 * D :], misc)
+            ends = jnp.where((lane >= EXPERTS) & (lane < EXPERTS + 3), ends, 0.0)
+            table_ref[:, 4 * D + 3 * FF :] = wide[:, 3 * FF :] + ends
+            settle.finish_z(settle_out)
 
     def whole(array):
         return pl.BlockSpec(
@@ -1030,24 +1152,32 @@
         return pl.BlockSpec(shape, lambda i: (0,) * len(shape))
 
     dma = pltpu.SemaphoreType.DMA
-    inputs = (tok, act, weights, query, key, value, lse, grad_heads, cosine, sine, group, early)
+    inputs = (tok, act, weights, query, key, value, lse, grad_heads, cosine, sine, early, tokens, mixed,
+              grad_mixed, probs, lin, gains, shared, routed)
+    table_shape = (ROW_PAD, 4 * D + 3 * FF + MISC)
     return pl.pallas_call(
         kernel,
         grid=(units,),
         out_shape=(
-            jax.ShapeDtypeStruct((ndp, grid.slots, SEG, D), BF16),
-            jax.ShapeDtypeStruct((ROW_PAD, early_width), F32),
-            jax.ShapeDtypeStruct((ROW_PAD, late_width), F32),
-            jax.ShapeDtypeStruct((nex - 1,) + routed.shape[1:], BF16),
+            jax.ShapeDtypeStruct((TOK_DEV, D), BF16),
+            jax.ShapeDtypeStruct((TOK_DEV, D), F32),
+            jax.ShapeDtypeStruct(table_shape, F32),
+            jax.ShapeDtypeStruct(partial.shape[1:], BF16),
         ),
-        in_specs=[pl.BlockSpec(memory_space=pltpu.SMEM)] + [whole(v) for v in inputs] + [any_spec()],
+        in_specs=[pl.BlockSpec(memory_space=pltpu.SMEM)]
+        + [whole(v) for v in inputs]
+        + [any_spec()],
         out_specs=(
-            any_spec(),
-            whole_out((ROW_PAD, early_width)),
-            whole_out((ROW_PAD, late_width)),
-            any_spec(),
+            whole_out((TOK_DEV, D)),
+            whole_out((TOK_DEV, D)),
+            whole_out(table_shape),
+            whole_out(partial.shape[1:]),
         ),
         scratch_shapes=[
+            pltpu.VMEM((ndp, grid.slots, SEG, D), BF16),
+            pltpu.VMEM((ROW_PAD, early_width), F32),
+            pltpu.VMEM((ROW_PAD, late_width), F32),
+            pltpu.VMEM((nex - 1,) + routed.shape[1:], BF16),
             pltpu.VMEM((length, D), F32),
             pltpu.VMEM((grid.slots, length, D), BF16),
             pltpu.VMEM((HEAD_DIM, length), F32),
@@ -1067,9 +1197,10 @@
         + early_sum.scratch_x()
         + early_sum.scratch_dp()
         + late_sum.scratch_x()
-        + late_sum.scratch_dp(),
+        + late_sum.scratch_dp()
+        + settle.scratch_z(),
         compiler_params=pltpu.CompilerParams(
-            collective_id=3, has_side_effects=True, vmem_limit_bytes=56 * MIB
+            collective_id=3, has_side_effects=True, vmem_limit_bytes=60 * MIB
         ),
         cost_estimate=pl.CostEstimate(
             flops=units * length * length * HEAD_DIM * 2 * 20,
@@ -1077,7 +1208,7 @@
             transcendentals=units * length * length,
         ),
         name="attend_back",
-    )(lives, *inputs, routed)
+    )(lengths, *inputs, partial)
 
 
 def experts_step(grid, number, weights, act_all, cot_all, ranks, gates, before, early, done=None):
@@ -1126,7 +1257,8 @@
             spread_ref = early_out if not last else take(1)[0] if first else early_ref
             scatter.bind(spread_ref)
         if settle is not None:
-            settle.bind(done_ref, take(len(settle.scratch())))
+            settle.bind(done_ref)
+            settle.bind_y(done_out, take(len(settle.scratch_y())))
         s = pl.program_id(0)
         dp, ex = lax.axis_index("dp"), lax.axis_index("expert")
 
@@ -1150,7 +1282,7 @@
                     peers += [(lax.rem(dp + d, ndp), ex) for d in range(1, ndp)]
                 greet(peers)
                 if settle is not None:
-                    settle.start()
+                    settle.start_y()
                 if first:
                     scatter.start()
                 else:
@@ -1238,13 +1370,6 @@
                 if last:
                     scatter.along_dp()
 
-        if settle is not None:
-            for n, which in enumerate(settle.order):
-
-                @pl.when(s == min(n, nex - 2))
-                def _():
-                    settle.along_z([which])
-
         own = []
         if last:
             own = [
@@ -1289,7 +1414,7 @@
         @pl.when(s == nex - 1)
         def _():
             if settle is not None:
-                settle.finish(done_out)
+                settle.finish_y()
             if last:
                 scatter.finish(early_out)
                 for step in range(nex - 1):
@@ -1342,8 +1467,8 @@
         out_shape.append(jax.ShapeDtypeStruct(shape, F32 if last else BF16))
         out_specs.append(whole_out(shape))
     if settle is not None:
-        out_shape.append(jax.ShapeDtypeStruct(done.shape[1:], BF16))
-        out_specs.append(whole_out(done.shape[1:]))
+        out_shape.append(jax.ShapeDtypeStruct((grid.nz,) + done.shape[1:], BF16))
+        out_specs.append(any_spec())
     scratch = [
         pltpu.VMEM((D, batch * CAP), BF16),
         pltpu.VMEM((D, batch * CAP), BF16),
@@ -1369,7 +1494,7 @@
     if first and last:
         scratch.append(pltpu.VMEM(scatter.spread_shape(), BF16))
     if settle is not None:
-        scratch += settle.scratch()
+        scratch += settle.scratch_y()
     return pl.pallas_call(
         kernel,
         grid=(nex,),
@@ -1388,6 +1513,142 @@
             transcendentals=nex * CAP * FF,
         ),
         name="experts_step",
+    )(*inputs)
+
+
+def middle_step(grid, gin, ggate, mixed, probs, lin, gact, act_across, heads, grad_out, small, gain, terms,
+                partial):
+    ndp, nex, units = grid.ndp, grid.nex, grid.units
+    local = EXPERTS // nex
+    settle = ShardScatter(grid, *terms.shape[1:])
+    settle_before = None if partial is None else ShardScatter(grid, *partial.shape[1:])
+
+    def kernel(gin_ref, ggate_ref, mixed_ref, probs_ref, lin_ref, gact_ref, across_ref, heads_ref,
+               go_ref, small_ref, gain_ref, terms_ref, *refs):
+        refs = list(refs)
+        partial_ref = refs.pop(0) if settle_before is not None else None
+        dst, grad_mixed_ref, middle_ref, settle_out = refs[:4]
+        del refs[:4]
+        before_out = refs.pop(0) if settle_before is not None else None
+        flipped, buf, send, recv, loc = refs[:5]
+        settle_refs, before_refs = refs[5:9], refs[9:]
+        dp, ex = lax.axis_index("dp"), lax.axis_index("expert")
+        greet([(lax.rem(dp + d, ndp), ex) for d in range(1, ndp)])
+        settle.bind(terms_ref)
+        settle.bind_y(settle_out, settle_refs)
+        settle.start_y()
+        if settle_before is not None:
+            settle_before.bind(partial_ref)
+            settle_before.bind_z(before_refs)
+            settle_before.start_z()
+
+        grad_out = go_ref[...].astype(F32)
+        probs = probs_ref[...]
+        shared_gate = probs[:, EXPERTS : EXPERTS + 1]
+        flipped[...] = jnp.zeros_like(flipped)
+        for n in range(nex):
+            flipped[n * local : (n + 1) * local] = ggate_ref[n]
+        grad_probs = flipped[...].T
+        lane = lax.broadcasted_iota(jnp.int32, probs.shape, 1)
+        inner = jnp.sum(
+            jnp.where(lane < EXPERTS, probs * grad_probs, 0.0), axis=1, keepdims=True
+        )
+        svec = shared_gate * (1.0 - shared_gate)
+        svec = svec * jnp.sum(grad_out * lin_ref[...], axis=1, keepdims=True)
+        grad_misc = jnp.where(
+            lane < EXPERTS,
+            probs * (grad_probs - inner),
+            jnp.where(lane == EXPERTS, svec, 0.0),
+        ).astype(BF16)
+        grad_act = gact_ref[...] + dot(grad_misc, small_ref[:, :MISC], 1, 1)
+        for n in range(nex):
+            grad_act += gin_ref[n].astype(F32)
+        mixed = mixed_ref[...]
+        scale = lax.rsqrt(jnp.mean(mixed * mixed, axis=-1, keepdims=True) + eps_norm)
+        normed = mixed * scale
+        gain_grad = jnp.sum(grad_act * normed, axis=0, keepdims=True)
+        weighted = grad_act * gain_ref[2:3]
+        grad_mixed = grad_out + scale * (
+            weighted - normed * jnp.mean(weighted * normed, axis=-1, keepdims=True)
+        )
+        grad_mixed_ref[...] = grad_mixed
+        grad_low = grad_mixed.astype(BF16)
+        for s in range(SERIES_DEV):
+            rows = slice(s * SEG, (s + 1) * SEG)
+            grad = dot(small_ref[:, MISC:], grad_low[rows], 1, 1).astype(BF16)
+            buf[s * HEADS : (s + 1) * HEADS] = grad.reshape(HEADS, HEAD_DIM, SEG)
+        if units * ndp > UNITS_ALL:
+            buf[UNITS_ALL:] = jnp.zeros((units * ndp - UNITS_ALL, HEAD_DIM, SEG), BF16)
+        lanes = pl.ds(pl.multiple_of(dp * SEG, SEG), SEG)
+        copies = []
+        for d in far_first(ndp):
+            target = lax.rem(dp + d, ndp)
+            copy = remote(
+                buf.at[pl.ds(target * units, units)], dst.at[:, :, lanes],
+                send.at[d - 1], recv.at[d - 1], (target, ex),
+            )
+            copy.start()
+            copies.append(copy)
+        copy = pltpu.make_async_copy(
+            buf.at[pl.ds(dp * units, units)], dst.at[:, :, lanes], loc
+        )
+        copy.start()
+        copies.append(copy)
+        group = group_matrix(grid)
+        total = jnp.zeros((D, D), F32)
+        for s in range(SERIES_DEV):
+            attn = heads_ref[s * HEADS : (s + 1) * HEADS].reshape(D, SEG)
+            attn = dot(group, attn).astype(BF16)
+            total += dot(attn, grad_low[s * SEG : (s + 1) * SEG])
+        middle_ref[:, :D] = total.astype(BF16)
+        gain_rows = jnp.broadcast_to(gain_grad, (MISC, D)).astype(BF16)
+        gain_column = dot(group, gain_rows, 1, 1)
+        misc_grad = dot(across_ref[...], grad_misc)
+        lane = lax.broadcasted_iota(jnp.int32, misc_grad.shape, 1)
+        misc_grad = jnp.where(lane == EXPERTS + 2, gain_column, misc_grad)
+        middle_ref[:, D:] = misc_grad.astype(BF16)
+        settle.finish_y()
+        for copy in copies:
+            copy.wait()
+        if settle_before is not None:
+            settle_before.finish_z(before_out)
+
+    dma = pltpu.SemaphoreType.DMA
+    vmem = pl.BlockSpec(memory_space=pltpu.VMEM)
+    hbm = pl.BlockSpec(memory_space=pltpu.HBM)
+    inputs = [gin, ggate, mixed, probs, lin, gact, act_across, heads, grad_out, small, gain]
+    in_specs = [vmem] * len(inputs) + [any_spec()]
+    out_shape = [
+        jax.ShapeDtypeStruct((units, HEAD_DIM, SEG * ndp), BF16),
+        jax.ShapeDtypeStruct((TOK_DEV, D), F32),
+        jax.ShapeDtypeStruct((D, D + MISC), BF16),
+        jax.ShapeDtypeStruct((grid.nz,) + terms.shape[1:], BF16),
+    ]
+    out_specs = [any_spec(), vmem, vmem, hbm]
+    scratch = [
+        pltpu.VMEM((MISC, TOK_DEV), F32),
+        pltpu.VMEM((units * ndp, HEAD_DIM, SEG), BF16),
+        dma((ndp - 1,)),
+        dma((ndp - 1,)),
+        dma,
+    ] + settle.scratch_y()
+    inputs.append(terms)
+    if settle_before is not None:
+        inputs.append(partial)
+        in_specs.append(any_spec())
+        out_shape.append(jax.ShapeDtypeStruct(partial.shape[1:], BF16))
+        out_specs.append(vmem)
+        scratch += settle_before.scratch_z()
+    return pl.pallas_call(
+        kernel,
+        out_shape=tuple(out_shape),
+        in_specs=in_specs,
+        out_specs=tuple(out_specs),
+        scratch_shapes=scratch,
+        compiler_params=pltpu.CompilerParams(
+            collective_id=2, has_side_effects=True, vmem_limit_bytes=60 * MIB
+        ),
+        name="middle_step",
     )(*inputs)
 
 
@@ -1453,145 +1714,47 @@
     tok_all, dense_all, cot_all, rank_all = first_exchange(
         grid, tokens, shard_first, grad_out_low, ranks
     )
-    tok_all, expert_send = lax.optimization_barrier((tok_all, expert_send))
     expert_all = [
         lax.all_gather(expert_send[e], "dp", axis=0, tiled=True) for e in range(local_experts)
     ]
     tok_all = tok_all.reshape(grid.slots, length, D)
 
     dense_all = dense_all.reshape(grid.ndev * ROW_PAD, -1)
-    row = jnp.arange(D, dtype=jnp.int32)
-    row_from = (row // rows_dev) * ROW_PAD + row % rows_dev
-    unpad = (row_from[:, None] == jnp.arange(grid.ndev * ROW_PAD)[None, :]).astype(BF16)
-    qkv_rows = dot(dense_all[:, : 3 * D], unpad, 0, 1).astype(BF16)
-    w_misc = dot(unpad, dense_all[:, 3 * D :]).astype(BF16)
-    w_misc, w_output = w_misc[:, :MISC], w_misc[:, MISC:]
-    gain_first = w_misc[:, EXPERTS + 1].astype(F32)
-    gain_second = w_misc[:, EXPERTS + 2].astype(F32)
-
-    unit = jnp.minimum(dp * grid.units + jnp.arange(grid.units, dtype=jnp.int32), UNITS_ALL - 1)
-    lives = lengths[unit // HEADS]
+
     half = HEAD_DIM // 2
     inverse = rope_base ** (-jnp.arange(half, dtype=F32) * 2.0 / HEAD_DIM)
     angles = inverse[:, None] * jnp.arange(length, dtype=jnp.int32).astype(F32)[None, :]
     cosine, sine = jnp.cos(angles), jnp.sin(angles)
-    heads_here, rest, act_one, query, key, value, lse = attend(
-        grid, lives, tok_all, qkv_rows, gain_first[None, :], cosine, sine, shard_rest
+    heads_here, rest, act_one, query, key, value, lse, qkv_rows = attend(
+        grid, lengths, tok_all, dense_all, cosine, sine, shard_rest
     )
-    w_shared = dot(unpad, rest.reshape(grid.ndev * ROW_PAD, -1)).astype(BF16)
     heads_here = heads_here.reshape(-1, HEAD_DIM, SEG)[:UNITS_ALL]
-    attn_low = heads_here.reshape(SERIES_DEV, D, SEG).transpose(0, 2, 1).reshape(TOK_DEV, D)
-
-    residual = tokens.astype(F32).reshape(TOK_DEV, D)
-    mixed_rows = residual + dot(attn_low, w_output)
-    scale_two = lax.rsqrt(jnp.mean(mixed_rows * mixed_rows, axis=-1, keepdims=True) + eps_norm)
-    normed_two = mixed_rows * scale_two
-    act_two = (normed_two * gain_second).astype(BF16)
-    misc = dot(act_two, w_misc)
-    router_probs = jax.nn.softmax(misc[:, :EXPERTS], axis=-1)
-    shared_gate = jax.nn.sigmoid(misc[:, EXPERTS : EXPERTS + 1])
-
-    row_dev = row // rows_dev
-    row_to = ((row_dev % nex) * ndp + row_dev // nex) * rows_dev + row % rows_dev
-    group = (row[:, None] == row_to[None, :]).astype(BF16)
-    act_all, gates_all, shared_lin, grad_act_shared, early = gather_shared(
-        grid,
-        act_two,
-        router_probs.T.reshape(nex, local_experts, TOK_DEV),
-        shared_gate,
-        grad_out_low,
-        w_shared,
-        group,
+
+    (act_all, gates_all, mixed_rows, probs, shared_lin, grad_act_shared, early, act_across, small,
+     gains) = route_rows(
+        grid, heads_here, tokens, dense_all, grad_out_low, rest.reshape(grid.ndev * ROW_PAD, -1)
     )
-    before, terms, expert_sums = None, None, []
+    before, terms, partial = None, None, None
     for e in range(local_experts):
         results = experts_step(
             grid, e, expert_all[e], act_all, cot_all, rank_all, gates_all, before, early, terms
         )
-        before, terms, early = results[:3], results[3], results[4]
-        expert_sums += results[5:]
-        if e + 1 < local_experts:
-            terms = terms.reshape(ndp, shard_rows, FF)
-    expert_sums.append(lax.psum_scatter(terms, "dp", scatter_dimension=0, tiled=True))
+        before, early = results[:3], results[4]
+        terms = results[3].reshape(ndp, shard_rows, FF)
+        partial = results[5] if e else None
     gin_back, ggate_back, routed_parts = before
 
-    grad_out = grad_out_low.astype(F32)
-    grad_svec_logit = (
-        shared_gate * (1.0 - shared_gate) * jnp.sum(grad_out * shared_lin, axis=-1, keepdims=True)
-    ).astype(BF16)
-    grad_router_probs = ggate_back.reshape(EXPERTS, TOK_DEV).T
-    grad_logits = (
-        router_probs
-        * (grad_router_probs - jnp.sum(router_probs * grad_router_probs, axis=-1, keepdims=True))
-    ).astype(BF16)
-    grad_misc = jnp.concatenate(
-        [grad_logits, grad_svec_logit, jnp.zeros((TOK_DEV, MISC - EXPERTS - 1), BF16)], axis=1
+    grad_heads, grad_mixed, middle, partial, *expert_sums = middle_step(
+        grid, gin_back, ggate_back, mixed_rows, probs, shared_lin, grad_act_shared, act_across,
+        heads_here, grad_out_low, small, gains, terms, partial,
     )
-    grad_act_two = (
-        jnp.sum(gin_back.astype(F32), axis=0)
-        + grad_act_shared
-        + dot(grad_misc, w_misc, 1, 1)
+
+    output, grad_tokens, dense_table, last_sum = attend_back(
+        grid, lengths, tok_all, act_one, qkv_rows, query, key, value, lse, grad_heads, cosine, sine,
+        middle, routed_parts, partial, tokens, mixed_rows, grad_mixed, probs, shared_lin, gains, early,
     )
-    grad_gain_two = jnp.sum(grad_act_two * normed_two, axis=0)
-    weighted_two = grad_act_two * gain_second
-    grad_mixed = grad_out + scale_two * (
-        weighted_two - normed_two * jnp.mean(weighted_two * normed_two, axis=-1, keepdims=True)
-    )
-    grad_attn_low = grad_mixed.astype(BF16)
-    grad_heads = dot(grad_attn_low, w_output, 1, 1).astype(BF16)
-    grad_heads = grad_heads.reshape(SERIES_DEV, SEG, D).transpose(0, 2, 1)
-    grad_heads = grad_heads.reshape(UNITS_ALL, HEAD_DIM, SEG)
-    grad_heads = jnp.pad(grad_heads, ((0, grid.units * ndp - UNITS_ALL), (0, 0), (0, 0)))
-    attn_grouped = jnp.einsum(
-        "gf,sfp->gsp", group, heads_here.reshape(SERIES_DEV, D, SEG), preferred_element_type=F32
-    )
-    grad_heads, middle = heads_in(
-        grid,
-        grad_heads.reshape(ndp, grid.units, HEAD_DIM, SEG),
-        dot(group, act_two, 1, 1).astype(BF16),
-        attn_grouped.astype(BF16).reshape(D, TOK_DEV),
-        grad_attn_low,
-        grad_misc,
-    )
-    gain_two_grouped = dot(group, grad_gain_two.astype(BF16)[:, None]).astype(BF16)
-    middle = middle.at[:, D + EXPERTS + 2].set(gain_two_grouped[:, 0])
-
-    back, middle, late, routed_back = attend_back(
-        grid, lives, tok_all, act_one, qkv_rows, query, key, value, lse,
-        grad_heads, cosine, sine, group, middle, routed_parts,
-    )
-    routed = jnp.sum(routed_back.astype(F32), axis=0) + routed_parts[nex - 1].astype(F32)
-    output = (mixed_rows + routed + shared_gate * shared_lin).astype(BF16)
-    grad_act_one = jnp.stack(
-        [
-            sum(
-                back[owner, owned.index(s)].astype(F32)
-                for owner, owned in enumerate(grid.owned)
-                if s in owned
-            )
-            for s in range(SERIES_DEV)
-        ]
-    ).reshape(TOK_DEV, D)
-    scale_one = lax.rsqrt(jnp.mean(residual * residual, axis=-1, keepdims=True) + eps_norm)
-    normed_one = residual * scale_one
-    weighted_one = grad_act_one * gain_first
-    grad_tokens = grad_mixed + scale_one * (
-        weighted_one - normed_one * jnp.mean(weighted_one * normed_one, axis=-1, keepdims=True)
-    )
-
-    early, middle, late = early[:rows_dev], middle[:rows_dev], late[:rows_dev]
-    dense_grad = jnp.concatenate(
-        [
-            late[:, : 3 * D],
-            middle[:, : D + EXPERTS],
-            early,
-            middle[:, D + EXPERTS : D + EXPERTS + 1],
-            late[:, 3 * D : 3 * D + 1],
-            middle[:, D + EXPERTS + 2 : D + EXPERTS + 3],
-        ],
-        axis=1,
-    ).reshape(-1)
-
+    dense_grad = dense_table[:rows_dev, : dense_weights.shape[0] // rows_dev].reshape(-1)
+    expert_sums.append(last_sum)
     expert_sums = jnp.stack(expert_sums)
     unmixed = jnp.einsum("erg,fg->erf", expert_sums, mix, preferred_element_type=F32)
     expert_grad = jnp.where(is_down, expert_sums.astype(F32), unmixed)

time: 460 us -> 444 us (0.965)
  Pallas kernels: 353 us -> 392 us
  local copies, waits for them, and re-layouts: 32.9 us -> 9.98 us
  other arithmetic: 32 us -> 14 us
  matrix products: 22 us -> 5.64 us
    pallas_call x3, Pallas kernels: 125 us -> 169 us  [the longest x1 85.9 us: attend_back(): pl.pallas_call(kernel, grid=(units,), out_shape=(jax.ShapeDtypeStruct((TO...]
    dot_general x9 -> x0, matrix products: 15.8 us -> none  [dot(): lax.dot_general(left, right, (((left_dim,), (right_dim,)), ((), ())), pre...]
    unnamed x135 -> x35, local copies, waits for them, and re-layouts: 19 us -> 5.4 us
    pallas_call x2, Pallas kernels: 118 us -> 109 us  [experts_step(): pl.pallas_call(kernel, grid=(nex,), out_shape=tuple(out_shape), in_specs=...]
    reduce_sum x7 -> x0, other arithmetic: 7.77 us -> none  [the longest x1 3.13 us: local(): jnp.sum(gin_back.astype(F32), axis=0) + grad_act_shared]
  transfers between devices with their start and end apart: 3 -> 2, of which waited for: 0 -> 0; matrix products, arithmetic and copies ran while one was open for 9% -> 1% of each run, Pallas kernels for 52% -> 42%
where the time goes in v4:
time: 444 us; the launch traced here: 437 us
  Pallas kernels  392 us (88%)
  between operations  14.6 us (3%)
  other arithmetic  14 us (3%)
  local copies, waits for them, and re-layouts  9.98 us (2%)
  matrix products  5.64 us (1%)
    pallas_call x2, Pallas kernels, experts_step(): pl.pallas_call(kernel, grid=(nex,), out_shape=tuple(out_shape), in_specs=...  109 us
    pallas_call x1, Pallas kernels, attend_back(): pl.pallas_call(kernel, grid=(units,), out_shape=(jax.ShapeDtypeStruct((TO...  85.9 us
    pallas_call x1, Pallas kernels, attend(): pl.pallas_call(kernel, grid=(units,), out_shape=(jax.ShapeDtypeStruct((nd...  66.5 us
    pallas_call x1, Pallas kernels, middle_step(): pl.pallas_call(kernel, out_shape=tuple(out_shape), in_specs=in_specs, out...  58 us
    pallas_call x1, Pallas kernels, first_exchange(): pl.pallas_call(kernel, out_shape=(jax.ShapeDtypeStruct((grid.slots, ndp,...  47.3 us
    pallas_call x1, Pallas kernels, route_rows(): pl.pallas_call(kernel, out_shape=(jax.ShapeDtypeStruct((nex, TOK_DEV, D),...  25.2 us
    add x2, other arithmetic, adamw_update(): average_new = average_keep * average + (1.0 - average_keep) * weights_new  10.1 us
  transfers between devices with their start and end apart: 2, of which 0 were waited for; matrix products, arithmetic and copies ran while one was open for 1% of the time, Pallas kernels for 42%

profile of v4, /device:TPU:0, one launch (start us, length us, event | category | flops | bytes accessed | tf_op | source)
XLA Modules:
  0.0 437.0 jit_solution(16100682015216879656)
XLA Ops:
  7.2 0.0 all-gather.7.cloned.1.call-start
  7.3 1.8 convert_element_type.53
  9.1 1.9 fusion.19
  11.0 0.0 copy-start.5
  11.0 0.0 copy-start.13
  11.0 1.0 fusion.44
  12.0 0.0 all-gather.7.cloned.1.call-update
  12.0 0.0 all-gather.5.cloned.1.call-start
  12.1 0.7 all-gather.5.cloned.1.call-update
  12.8 0.0 copy-done.5
  12.8 0.2 reshape.140
  13.0 0.1 slice.34
  13.1 0.1 slice.36
  13.3 0.3 fusion.24
  13.6 0.6 reshape.142.rank_in
  14.2 0.1 concatenate.3
  14.3 0.6 pad.8.shd
  14.9 0.7 pad.9.shard_ref
  15.6 0.1 compare_convert_fusion
  15.7 1.0 multiply_convert_fusion
  16.7 47.3 %first_exchange.1 = (bf16[2,8,128,384]{3,2,1,0:T(8,128)(2,1)}, bf16[32,16,1664]{2,1,0:T(8,128)(2,1)}, bf16[4,768,384]{2,1,0:T(8,128)(2,1)}, f32[4,2,768]{2,1,0:T(2,128)}) custom-call(bf16[6,128,384]{2,1,0:T(8,128)(2,1)} %refs_12_.1, bf16[16,1664]{1,0:T(8,128)(2,1)} %pad.8.shd, bf16[768,384]{1,0:T(8,128)(2,1)} %bitcast.45, f32[4,2,768]{2,1,0:T(2,128)} %reshape.142.rank_in), custom_call_target="tpu_custom_call" | custom-call | tf_op jit(solution)/shard_map/first_exchange/pallas_call | solution.py:401
  64.1 1.0 multiply_sine_fusion
  65.0 66.5 %attend.1 = (bf16[8,9,32,128]{3,2,1,0:T(8,128)(2,1)}, bf16[32,16,4608]{2,1,0:T(8,128)(2,1)}, bf16[2,1024,384]{2,1,0:T(8,128)(2,1)}, bf16[9,32,1024]{2,1,0:T(8,12...) custom-call(s32[6]{0:T(128)} %refs_0_.1, ...), custom_call_target="tpu_custom_call" | custom-call | flops 4831838208 | bytes 8388608 | tf_op jit(solution)/shard_map/attend/pallas_call | solution.py:892
  131.5 25.2 %route_rows.1 = (bf16[4,768,384]{2,1,0:T(8,128)(2,1)}, f32[4,2,768]{2,1,0:T(2,128)}, f32[768,384]{1,0:T(8,128)}, f32[768,128]{1,0:T(8,128)}, f32[768,384]{1,0:T(...) custom-call(bf16[72,32,128]{2,1,0:T(8,128)(2,1)} %bitcast.52, ...), custom_call_target="tpu_custom_call" | custom-call | tf_op jit(solution)/shard_map/route_rows/pallas_call | solution.py:725
  156.7 0.0 all-gather.7.cloned.1.call-done
  156.8 46.6 %experts_step.2 = (f32[4,768,384]{2,1,0:T(8,128)}, f32[4,1,768]{2,1,0:T(1,128)}, f32[4,768,384]{2,1,0:T(8,128)}, bf16[1152,1536]{1,0:T(8,128)(2,1)}, bf16[128,4608]{1,0:T(8,128)(2,1)}) custom-call(bf16[1152,1536]{1,0:T(8,128)(2,1)} %bitcast.62, bf16[4,768,384]{2,1,0:T(8,128)(2,1)} %get-tuple-element.64.refs_1_, ...), custom_call_target="tpu_custom_call" | custom-call | flops 19931332608 | bytes 26214400 | tf_op jit(solution)/shard_map/experts_step/pallas_call | solution.py:1498
  203.4 0.0 all-gather.5.cloned.1.call-done
  203.4 62.4 %experts_step.3 = (bf16[4,768,384]{2,1,0:T(8,128)(2,1)}, f32[4,2,768]{2,1,0:T(2,128)}, bf16[4,768,384]{2,1,0:T(8,128)(2,1)}, bf16[1152,1536]{1,0:T(8,128)(2,1)},...) custom-call(bf16[1152,1536]{1,0:T(8,128)(2,1)} %bitcast.61, bf16[4,768,384]{2,1,0:T(8,128)(2,1)} %get-tuple-element.64.refs_1_, ...), custom_call_target="tpu_custom_call" | custom-call | flops 19931332608 | bytes 26214400 | tf_op jit(solution)/shard_map/experts_step/pallas_call | solution.py:1498
  265.7 58.0 %middle_step.1 = (bf16[9,32,1024]{2,1,0:T(8,128)(2,1)}, f32[768,384]{1,0:T(8,128)}, bf16[384,512]{1,0:T(8,128)(2,1)}, bf16[4,144,1536]{2,1,0:T(8,128)(2,1)}, bf16[144,1536]{1,0:T(8,128)(2,1)}) custom-call(bf16[4,768,384]{2,1,0:T(8,128)(2,1)} %get-tuple-element.74.gin_ref, f32[4,2,768]{2,1,0:T(2,128)} %get-tuple-element.75.ggate_ref, ...), custom_call_target="tpu_custom_call" | custom-call | tf_op jit(solution)/shard_map/middle_step/pallas_call | solution.py:1642
  323.8 85.9 %attend_back.1 = (bf16[768,384]{1,0:T(8,128)(2,1)}, f32[768,384]{1,0:T(8,128)}, f32[16,6272]{1,0:T(8,128)}, bf16[144,1536]{1,0:T(8,128)(2,1)}) custom-call(s32[6]{0:T(128)} %refs_0_.1, bf16[2,1024,384]{2,1,0:T(8,128)(2,1)} %bitcast.65, bf16[2,1024,384]{2,1,0:T(8,128)(2,1)} %get-tuple-element.56.refs_2_, bf16[1280,384]{1,0:T(8,128)(2,1)} %get-tuple-element.57.refs_3_, ...), custom_call_target="tpu_custom_call" | custom-call | flops 12079595520 | bytes 12582912 | tf_op jit(solution)/shard_map/attend_back/pallas_call | solution.py:1158
  409.7 1.2 reshape.154
  410.9 0.0 copy-start.6
  410.9 0.0 copy-start.10
  410.9 0.0 copy-start.11
  410.9 0.0 copy-start.12
  410.9 0.0 copy-start.4
  410.9 3.4 fusion.10
  414.4 0.0 copy-start.2
  414.4 0.0 copy-start.3
  414.4 1.4 copy.26
  415.8 0.0 copy-start
  415.8 0.0 copy-start.1
  415.8 1.2 multiply_add_fusion.3
  417.0 1.5 copy-done.1
  418.5 8.9 %multiply_add_fusion.1 = (f32[2,221184]{1,0:T(2,128)}, f32[2,221184]{1,0:T(2,128)}, f32[2,221184]{1,0:T(2,128)}, f32[2,221184]{1,0:T(2,128)}) fusion(f32[2,221184]{1,0:T(2,128)S(1)} %copy-done.2, f32[2,221184]{1,0:T(2,128)S(1)} %copy-done.1, f32[2,221184]{1,0:T(2,128)S(1)} %bitcast.48, f32[2,221184]{1,0:T(2,128)S(1)} %copy-done.3, f32[2,221184]{1,0:T(2,128)S(1)} %copy-done.4), kind=kLoop, calls=%fused_computation.16 | loop fusion | flops 7520256 | bytes 15925248 | tf_op jit(solution)/shard_map/add | solution.py:51
  427.4 0.8 copy.33
  428.2 0.7 copy-done.7
  428.9 1.0 copy.34
  (29 shorter events, 0.1 us)
Async XLA Ops:
  7.2 149.6 %all-gather.7.cloned.1.call-start = ((), (), s32[]{:S(2)}) async-start(), calls=%async_computation.1 | async-start | bytes 3981312 | tf_op jit(solution)/shard_map/all_gather | solution.py:1718
  11.0 1.8 copy-start.5
  11.0 2.2 copy-start.13
  12.0 3.6 copy-start.14
  12.0 3.7 copy-start.8
  12.0 191.4 %all-gather.5.cloned.1.call-start = ((), (), s32[]{:S(2)}) async-start(), calls=%async_computation | async-start | bytes 3981312 | tf_op jit(solution)/shard_map/all_gather | solution.py:1718
  323.8 87.1 %copy-start.15 = (bf16[144,1536]{1,0:T(8,128)(2,1)S(1)}, bf16[144,1536]{1,0:T(8,128)(2,1)}, u32[]{:S(2)}) copy-start(bf16[144,1536]{1,0:T(8,128)(2,1)} %get-tuple-element.94) | copy-start | bytes 1327108
  410.9 4.9 %copy-start.6 = (f32[73860]{0:T(1024)}, f32[73860]{0:T(1024)S(1)}, u32[]{:S(2)}) copy-start(f32[73860]{0:T(1024)S(1)} %reshape.154) | copy-start | bytes 886324
  410.9 4.9 %copy-start.10 = (f32[73860]{0:T(1024)S(1)}, f32[73860]{0:T(1024)}, u32[]{:S(2)}) copy-start(f32[73860]{0:T(1024)} %param.19) | copy-start | bytes 886324
  410.9 4.9 %copy-start.11 = (f32[73860]{0:T(1024)S(1)}, f32[73860]{0:T(1024)}, u32[]{:S(2)}) copy-start(f32[73860]{0:T(1024)} %param.18) | copy-start | bytes 886324
  410.9 4.9 %copy-start.12 = (f32[73860]{0:T(1024)S(1)}, f32[73860]{0:T(1024)}, u32[]{:S(2)}) copy-start(f32[73860]{0:T(1024)} %param.17) | copy-start | bytes 886324
  410.9 6.1 %copy-start.4 = (f32[2,221184]{1,0:T(2,128)S(1)}, f32[2,221184]{1,0:T(2,128)}, u32[]{:S(2)}) copy-start(f32[2,221184]{1,0:T(2,128)} %param.21) | copy-start | bytes 5308420
  414.4 2.7 copy-start.2
  414.4 2.7 copy-start.3
  415.8 11.6 %copy-start = (f32[1,2,144,1536]{3,1,2,0:T(2,128)}, f32[1,2,144,1536]{3,1,2,0:T(2,128)S(1)}, u32[]{:S(2)}) copy-start(f32[1,2,144,1536]{3,1,2,0:T(2,128)S(1)} %copy.26) | copy-start | bytes 5308420
  415.8 2.7 copy-start.1
  418.5 8.9 %copy-start.9 = (bf16[768,384]{1,0:T(8,128)(2,1)S(1)}, bf16[768,384]{1,0:T(8,128)(2,1)}, u32[]{:S(2)}) copy-start(bf16[768,384]{1,0:T(8,128)(2,1)} %get-tuple-element.91) | copy-start | bytes 1769476
  427.4 1.5 copy-start.7
Sparse Core Ops, SparseCore 0:
  12.1 109.6 all-gather.6
  124.6 64.0 all-gather.4

commit v5 on v4

--- a/solution.py
+++ b/solution.py
@@ -535,41 +535,51 @@
 
     def scratch_z(self):
         g = self.grid
-        block = (self.rows, self.width)
         dma = pltpu.SemaphoreType.DMA
-        return [pltpu.VMEM(block, BF16), pltpu.VMEM((g.nz,) + block, BF16), dma((g.nz, 2)), dma]
-
-    def bind(self, source):
-        self.source = source
+        return [pltpu.VMEM((g.nz, self.rows, self.width), BF16), dma((g.nz, 2))]
+
+    def scratch_own(self):
+        return [pltpu.VMEM((self.rows, self.width), BF16), pltpu.SemaphoreType.DMA]
+
+    def where(self):
         g = self.grid
         self.dp, self.ex = lax.axis_index("dp"), lax.axis_index("expert")
         self.z, self.y = self.dp // g.ny, lax.rem(self.dp, g.ny)
         self.order = far_first(g.nz) + [0]
 
-    def bind_y(self, out, refs):
-        self.out = out
+    def bind_y(self, source, refs):
+        self.where()
+        self.source = source
         self.mine, self.got_y, self.sem_y, self.loc = refs
+        self.sums = self.mine
 
     def bind_z(self, refs):
-        self.own, self.got_z, self.sem_z, self.loc = refs
+        self.got_z, self.sem_z = refs
+
+    def bind_own(self, sums, refs):
+        self.where()
+        self.sums = sums
+        self.own, self.own_sem = refs
 
     def place(self, dz, dy):
         g = self.grid
         return lax.rem(self.z + dz, g.nz) * g.ny + lax.rem(self.y + dy, g.ny)
+
+    def block(self, number):
+        if len(self.source.shape) == 3:
+            return self.source.at[number]
+        return self.source.at[pl.ds(pl.multiple_of(number * self.rows, ROW_PAD), self.rows)]
 
     def y_copy(self, dy, dz):
         return remote(
-            self.source.at[self.place(dz, dy)], self.got_y.at[dy - 1, dz],
+            self.block(self.place(dz, dy)), self.got_y.at[dy - 1, dz],
             self.sem_y.at[dy, dz, 0], self.sem_y.at[dy, dz, 1], (self.place(0, dy), self.ex),
         )
 
     def load(self, dz):
         return pltpu.make_async_copy(
-            self.source.at[self.place(dz, 0)], self.mine.at[dz], self.loc.at[dz]
+            self.block(self.place(dz, 0)), self.mine.at[dz], self.loc.at[dz]
         )
-
-    def store(self, dz):
-        return pltpu.make_async_copy(self.mine.at[dz], self.out.at[dz], self.loc.at[dz])
 
     def start_y(self):
         for dz in self.order:
@@ -577,7 +587,7 @@
                 self.y_copy(dy, dz).start()
             self.load(dz).start()
 
-    def finish_y(self):
+    def sum_y(self, then=None):
         g = self.grid
         for dz in self.order:
             self.load(dz).wait()
@@ -588,31 +598,42 @@
                 for dy in range(1, g.ny):
                     total += self.got_y[dy - 1, dz].astype(F32)
                 self.mine[dz] = total.astype(BF16)
-            self.store(dz).start()
+            if then is not None:
+                then(dz)
+
+    def store_y(self, out):
+        def store(dz):
+            return pltpu.make_async_copy(self.mine.at[dz], out.at[dz], self.loc.at[dz])
+
+        self.sum_y(lambda dz: store(dz).start())
         for dz in self.order:
-            self.store(dz).wait()
+            store(dz).wait()
 
     def z_copy(self, dz):
         return remote(
-            self.source.at[dz], self.got_z.at[dz], self.sem_z.at[dz, 0], self.sem_z.at[dz, 1],
+            self.sums.at[dz], self.got_z.at[dz], self.sem_z.at[dz, 0], self.sem_z.at[dz, 1],
             (self.place(dz, 0), self.ex),
         )
 
     def own_copy(self):
-        return pltpu.make_async_copy(self.source.at[0], self.own, self.loc)
+        return pltpu.make_async_copy(self.sums.at[0], self.own, self.own_sem)
 
     def start_z(self):
         for dz in far_first(self.grid.nz):
             self.z_copy(dz).start()
-        self.own_copy().start()
+        if self.sums is not getattr(self, "mine", None):
+            self.own_copy().start()
 
     def finish_z(self, out):
-        self.own_copy().wait()
-        total = self.own[...].astype(F32)
+        if self.sums is getattr(self, "mine", None):
+            total = self.mine[0].astype(F32)
+        else:
+            self.own_copy().wait()
+            total = self.own[...].astype(F32)
         for dz in range(1, self.grid.nz):
             self.z_copy(dz).wait()
             total += self.got_z[dz].astype(F32)
-        out[...] = total.astype(BF16)
+        out[...] = total.astype(out.dtype)
 
 
 def route_rows(grid, heads, tokens, table, grad_out, weights):
@@ -937,7 +958,7 @@
 
 
 def attend_back(grid, lengths, tok, act, weights, query, key, value, lse, grad_heads, cosine, sine,
-                early, routed, partial, tokens, mixed, grad_mixed, probs, lin, gains, shared):
+                early, routed, zs, tokens, mixed, grad_mixed, probs, lin, gains, shared):
     units, length, ndp, nex = grid.units, act.shape[1], grid.ndp, grid.nex
     blocks = length // QBLOCK
     scale = HEAD_DIM ** (-0.5)
@@ -945,17 +966,21 @@
     early_sum, late_sum = RowScatter(grid, early_width), RowScatter(grid, late_width)
     early = early.reshape(grid.nx, grid.nc, early_sum.rows, early_width)
     steps = [min(n, units - 1) for n in (0, 3)]
-    settle = ShardScatter(grid, *partial.shape[1:])
+    works_z = [ShardScatter(grid, *v.shape[1:]) for v in zs]
+    many = len(zs)
 
     def kernel(*refs):
+        refs = list(refs)
+        z_refs, z_outs = refs[20 : 20 + many], refs[23 + many : 23 + 2 * many]
+        del refs[23 + many : 23 + 2 * many], refs[20 : 20 + many]
         (len_ref, tok_ref, act_ref, w_ref, q_ref, k_ref, v_ref, lse_ref, do_ref, cos_ref, sin_ref,
          early_ref, tokens_ref, mixed_ref, grad_mixed_ref, probs_ref, lin_ref, gains_ref, shared_ref,
-         routed_ref, partial_ref,
-         output_ref, grad_tokens_ref, table_ref, settle_out,
+         routed_ref,
+         output_ref, grad_tokens_ref, table_ref,
          rows_out, early_out, late_out, routed_out,
          acc, back, dq, dk, dv, grads, gain, late_ref, b_send, b_recv, b_loc,
-         early_spread, late_spread, r_send, r_recv) = refs[:44]
-        at = 44
+         early_spread, late_spread, r_send, r_recv) = refs[:42]
+        at = 42
         for work, source, spread in (
             (early_sum, early_ref, early_spread),
             (late_sum, late_ref, late_spread),
@@ -964,8 +989,10 @@
             work.bind_x(source, refs[at : at + 5])
             work.bind_dp(refs[at + 5 : at + 7])
             at += 7
-        settle.bind(partial_ref)
-        settle.bind_z(refs[at:])
+        for work, ref in zip(works_z, z_refs):
+            work.bind_own(ref, refs[at : at + 2])
+            work.bind_z(refs[at + 2 : at + 4])
+            at += 4
 
         def routed_copy(step):
             return remote(
@@ -1003,7 +1030,8 @@
                 [(lax.rem(dp + d, ndp), ex) for d in range(1, ndp)]
                 + [(dp, lax.rem(ex + d, nex)) for d in range(1, nex)]
             )
-            settle.start_z()
+            for work in works_z:
+                work.start_z()
             early_sum.start()
             grads[...] = jnp.zeros_like(grads)
             gain[...] = jnp.zeros_like(gain)
@@ -1141,7 +1169,8 @@
             ends = jnp.where(lane == EXPERTS + 1, late[:, 3 * D :], misc)
             ends = jnp.where((lane >= EXPERTS) & (lane < EXPERTS + 3), ends, 0.0)
             table_ref[:, 4 * D + 3 * FF :] = wide[:, 3 * FF :] + ends
-            settle.finish_z(settle_out)
+            for work, out in zip(works_z, z_outs):
+                work.finish_z(out)
 
     def whole(array):
         return pl.BlockSpec(
@@ -1162,17 +1191,17 @@
             jax.ShapeDtypeStruct((TOK_DEV, D), BF16),
             jax.ShapeDtypeStruct((TOK_DEV, D), F32),
             jax.ShapeDtypeStruct(table_shape, F32),
-            jax.ShapeDtypeStruct(partial.shape[1:], BF16),
-        ),
+        )
+        + tuple(jax.ShapeDtypeStruct((work.rows, work.width), BF16) for work in works_z),
         in_specs=[pl.BlockSpec(memory_space=pltpu.SMEM)]
         + [whole(v) for v in inputs]
-        + [any_spec()],
+        + [any_spec()] * many,
         out_specs=(
             whole_out((TOK_DEV, D)),
             whole_out((TOK_DEV, D)),
             whole_out(table_shape),
-            whole_out(partial.shape[1:]),
-        ),
+        )
+        + tuple(whole_out((work.rows, work.width)) for work in works_z),
         scratch_shapes=[
             pltpu.VMEM((ndp, grid.slots, SEG, D), BF16),
             pltpu.VMEM((ROW_PAD, early_width), F32),
@@ -1198,7 +1227,7 @@
         + early_sum.scratch_dp()
         + late_sum.scratch_x()
         + late_sum.scratch_dp()
-        + settle.scratch_z(),
+        + sum((work.scratch_own() + work.scratch_z() for work in works_z), []),
         compiler_params=pltpu.CompilerParams(
             collective_id=3, has_side_effects=True, vmem_limit_bytes=60 * MIB
         ),
@@ -1208,20 +1237,25 @@
             transcendentals=units * length * length,
         ),
         name="attend_back",
-    )(lengths, *inputs, partial)
-
-
-def experts_step(grid, number, weights, act_all, cot_all, ranks, gates, before, early, done=None):
+    )(lengths, *inputs, *zs)
+
+
+def experts_step(grid, number, weights, act_all, cot_all, ranks, gates, before, early, ys, zs):
     nex, nc, ndp = grid.nex, grid.nc, grid.ndp
     rows = act_all.shape[1]
     local = EXPERTS // nex
-    parts, wide = FF // D, 2 * D
+    parts, wide = FF // D, FF // 2
     first, last = number == 0, number == local - 1
     batch = math.gcd(nex, 4)
     flushes = nex // batch
+    steps = 2 * nex
+    shard_rows = 3 * D // ndp
+    inline = shard_rows % ROW_PAD == 0
     scatter = RowScatter(grid, 3 * FF) if first or last else None
-    talks = first or last
-    settle = None if done is None else ShardScatter(grid, *done.shape[1:])
+    early_work = ShardScatter(grid, ROW_PAD, 3 * FF) if last else None
+    works_y = [ShardScatter(grid, *v.shape[1:]) for v in ys]
+    works_z = [ShardScatter(grid, *v.shape[1:]) for v in zs]
+    work_own = ShardScatter(grid, shard_rows, wide) if inline else None
     if first:
         early = early.reshape(grid.nx, nc, scatter.rows, 3 * FF)
 
@@ -1235,250 +1269,301 @@
 
         w_ref, act_ref, cot_ref, rank_ref, gate_ref = take(5)
         prev = take(3) if before is not None else None
-        early_ref = take(1)[0] if talks else None
-        done_ref = take(1)[0] if settle is not None else None
-        if last:
-            gin_out, ggate_out = take(2)
-            routed_ref, grad_ref = take(2)
-        else:
-            gin_ref, ggate_ref = take(2)
-            routed_ref, grad_ref = take(2)
-        early_out = take(1)[0] if talks else None
-        done_out = take(1)[0] if settle is not None else None
+        early_ref = take(1)[0] if scatter is not None else None
+        y_refs, z_refs = take(len(ys)), take(len(zs))
+        gin_ref, ggate_ref, routed_ref = take(3)
+        early_out = take(1)[0] if scatter is not None else None
+        own_outs = take(2)
+        sum_outs = take(len(ys) + len(zs))
         xt_ref, dyt_ref, dg_ref, du_ref, hid_ref, down_ref = take(6)
+        taken_ref, rows_ref, result_ref, back_ref, grad_ref, own_sem = take(6)
         acc_ref = take(1)[0] if flushes > 1 else None
         if last:
             gin_buf, ggate_buf, send, recv, loc = take(5)
         if first:
             scatter.bind_x(early_ref, take(len(scatter.scratch_x())))
-        if last:
-            scatter.bind_dp(take(len(scatter.scratch_dp())))
-        if talks:
+        if scatter is not None:
             spread_ref = early_out if not last else take(1)[0] if first else early_ref
             scatter.bind(spread_ref)
-        if settle is not None:
-            settle.bind(done_ref)
-            settle.bind_y(done_out, take(len(settle.scratch_y())))
-        s = pl.program_id(0)
+        if last:
+            early_work.bind_y(spread_ref, take(4))
+            early_work.bind_z(take(2))
+        for work, ref in zip(works_y, y_refs):
+            work.bind_y(ref, take(4))
+            work.bind_z(take(2))
+        for work, ref in zip(works_z, z_refs):
+            work.bind_own(ref, take(2))
+            work.bind_z(take(2))
+        if inline:
+            work_own.bind_y(grad_ref.at[0], take(4))
+        t = pl.program_id(0)
+        half, part = lax.rem(t // batch, 2), lax.rem(t, batch)
+        s = (t // (2 * batch)) * batch + part
         dp, ex = lax.axis_index("dp"), lax.axis_index("expert")
 
         def copies(step):
             target = lax.rem(ex + 1 + step, nex)
             pairs = (
-                (gin_buf.at[step], gin_out.at[step]),
-                (ggate_buf.at[step], ggate_out.at[ex]),
+                (gin_buf.at[step], gin_ref.at[step]),
+                (ggate_buf.at[step], ggate_ref.at[ex]),
             )
             return [
                 remote(src, dst, send.at[step, n], recv.at[step, n], (dp, target))
                 for n, (src, dst) in enumerate(pairs)
             ]
 
-        if talks:
-
-            @pl.when(s == 0)
-            def _():
-                peers = [(dp, lax.rem(ex + d, nex)) for d in range(1, nex)]
-                if last:
-                    peers += [(lax.rem(dp + d, ndp), ex) for d in range(1, ndp)]
-                greet(peers)
-                if settle is not None:
-                    settle.start_y()
-                if first:
-                    scatter.start()
-                else:
-                    scatter.along_dp()
-
-        @pl.when(s == 0)
+        @pl.when(t == 0)
         def _():
-            for part in range(parts):
-                lanes = slice(part * D, (part + 1) * D)
+            greet(
+                [(dp, lax.rem(ex + d, nex)) for d in range(1, nex)]
+                + [(lax.rem(dp + d, ndp), ex) for d in range(1, ndp)]
+            )
+            for work in works_y:
+                work.start_y()
+            for work in works_z:
+                work.start_z()
+            if first:
+                scatter.start()
+            elif last:
+                early_work.start_y()
+            for n in range(parts):
+                lanes = slice(n * D, (n + 1) * D)
                 down_ref[lanes] = w_ref[2 * D : 3 * D, lanes]
 
         rank = rank_ref[0, number : number + 1, :]
-        rank_column = jnp.broadcast_to(rank, (8, rows)).T[:, :1]
         slot_down = lax.broadcasted_iota(jnp.int32, (CAP, rows), 0).astype(F32)
-        slot_across = lax.broadcasted_iota(jnp.int32, (rows, CAP), 1).astype(F32)
         pick = slot_down == rank
-        pick_low = pick.astype(F32).astype(BF16)
-        spread = (slot_across == rank_column).astype(F32).astype(BF16)
-        picked = dot(pick_low, jnp.concatenate([act_ref[0], cot_ref[0]], axis=1))
-        taken_wide, grad_rows = picked[:, :D], picked[:, D:]
-        taken = taken_wide.astype(BF16)
         gate_row = gate_ref[0, number : number + 1, :]
         gate = jnp.sum(jnp.where(pick, gate_row, 0.0), axis=1, keepdims=True)
-        grad_wide = gate * grad_rows
-        grad_result = grad_wide.astype(BF16)
-        block = pl.ds(pl.multiple_of(lax.rem(s, batch) * CAP, CAP), CAP)
-        xt_ref[:, block] = taken_wide.T.astype(BF16)
-        dyt_ref[:, block] = grad_wide.T.astype(BF16)
-        result = jnp.zeros((CAP, D), F32)
-        grad_taken = jnp.zeros((CAP, D), F32)
-        for part in range(0, FF, wide):
-            lanes = slice(part, part + wide)
-            w_gate = w_ref[0:D, lanes]
-            w_up = w_ref[D : 2 * D, lanes]
-            w_down = down_ref[lanes]
-            gate_lin = dot(taken, w_gate)
-            up_lin = dot(taken, w_up)
-            sig = 0.5 * jnp.tanh(0.5 * gate_lin) + 0.5
-            silu = gate_lin * sig
-            hidden = (silu * up_lin).astype(BF16)
-            result += dot(hidden, w_down)
-            grad_hidden = dot(grad_result, w_down, 1, 1)
-            grad_gate = (grad_hidden * up_lin * (sig + silu * (1.0 - sig))).astype(BF16)
-            grad_up = (grad_hidden * silu).astype(BF16)
-            hid_ref[block, lanes] = hidden
-            dg_ref[block, lanes] = grad_gate
-            du_ref[block, lanes] = grad_up
-            grad_taken += dot(grad_gate, w_gate, 1, 1) + dot(grad_up, w_up, 1, 1)
-        result = result.astype(BF16).astype(F32)
-        grad_gate_slot = jnp.sum(grad_rows * result, axis=1, keepdims=True)
-        grad_gate_row = jnp.sum(jnp.where(pick, grad_gate_slot, 0.0), axis=0, keepdims=True)
-        both = jnp.concatenate([gate * result, grad_taken], axis=1).astype(BF16)
-        both = dot(spread, both)
-        routed, grad_in = both[:, :D], both[:, D:]
-        if prev is not None:
-            grad_in += prev[0][0]
-            routed += prev[2][0]
+        block = pl.ds(pl.multiple_of(part * CAP, CAP), CAP)
+
+        @pl.when(half == 0)
+        def _():
+            pick_low = pick.astype(F32).astype(BF16)
+            picked = dot(pick_low, jnp.concatenate([act_ref[0], cot_ref[0]], axis=1))
+            taken_ref[part] = picked[:, :D].astype(BF16)
+            rows_ref[part] = picked[:, D:].astype(BF16)
+            xt_ref[:, block] = picked[:, :D].T.astype(BF16)
+            dyt_ref[:, block] = (gate * picked[:, D:]).T.astype(BF16)
+
+        taken, grad_rows = taken_ref[part], rows_ref[part].astype(F32)
+        grad_result = (gate * grad_rows).astype(BF16)
+        lanes = pl.ds(pl.multiple_of(half * wide, wide), wide)
+        w_gate, w_up, w_down = w_ref[0:D, lanes], w_ref[D : 2 * D, lanes], down_ref[lanes]
+        gate_lin = dot(taken, w_gate)
+        up_lin = dot(taken, w_up)
+        sig = 0.5 * jnp.tanh(0.5 * gate_lin) + 0.5
+        silu = gate_lin * sig
+        hidden = (silu * up_lin).astype(BF16)
+        result = dot(hidden, w_down)
+        grad_hidden = dot(grad_result, w_down, 1, 1)
+        grad_gate = (grad_hidden * up_lin * (sig + silu * (1.0 - sig))).astype(BF16)
+        grad_up = (grad_hidden * silu).astype(BF16)
+        hid_ref[block], dg_ref[block], du_ref[block] = hidden, grad_gate, grad_up
+        grad_taken = dot(grad_gate, w_gate, 1, 1) + dot(grad_up, w_up, 1, 1)
+
+        @pl.when(half == 0)
+        def _():
+            result_ref[part], back_ref[part] = result, grad_taken
+
+        @pl.when(half == 1)
+        def _():
+            out = (result_ref[part] + result).astype(BF16).astype(F32)
+            grad_gate_slot = jnp.sum(grad_rows * out, axis=1, keepdims=True)
+            grad_gate_row = jnp.sum(jnp.where(pick, grad_gate_slot, 0.0), axis=0, keepdims=True)
+            rank_column = jnp.broadcast_to(rank, (8, rows)).T[:, :1]
+            slot_across = lax.broadcasted_iota(jnp.int32, (rows, CAP), 1).astype(F32)
+            spread = (slot_across == rank_column).astype(F32).astype(BF16)
+            both = jnp.concatenate([gate * out, back_ref[part] + grad_taken], axis=1)
+            both = dot(spread, both.astype(BF16))
+            routed, grad_in = both[:, :D], both[:, D:]
+            if prev is not None:
+                grad_in += prev[0][0]
+                routed += prev[2][0]
+            if last:
+                routed_ref[0] = routed.astype(BF16)
+                gin_buf[s] = grad_in.astype(BF16)
+                if prev is not None:
+                    ggate_buf[s, 0:number] = prev[1][0]
+                ggate_buf[s, number : number + 1] = grad_gate_row
+            else:
+                routed_ref[0] = routed
+                gin_ref[0] = grad_in
+                if prev is not None:
+                    ggate_ref[0, 0:number] = prev[1][0]
+                ggate_ref[0, number : number + 1] = grad_gate_row
+
         if last:
-            routed_ref[0] = routed.astype(BF16)
-            gin_buf[s] = grad_in.astype(BF16)
-            if prev is not None:
-                ggate_buf[s, 0:number] = prev[1][0]
-            ggate_buf[s, number : number + 1] = grad_gate_row
-
-            @pl.when(s < nex - 1)
+
+            @pl.when((half == 1) & (s < nex - 1))
             def _():
                 for copy in copies(s):
                     copy.start()
-        else:
-            routed_ref[0] = routed
-            gin_ref[0] = grad_in
-            if prev is not None:
-                ggate_ref[0, 0:number] = prev[1][0]
-            ggate_ref[0, number : number + 1] = grad_gate_row
 
         if first:
 
-            @pl.when(s == 0)
+            @pl.when(t == 0)
             def _():
                 scatter.along_x()
 
-            @pl.when(s == min(2, nex - 1))
+            @pl.when(t == nex)
             def _():
                 scatter.after_x()
                 if last:
-                    scatter.along_dp()
-
-        own = []
+                    early_work.start_y()
+
         if last:
-            own = [
-                pltpu.make_async_copy(src, dst, loc.at[n])
-                for n, (src, dst) in enumerate(
-                    (
-                        (gin_buf.at[nex - 1], gin_out.at[nex - 1]),
-                        (ggate_buf.at[nex - 1], ggate_out.at[ex]),
-                    )
-                )
-            ]
-
-        @pl.when(s == nex - 1)
+
+            @pl.when(t == (steps - 1 if first else nex + 1))
+            def _():
+                early_work.sum_y()
+                early_work.start_z()
+
+        @pl.when(t == nex)
         def _():
-            for copy in own:
-                copy.start()
-
-        def weight_grads(flush):
+            for work in works_y:
+                work.sum_y()
+                work.start_z()
+
+        def weight_grads(flush, which):
             def put(at, lanes, value):
                 if flush:
-                    value += acc_ref[at : at + D, lanes]
+                    value += acc_ref[which, at : at + D, lanes]
                 if flush < flushes - 1:
-                    acc_ref[at : at + D, lanes] = value
+                    acc_ref[which, at : at + D, lanes] = value
                 else:
-                    grad_ref[at : at + D, lanes] = value.astype(BF16)
-
-            def columns(part, carry):
-                begin = pl.multiple_of(part * wide, wide)
-                lanes = pl.ds(begin, wide)
-                put(0, lanes, dot(xt_ref[...], dg_ref[:, lanes]))
-                put(D, lanes, dot(xt_ref[...], du_ref[:, lanes]))
-                down = dot(dyt_ref[...], hid_ref[:, lanes])
-                for n in range(0, wide, D):
-                    put(2 * D, pl.ds(begin + n, D), down[:, n : n + D].T)
-                return carry
-
-            lax.fori_loop(0, FF // wide, columns, 0)
+                    grad_ref[which, at : at + D, lanes] = value.astype(BF16)
+
+            every = slice(0, wide)
+            put(0, every, dot(xt_ref[...], dg_ref[...]))
+            put(D, every, dot(xt_ref[...], du_ref[...]))
+            down = dot(dyt_ref[...], hid_ref[...])
+            for n in range(0, wide, D):
+                put(2 * D, slice(n, n + D), down[:, n : n + D].T)
+
+        def keep(which):
+            return pltpu.make_async_copy(grad_ref.at[which], own_outs[which], own_sem.at[which])
 
         for flush in range(flushes):
-            pl.when(s == (flush + 1) * batch - 1)(functools.partial(weight_grads, flush))
-
-        @pl.when(s == nex - 1)
+            for which in range(2):
+                end = (2 * flush + which + 1) * batch - 1
+                pl.when(t == end)(functools.partial(weight_grads, flush, which))
+
+        @pl.when(t == steps - batch - 1)
         def _():
-            if settle is not None:
-                settle.finish_y()
+            if inline:
+                work_own.start_y()
+            else:
+                keep(0).start()
+
+        @pl.when(t == steps - 1)
+        def _():
+            keep(1).start()
+            own = []
             if last:
-                scatter.finish(early_out)
+                own = [
+                    pltpu.make_async_copy(src, dst, loc.at[n])
+                    for n, (src, dst) in enumerate(
+                        (
+                            (gin_buf.at[nex - 1], gin_ref.at[nex - 1]),
+                            (ggate_buf.at[nex - 1], ggate_ref.at[ex]),
+                        )
+                    )
+                ]
+                for copy in own:
+                    copy.start()
+            if inline:
+                work_own.store_y(own_outs[0])
+            else:
+                keep(0).wait()
+            for work, out in zip(works_y + works_z, sum_outs):
+                work.finish_z(out)
+            if last:
+                early_work.finish_z(early_out)
                 for step in range(nex - 1):
                     for copy in copies(step):
                         copy.wait()
                 for copy in own:
                     copy.wait()
-
-    def per_source(*tail):
-        return pl.BlockSpec((1,) + tail, lambda s: (s,) + (0,) * len(tail))
+            keep(1).wait()
+
+    def source(t):
+        return (t // (2 * batch)) * batch + t % batch
+
+    def early_source(t):
+        half = (t // batch) % 2
+        return (t // (2 * batch)) * batch + (1 - half) * (t % batch) + half * (batch - 1)
+
+    def late_source(t):
+        return (t // (2 * batch)) * batch + ((t // batch) % 2) * (t % batch)
+
+    def per_source(which, *tail):
+        return pl.BlockSpec((1,) + tail, lambda t: (which(t),) + (0,) * len(tail))
 
     def whole(shape):
-        return pl.BlockSpec(shape, lambda s: (0,) * len(shape), pipeline_mode=pl.Buffered(1))
+        return pl.BlockSpec(shape, lambda t: (0,) * len(shape), pipeline_mode=pl.Buffered(1))
 
     def whole_out(shape):
-        return pl.BlockSpec(shape, lambda s: (0,) * len(shape))
-
+        return pl.BlockSpec(shape, lambda t: (0,) * len(shape))
+
+    dma = pltpu.SemaphoreType.DMA
+    kind = BF16 if last else F32
     inputs = [weights, act_all, cot_all, ranks, gates]
     in_specs = [
         whole(weights.shape),
-        per_source(rows, D),
-        per_source(rows, D),
-        per_source(local, rows),
-        per_source(local, rows),
+        per_source(early_source, rows, D),
+        per_source(early_source, rows, D),
+        per_source(source, local, rows),
+        per_source(source, local, rows),
     ]
-    if before is not None:
-        inputs += list(before)
-        in_specs += [per_source(rows, D), per_source(number, rows), per_source(rows, D)]
-    if talks:
-        inputs.append(early)
-        in_specs.append(whole(early.shape))
-    if settle is not None:
-        inputs.append(done)
-        in_specs.append(any_spec())
-    dma = pltpu.SemaphoreType.DMA
-    kind = BF16 if last else F32
     out_shape = [
         jax.ShapeDtypeStruct((nex, rows, D), kind),
         jax.ShapeDtypeStruct((nex, number + 1, rows), F32),
         jax.ShapeDtypeStruct((nex, rows, D), kind),
-        jax.ShapeDtypeStruct(weights.shape, BF16),
     ]
-    if last:
-        out_specs = [any_spec()] * 2
-    else:
-        out_specs = [per_source(rows, D), per_source(number + 1, rows)]
-    out_specs += [per_source(rows, D), whole_out(weights.shape)]
-    if talks:
+    out_specs = [
+        any_spec() if last else per_source(late_source, rows, D),
+        any_spec() if last else per_source(late_source, number + 1, rows),
+        per_source(late_source, rows, D),
+    ]
+    scratch = [
+        pltpu.VMEM((D, batch * CAP), BF16),
+        pltpu.VMEM((D, batch * CAP), BF16),
+        pltpu.VMEM((batch * CAP, wide), BF16),
+        pltpu.VMEM((batch * CAP, wide), BF16),
+        pltpu.VMEM((batch * CAP, wide), BF16),
+        pltpu.VMEM((FF, D), BF16),
+        pltpu.VMEM((batch, CAP, D), BF16),
+        pltpu.VMEM((batch, CAP, D), BF16),
+        pltpu.VMEM((batch, CAP, D), F32),
+        pltpu.VMEM((batch, CAP, D), F32),
+        pltpu.VMEM((2, 3 * D, wide), BF16),
+        dma((2,)),
+    ]
+    if before is not None:
+        inputs += list(before)
+        in_specs += [
+            per_source(late_source, rows, D),
+            per_source(late_source, number, rows),
+            per_source(late_source, rows, D),
+        ]
+    if scatter is not None:
+        inputs.append(early)
+        in_specs.append(whole(early.shape))
         shape = (ROW_PAD, 3 * FF) if last else scatter.spread_shape()
         out_shape.append(jax.ShapeDtypeStruct(shape, F32 if last else BF16))
         out_specs.append(whole_out(shape))
-    if settle is not None:
-        out_shape.append(jax.ShapeDtypeStruct((grid.nz,) + done.shape[1:], BF16))
+    inputs += list(ys) + list(zs)
+    in_specs += [any_spec()] * (len(ys) + len(zs))
+    own_shape = (grid.nz, shard_rows, wide) if inline else (3 * D, wide)
+    for shape in (own_shape, (3 * D, wide)):
+        out_shape.append(jax.ShapeDtypeStruct(shape, BF16))
         out_specs.append(any_spec())
-    scratch = [
-        pltpu.VMEM((D, batch * CAP), BF16),
-        pltpu.VMEM((D, batch * CAP), BF16),
-        pltpu.VMEM((batch * CAP, FF), BF16),
-        pltpu.VMEM((batch * CAP, FF), BF16),
-        pltpu.VMEM((batch * CAP, FF), BF16),
-        pltpu.VMEM((FF, D), BF16),
-    ]
+    for work in works_y + works_z:
+        out_shape.append(jax.ShapeDtypeStruct((work.rows, work.width), BF16))
+        out_specs.append(whole_out((work.rows, work.width)))
     if flushes > 1:
-        scratch.append(pltpu.VMEM(weights.shape, F32))
+        scratch.append(pltpu.VMEM((2, 3 * D, wide), F32))
     if last:
         scratch += [
             pltpu.VMEM((nex, rows, D), BF16),
@@ -1489,23 +1574,25 @@
         ]
     if first:
         scratch += scatter.scratch_x()
-    if last:
-        scratch += scatter.scratch_dp()
     if first and last:
         scratch.append(pltpu.VMEM(scatter.spread_shape(), BF16))
-    if settle is not None:
-        scratch += settle.scratch_y()
-    return pl.pallas_call(
+    if last:
+        scratch += early_work.scratch_y() + early_work.scratch_z()
+    for work in works_y:
+        scratch += work.scratch_y() + work.scratch_z()
+    for work in works_z:
+        scratch += work.scratch_own() + work.scratch_z()
+    if inline:
+        scratch += work_own.scratch_y()
+    results = pl.pallas_call(
         kernel,
-        grid=(nex,),
+        grid=(steps,),
         out_shape=tuple(out_shape),
         in_specs=in_specs,
         out_specs=tuple(out_specs),
         scratch_shapes=scratch,
         compiler_params=pltpu.CompilerParams(
-            vmem_limit_bytes=60 * MIB,
-            collective_id=5 + number if talks else None,
-            has_side_effects=talks,
+            vmem_limit_bytes=62 * MIB, collective_id=5 + number, has_side_effects=True
         ),
         cost_estimate=pl.CostEstimate(
             flops=nex * CAP * D * FF * 2 * 11,
@@ -1514,33 +1601,45 @@
         ),
         name="experts_step",
     )(*inputs)
-
-
-def middle_step(grid, gin, ggate, mixed, probs, lin, gact, act_across, heads, grad_out, small, gain, terms,
-                partial):
+    results = list(results)
+    sums = results[:3]
+    del results[:3]
+    if scatter is not None:
+        early = results.pop(0)
+    return sums, early, results[:2], results[2:]
+
+
+def middle_step(grid, gin, ggate, mixed, probs, lin, gact, act_across, heads, grad_out, small, gain, ys,
+                zs):
     ndp, nex, units = grid.ndp, grid.nex, grid.units
     local = EXPERTS // nex
-    settle = ShardScatter(grid, *terms.shape[1:])
-    settle_before = None if partial is None else ShardScatter(grid, *partial.shape[1:])
+    works_y = [ShardScatter(grid, *v.shape[1:]) for v in ys]
+    works_z = [ShardScatter(grid, *v.shape[1:]) for v in zs]
 
     def kernel(gin_ref, ggate_ref, mixed_ref, probs_ref, lin_ref, gact_ref, across_ref, heads_ref,
-               go_ref, small_ref, gain_ref, terms_ref, *refs):
+               go_ref, small_ref, gain_ref, *refs):
         refs = list(refs)
-        partial_ref = refs.pop(0) if settle_before is not None else None
-        dst, grad_mixed_ref, middle_ref, settle_out = refs[:4]
-        del refs[:4]
-        before_out = refs.pop(0) if settle_before is not None else None
-        flipped, buf, send, recv, loc = refs[:5]
-        settle_refs, before_refs = refs[5:9], refs[9:]
+
+        def take(count):
+            taken = refs[:count]
+            del refs[:count]
+            return taken
+
+        y_refs, z_refs = take(len(ys)), take(len(zs))
+        dst, grad_mixed_ref, middle_ref = take(3)
+        y_outs, z_outs = take(len(ys)), take(len(zs))
+        flipped, buf, send, recv, loc = take(5)
+        for work, ref in zip(works_y, y_refs):
+            work.bind_y(ref, take(4))
+        for work, ref in zip(works_z, z_refs):
+            work.bind_own(ref, take(2))
+            work.bind_z(take(2))
         dp, ex = lax.axis_index("dp"), lax.axis_index("expert")
         greet([(lax.rem(dp + d, ndp), ex) for d in range(1, ndp)])
-        settle.bind(terms_ref)
-        settle.bind_y(settle_out, settle_refs)
-        settle.start_y()
-        if settle_before is not None:
-            settle_before.bind(partial_ref)
-            settle_before.bind_z(before_refs)
-            settle_before.start_z()
+        for work in works_y:
+            work.start_y()
+        for work in works_z:
+            work.start_z()
 
         grad_out = go_ref[...].astype(F32)
         probs = probs_ref[...]
@@ -1607,38 +1706,40 @@
         lane = lax.broadcasted_iota(jnp.int32, misc_grad.shape, 1)
         misc_grad = jnp.where(lane == EXPERTS + 2, gain_column, misc_grad)
         middle_ref[:, D:] = misc_grad.astype(BF16)
-        settle.finish_y()
+        for work, out in zip(works_y, y_outs):
+            work.store_y(out)
         for copy in copies:
             copy.wait()
-        if settle_before is not None:
-            settle_before.finish_z(before_out)
+        for work, out in zip(works_z, z_outs):
+            work.finish_z(out)
 
     dma = pltpu.SemaphoreType.DMA
     vmem = pl.BlockSpec(memory_space=pltpu.VMEM)
     hbm = pl.BlockSpec(memory_space=pltpu.HBM)
     inputs = [gin, ggate, mixed, probs, lin, gact, act_across, heads, grad_out, small, gain]
-    in_specs = [vmem] * len(inputs) + [any_spec()]
+    in_specs = [vmem] * len(inputs) + [any_spec()] * (len(ys) + len(zs))
     out_shape = [
         jax.ShapeDtypeStruct((units, HEAD_DIM, SEG * ndp), BF16),
         jax.ShapeDtypeStruct((TOK_DEV, D), F32),
         jax.ShapeDtypeStruct((D, D + MISC), BF16),
-        jax.ShapeDtypeStruct((grid.nz,) + terms.shape[1:], BF16),
     ]
-    out_specs = [any_spec(), vmem, vmem, hbm]
+    out_specs = [any_spec(), vmem, vmem]
     scratch = [
         pltpu.VMEM((MISC, TOK_DEV), F32),
         pltpu.VMEM((units * ndp, HEAD_DIM, SEG), BF16),
         dma((ndp - 1,)),
         dma((ndp - 1,)),
         dma,
-    ] + settle.scratch_y()
-    inputs.append(terms)
-    if settle_before is not None:
-        inputs.append(partial)
-        in_specs.append(any_spec())
-        out_shape.append(jax.ShapeDtypeStruct(partial.shape[1:], BF16))
+    ]
+    inputs += list(ys) + list(zs)
+    for work in works_y:
+        out_shape.append(jax.ShapeDtypeStruct((grid.nz, work.rows, work.width), BF16))
+        out_specs.append(hbm)
+        scratch += work.scratch_y()
+    for work in works_z:
+        out_shape.append(jax.ShapeDtypeStruct((work.rows, work.width), BF16))
         out_specs.append(vmem)
-        scratch += settle_before.scratch_z()
+        scratch += work.scratch_own() + work.scratch_z()
     return pl.pallas_call(
         kernel,
         out_shape=tuple(out_shape),
@@ -1734,28 +1835,31 @@
      gains) = route_rows(
         grid, heads_here, tokens, dense_all, grad_out_low, rest.reshape(grid.ndev * ROW_PAD, -1)
     )
-    before, terms, partial = None, None, None
+    before, ys, zs, halves = None, [], [], []
     for e in range(local_experts):
-        results = experts_step(
-            grid, e, expert_all[e], act_all, cot_all, rank_all, gates_all, before, early, terms
+        before, early, own, sums = experts_step(
+            grid, e, expert_all[e], act_all, cot_all, rank_all, gates_all, before, early, ys, zs
         )
-        before, early = results[:3], results[4]
-        terms = results[3].reshape(ndp, shard_rows, FF)
-        partial = results[5] if e else None
+        halves += sums[::-1] if zs else sums
+        ys = [v.reshape(ndp, shard_rows, FF // 2) for v in own if v.ndim == 2]
+        zs = [v for v in own if v.ndim == 3]
     gin_back, ggate_back, routed_parts = before
 
-    grad_heads, grad_mixed, middle, partial, *expert_sums = middle_step(
+    grad_heads, grad_mixed, middle, *more = middle_step(
         grid, gin_back, ggate_back, mixed_rows, probs, shared_lin, grad_act_shared, act_across,
-        heads_here, grad_out_low, small, gains, terms, partial,
+        heads_here, grad_out_low, small, gains, ys, zs,
     )
-
-    output, grad_tokens, dense_table, last_sum = attend_back(
+    halves += more[len(ys) :]
+
+    output, grad_tokens, dense_table, *sums = attend_back(
         grid, lengths, tok_all, act_one, qkv_rows, query, key, value, lse, grad_heads, cosine, sine,
-        middle, routed_parts, partial, tokens, mixed_rows, grad_mixed, probs, shared_lin, gains, early,
+        middle, routed_parts, more[: len(ys)], tokens, mixed_rows, grad_mixed, probs, shared_lin, gains, early,
     )
     dense_grad = dense_table[:rows_dev, : dense_weights.shape[0] // rows_dev].reshape(-1)
-    expert_sums.append(last_sum)
-    expert_sums = jnp.stack(expert_sums)
+    halves += sums
+    expert_sums = jnp.stack(
+        [jnp.concatenate(halves[e : e + 2], axis=1) for e in range(0, 2 * local_experts, 2)]
+    )
     unmixed = jnp.einsum("erg,fg->erf", expert_sums, mix, preferred_element_type=F32)
     expert_grad = jnp.where(is_down, expert_sums.astype(F32), unmixed)
     expert_grad = expert_grad.reshape(expert_weights.shape)

time: 444 us -> 410 us (0.923)
  Pallas kernels: 392 us -> 358 us
    pallas_call x1, Pallas kernels: 85.9 us -> 67 us  [attend_back(): pl.pallas_call(kernel, grid=(units,), out_shape=(jax.ShapeDtypeStruct((TO...]
    pallas_call x1, Pallas kernels: 58 us -> 39.6 us  [middle_step(): pl.pallas_call(kernel, out_shape=tuple(out_shape), in_specs=in_specs, out...]
  transfers between devices with their start and end apart: 2 -> 2, of which waited for: 0 -> 0; matrix products, arithmetic and copies ran while one was open for 1% -> 1% of each run, Pallas kernels for 42% -> 47%
where the time goes in v5:
time: 410 us; the launch traced here: 404 us
  Pallas kernels  358 us (87%)
  other arithmetic  15.1 us (4%)
  between operations  14.9 us (4%)
  local copies, waits for them, and re-layouts  9.98 us (2%)
  matrix products  4.36 us (1%)
    pallas_call x2, Pallas kernels, experts_step(): pl.pallas_call(kernel, grid=(steps,), out_shape=tuple(out_shape), in_spec...  113 us
    pallas_call x1, Pallas kernels, attend_back(): pl.pallas_call(kernel, grid=(units,), out_shape=(jax.ShapeDtypeStruct((TO...  67 us
    pallas_call x1, Pallas kernels, attend(): pl.pallas_call(kernel, grid=(units,), out_shape=(jax.ShapeDtypeStruct((nd...  66.5 us
    pallas_call x1, Pallas kernels, first_exchange(): pl.pallas_call(kernel, out_shape=(jax.ShapeDtypeStruct((grid.slots, ndp,...  47.3 us
    pallas_call x1, Pallas kernels, middle_step(): pl.pallas_call(kernel, out_shape=tuple(out_shape), in_specs=in_specs, out...  39.6 us
    pallas_call x1, Pallas kernels, route_rows(): pl.pallas_call(kernel, out_shape=(jax.ShapeDtypeStruct((nex, TOK_DEV, D),...  25.4 us
    add x2, other arithmetic, adamw_update(): average_new = average_keep * average + (1.0 - average_keep) * weights_new  10.1 us
  transfers between devices with their start and end apart: 2, of which 0 were waited for; matrix products, arithmetic and copies ran while one was open for 1% of the time, Pallas kernels for 47%

profile of v5, /device:TPU:0, one launch (start us, length us, event | category | flops | bytes accessed | tf_op | source)
XLA Modules:
  0.0 403.6 jit_solution(7913491042439696719)
XLA Ops:
  7.2 0.0 all-gather.7.cloned.1.call-start
  7.3 1.8 convert_element_type.53
  9.1 1.9 fusion.19
  11.0 0.0 copy-start.5
  11.0 0.0 copy-start.16
  11.0 1.0 fusion.44
  12.0 0.0 all-gather.7.cloned.1.call-update
  12.0 0.0 all-gather.5.cloned.1.call-start
  12.1 0.7 all-gather.5.cloned.1.call-update
  12.8 0.2 reshape.140
  13.0 0.1 slice.34
  13.1 0.1 slice.36
  13.3 0.3 fusion.24
  13.6 0.6 reshape.142.rank_in
  14.2 0.1 concatenate.9
  14.3 0.6 pad.8.shd
  14.9 0.7 pad.9.shard_ref
  15.6 0.1 compare_convert_fusion
  15.7 1.0 multiply_convert_fusion
  16.7 47.3 %first_exchange.1 = (bf16[2,8,128,384]{3,2,1,0:T(8,128)(2,1)}, bf16[32,16,1664]{2,1,0:T(8,128)(2,1)}, bf16[4,768,384]{2,1,0:T(8,128)(2,1)}, f32[4,2,768]{2,1,0:T(2,128)}) custom-call(bf16[6,128,384]{2,1,0:T(8,128)(2,1)} %refs_12_.1, bf16[16,1664]{1,0:T(8,128)(2,1)} %pad.8.shd, bf16[768,384]{1,0:T(8,128)(2,1)} %bitcast.47, f32[4,2,768]{2,1,0:T(2,128)} %reshape.142.rank_in), custom_call_target="tpu_custom_call" | custom-call | tf_op jit(solution)/shard_map/first_exchange/pallas_call | solution.py:401
  64.1 1.0 multiply_sine_fusion
  65.0 66.5 %attend.1 = (bf16[8,9,32,128]{3,2,1,0:T(8,128)(2,1)}, bf16[32,16,4608]{2,1,0:T(8,128)(2,1)}, bf16[2,1024,384]{2,1,0:T(8,128)(2,1)}, bf16[9,32,1024]{2,1,0:T(8,12...) custom-call(s32[6]{0:T(128)} %refs_0_.1, ...), custom_call_target="tpu_custom_call" | custom-call | flops 4831838208 | bytes 8388608 | tf_op jit(solution)/shard_map/attend/pallas_call | solution.py:913
  131.6 25.4 %route_rows.1 = (bf16[4,768,384]{2,1,0:T(8,128)(2,1)}, f32[4,2,768]{2,1,0:T(2,128)}, f32[768,384]{1,0:T(8,128)}, f32[768,128]{1,0:T(8,128)}, f32[768,384]{1,0:T(...) custom-call(bf16[72,32,128]{2,1,0:T(8,128)(2,1)} %bitcast.53, ...), custom_call_target="tpu_custom_call" | custom-call | tf_op jit(solution)/shard_map/route_rows/pallas_call | solution.py:746
  157.0 0.0 all-gather.7.cloned.1.call-done
  157.0 51.1 %experts_step.2 = (f32[4,768,384]{2,1,0:T(8,128)}, f32[4,1,768]{2,1,0:T(1,128)}, f32[4,768,384]{2,1,0:T(8,128)}, bf16[128,4608]{1,0:T(8,128)(2,1)}, bf16[4,144,7...) custom-call(bf16[1152,1536]{1,0:T(8,128)(2,1)} %bitcast.64, bf16[4,768,384]{2,1,0:T(8,128)(2,1)} %get-tuple-element.67.refs_1_, ...), custom_call_target="tpu_custom_call" | custom-call | flops 19931332608 | bytes 26214400 | tf_op jit(solution)/shard_map/experts_step/pallas_call | solution.py:1587
  208.1 0.0 all-gather.5.cloned.1.call-done
  208.1 61.5 %experts_step.3 = (bf16[4,768,384]{2,1,0:T(8,128)(2,1)}, f32[4,2,768]{2,1,0:T(2,128)}, bf16[4,768,384]{2,1,0:T(8,128)(2,1)}, f32[16,4608]{1,0:T(8,128)}, bf16[4,...) custom-call(bf16[1152,1536]{1,0:T(8,128)(2,1)} %bitcast.63, ...), custom_call_target="tpu_custom_call" | custom-call | flops 19931332608 | bytes 26214400 | tf_op jit(solution)/shard_map/experts_step/pallas_call | solution.py:1587
  269.6 39.6 %middle_step.1 = (bf16[9,32,1024]{2,1,0:T(8,128)(2,1)}, f32[768,384]{1,0:T(8,128)}, bf16[384,512]{1,0:T(8,128)(2,1)}, bf16[4,144,768]{2,1,0:T(8,128)(2,1)}, bf16[144,768]{1,0:T(8,128)(2,1)}) custom-call(bf16[4,768,384]{2,1,0:T(8,128)(2,1)} %get-tuple-element.78.gin_ref, f32[4,2,768]{2,1,0:T(2,128)} %get-tuple-element.79.ggate_ref, ...), custom_call_target="tpu_custom_call" | custom-call | tf_op jit(solution)/shard_map/middle_step/pallas_call | solution.py:1743
  309.2 67.0 %attend_back.1 = (bf16[768,384]{1,0:T(8,128)(2,1)}, f32[768,384]{1,0:T(8,128)}, f32[16,6272]{1,0:T(8,128)}, bf16[144,768]{1,0:T(8,128)(2,1)}) custom-call(s32[6]{0:T(128)} %refs_0_.1, bf16[2,1024,384]{2,1,0:T(8,128)(2,1)} %bitcast.67, bf16[2,1024,384]{2,1,0:T(8,128)(2,1)} %get-tuple-element.59.refs_2_, bf16[1280,384]{1,0:T(8,128)(2,1)} %get-tuple-element.60.refs_3_, ...), custom_call_target="tpu_custom_call" | custom-call | flops 12079595520 | bytes 12582912 | tf_op jit(solution)/shard_map/attend_back/pallas_call | solution.py:1187
  376.3 1.2 reshape.154
  377.4 0.0 copy-start.6
  377.5 1.1 maximum_bitcast_fusion
  378.6 0.0 copy-start.10
  378.6 0.0 copy-start.11
  378.6 0.0 copy-start.12
  378.6 0.0 copy-start.4
  378.6 2.1 fusion.10
  380.8 0.0 copy-start.2
  380.8 0.0 copy-start.3
  380.8 1.4 copy.26
  382.2 0.0 copy-start
  382.2 0.0 copy-start.1
  382.2 1.2 multiply_add_fusion.3
  383.4 1.5 copy-done.1
  384.9 8.9 %multiply_add_fusion.1 = (f32[2,221184]{1,0:T(2,128)}, f32[2,221184]{1,0:T(2,128)}, f32[2,221184]{1,0:T(2,128)}, f32[2,221184]{1,0:T(2,128)}) fusion(f32[2,221184]{1,0:T(2,128)S(1)} %copy-done.2, f32[2,221184]{1,0:T(2,128)S(1)} %copy-done.1, f32[2,221184]{1,0:T(2,128)S(1)} %bitcast.50, f32[2,221184]{1,0:T(2,128)S(1)} %copy-done.3, f32[2,221184]{1,0:T(2,128)S(1)} %copy-done.4), kind=kLoop, calls=%fused_computation.16 | loop fusion | flops 7520256 | bytes 15925248 | tf_op jit(solution)/shard_map/add | solution.py:51
  393.8 0.8 copy.33
  394.6 0.7 copy-done.7
  395.3 1.0 copy.34
  (34 shorter events, 0.1 us)
Async XLA Ops:
  7.2 149.8 %all-gather.7.cloned.1.call-start = ((), (), s32[]{:S(2)}) async-start(), calls=%async_computation.1 | async-start | bytes 3981312 | tf_op jit(solution)/shard_map/all_gather | solution.py:1819
  11.0 1.8 copy-start.5
  11.0 2.2 copy-start.16
  12.0 3.6 copy-start.17
  12.0 3.7 copy-start.8
  12.0 196.1 %all-gather.5.cloned.1.call-start = ((), (), s32[]{:S(2)}) async-start(), calls=%async_computation | async-start | bytes 3981312 | tf_op jit(solution)/shard_map/all_gather | solution.py:1819
  309.2 68.2 %copy-start.13 = (bf16[144,768]{1,0:T(8,128)(2,1)S(1)}, bf16[144,768]{1,0:T(8,128)(2,1)}, u32[]{:S(2)}) copy-start(bf16[144,768]{1,0:T(8,128)(2,1)} %get-tuple-element.99) | copy-start | bytes 663556
  309.2 68.2 %copy-start.14 = (bf16[144,768]{1,0:T(8,128)(2,1)S(1)}, bf16[144,768]{1,0:T(8,128)(2,1)}, u32[]{:S(2)}) copy-start(bf16[144,768]{1,0:T(8,128)(2,1)} %get-tuple-element.98) | copy-start | bytes 663556
  309.2 68.2 %copy-start.15 = (bf16[144,768]{1,0:T(8,128)(2,1)S(1)}, bf16[144,768]{1,0:T(8,128)(2,1)}, u32[]{:S(2)}) copy-start(bf16[144,768]{1,0:T(8,128)(2,1)} %get-tuple-element.100) | copy-start | bytes 663556
  377.4 4.7 %copy-start.6 = (f32[73860]{0:T(1024)}, f32[73860]{0:T(1024)S(1)}, u32[]{:S(2)}) copy-start(f32[73860]{0:T(1024)S(1)} %reshape.154) | copy-start | bytes 886324
  378.6 3.6 copy-start.10
  378.6 3.6 copy-start.11
  378.6 3.6 copy-start.12
  378.6 4.8 %copy-start.4 = (f32[2,221184]{1,0:T(2,128)S(1)}, f32[2,221184]{1,0:T(2,128)}, u32[]{:S(2)}) copy-start(f32[2,221184]{1,0:T(2,128)} %param.21) | copy-start | bytes 5308420
  380.8 2.7 copy-start.2
  380.8 2.7 copy-start.3
  382.2 11.6 %copy-start = (f32[1,2,144,1536]{3,1,2,0:T(2,128)}, f32[1,2,144,1536]{3,1,2,0:T(2,128)S(1)}, u32[]{:S(2)}) copy-start(f32[1,2,144,1536]{3,1,2,0:T(2,128)S(1)} %copy.26) | copy-start | bytes 5308420
  382.2 2.7 copy-start.1
  384.9 8.9 %copy-start.9 = (bf16[768,384]{1,0:T(8,128)(2,1)S(1)}, bf16[768,384]{1,0:T(8,128)(2,1)}, u32[]{:S(2)}) copy-start(bf16[768,384]{1,0:T(8,128)(2,1)} %get-tuple-element.95) | copy-start | bytes 1769476
  393.8 1.5 copy-start.7
Sparse Core Ops, SparseCore 0:
  12.1 109.6 all-gather.6
  124.6 64.0 all-gather.4

commit v6 on v5

--- a/solution.py
+++ b/solution.py
@@ -1402,11 +1402,11 @@
 
         if first:
 
-            @pl.when(t == 0)
+            @pl.when(t == 1)
             def _():
                 scatter.along_x()
 
-            @pl.when(t == nex)
+            @pl.when(t == nex + 2)
             def _():
                 scatter.after_x()
                 if last:

time: 410 us -> 406 us (level)
  no operation moved by 1% of the time
where the time goes in v6:
time: 406 us; the launch traced here: 400 us
  Pallas kernels  355 us (87%)
  other arithmetic  15.1 us (4%)
  between operations  14.9 us (4%)
  local copies, waits for them, and re-layouts  9.98 us (2%)
  matrix products  4.37 us (1%)
    pallas_call x2, Pallas kernels, experts_step(): pl.pallas_call(kernel, grid=(steps,), out_shape=tuple(out_shape), in_spec...  110 us
    pallas_call x1, Pallas kernels, attend_back(): pl.pallas_call(kernel, grid=(units,), out_shape=(jax.ShapeDtypeStruct((TO...  66.6 us
    pallas_call x1, Pallas kernels, attend(): pl.pallas_call(kernel, grid=(units,), out_shape=(jax.ShapeDtypeStruct((nd...  66.5 us
    pallas_call x1, Pallas kernels, first_exchange(): pl.pallas_call(kernel, out_shape=(jax.ShapeDtypeStruct((grid.slots, ndp,...  47.3 us
    pallas_call x1, Pallas kernels, middle_step(): pl.pallas_call(kernel, out_shape=tuple(out_shape), in_specs=in_specs, out...  39.1 us
    pallas_call x1, Pallas kernels, route_rows(): pl.pallas_call(kernel, out_shape=(jax.ShapeDtypeStruct((nex, TOK_DEV, D),...  25.4 us
    add x2, other arithmetic, adamw_update(): average_new = average_keep * average + (1.0 - average_keep) * weights_new  10.1 us
  transfers between devices with their start and end apart: 2, of which 0 were waited for; matrix products, arithmetic and copies ran while one was open for 1% of the time, Pallas kernels for 47%

profile of v6, /device:TPU:0, one launch (start us, length us, event | category | flops | bytes accessed | tf_op | source)
XLA Modules:
  0.0 399.9 jit_solution(6992651873845725304)
XLA Ops:
  7.2 0.0 all-gather.7.cloned.1.call-start
  7.3 1.8 convert_element_type.53
  9.1 1.9 fusion.19
  11.0 0.0 copy-start.5
  11.0 0.0 copy-start.16
  11.0 1.0 fusion.44
  12.0 0.0 all-gather.7.cloned.1.call-update
  12.0 0.0 all-gather.5.cloned.1.call-start
  12.1 0.7 all-gather.5.cloned.1.call-update
  12.8 0.2 reshape.140
  13.0 0.1 slice.34
  13.1 0.1 slice.36
  13.3 0.3 fusion.24
  13.6 0.6 reshape.142.rank_in
  14.2 0.1 concatenate.9
  14.3 0.6 pad.8.shd
  14.9 0.7 pad.9.shard_ref
  15.6 0.1 compare_convert_fusion
  15.7 1.0 multiply_convert_fusion
  16.7 47.3 %first_exchange.1 = (bf16[2,8,128,384]{3,2,1,0:T(8,128)(2,1)}, bf16[32,16,1664]{2,1,0:T(8,128)(2,1)}, bf16[4,768,384]{2,1,0:T(8,128)(2,1)}, f32[4,2,768]{2,1,0:T(2,128)}) custom-call(bf16[6,128,384]{2,1,0:T(8,128)(2,1)} %refs_12_.1, bf16[16,1664]{1,0:T(8,128)(2,1)} %pad.8.shd, bf16[768,384]{1,0:T(8,128)(2,1)} %bitcast.47, f32[4,2,768]{2,1,0:T(2,128)} %reshape.142.rank_in), custom_call_target="tpu_custom_call" | custom-call | tf_op jit(solution)/shard_map/first_exchange/pallas_call | solution.py:401
  64.1 1.0 multiply_sine_fusion
  65.0 66.5 %attend.1 = (bf16[8,9,32,128]{3,2,1,0:T(8,128)(2,1)}, bf16[32,16,4608]{2,1,0:T(8,128)(2,1)}, bf16[2,1024,384]{2,1,0:T(8,128)(2,1)}, bf16[9,32,1024]{2,1,0:T(8,12...) custom-call(s32[6]{0:T(128)} %refs_0_.1, ...), custom_call_target="tpu_custom_call" | custom-call | flops 4831838208 | bytes 8388608 | tf_op jit(solution)/shard_map/attend/pallas_call | solution.py:913
  131.6 25.4 %route_rows.1 = (bf16[4,768,384]{2,1,0:T(8,128)(2,1)}, f32[4,2,768]{2,1,0:T(2,128)}, f32[768,384]{1,0:T(8,128)}, f32[768,128]{1,0:T(8,128)}, f32[768,384]{1,0:T(...) custom-call(bf16[72,32,128]{2,1,0:T(8,128)(2,1)} %bitcast.53, ...), custom_call_target="tpu_custom_call" | custom-call | tf_op jit(solution)/shard_map/route_rows/pallas_call | solution.py:746
  157.0 0.0 all-gather.7.cloned.1.call-done
  157.0 47.6 %experts_step.2 = (f32[4,768,384]{2,1,0:T(8,128)}, f32[4,1,768]{2,1,0:T(1,128)}, f32[4,768,384]{2,1,0:T(8,128)}, bf16[128,4608]{1,0:T(8,128)(2,1)}, bf16[4,144,7...) custom-call(bf16[1152,1536]{1,0:T(8,128)(2,1)} %bitcast.64, bf16[4,768,384]{2,1,0:T(8,128)(2,1)} %get-tuple-element.67.refs_1_, ...), custom_call_target="tpu_custom_call" | custom-call | flops 19931332608 | bytes 26214400 | tf_op jit(solution)/shard_map/experts_step/pallas_call | solution.py:1587
  204.6 0.0 all-gather.5.cloned.1.call-done
  204.6 62.2 %experts_step.3 = (bf16[4,768,384]{2,1,0:T(8,128)(2,1)}, f32[4,2,768]{2,1,0:T(2,128)}, bf16[4,768,384]{2,1,0:T(8,128)(2,1)}, f32[16,4608]{1,0:T(8,128)}, bf16[4,...) custom-call(bf16[1152,1536]{1,0:T(8,128)(2,1)} %bitcast.63, ...), custom_call_target="tpu_custom_call" | custom-call | flops 19931332608 | bytes 26214400 | tf_op jit(solution)/shard_map/experts_step/pallas_call | solution.py:1587
  266.8 39.1 %middle_step.1 = (bf16[9,32,1024]{2,1,0:T(8,128)(2,1)}, f32[768,384]{1,0:T(8,128)}, bf16[384,512]{1,0:T(8,128)(2,1)}, bf16[4,144,768]{2,1,0:T(8,128)(2,1)}, bf16[144,768]{1,0:T(8,128)(2,1)}) custom-call(bf16[4,768,384]{2,1,0:T(8,128)(2,1)} %get-tuple-element.78.gin_ref, f32[4,2,768]{2,1,0:T(2,128)} %get-tuple-element.79.ggate_ref, ...), custom_call_target="tpu_custom_call" | custom-call | tf_op jit(solution)/shard_map/middle_step/pallas_call | solution.py:1743
  306.0 66.6 %attend_back.1 = (bf16[768,384]{1,0:T(8,128)(2,1)}, f32[768,384]{1,0:T(8,128)}, f32[16,6272]{1,0:T(8,128)}, bf16[144,768]{1,0:T(8,128)(2,1)}) custom-call(s32[6]{0:T(128)} %refs_0_.1, bf16[2,1024,384]{2,1,0:T(8,128)(2,1)} %bitcast.67, bf16[2,1024,384]{2,1,0:T(8,128)(2,1)} %get-tuple-element.59.refs_2_, bf16[1280,384]{1,0:T(8,128)(2,1)} %get-tuple-element.60.refs_3_, ...), custom_call_target="tpu_custom_call" | custom-call | flops 12079595520 | bytes 12582912 | tf_op jit(solution)/shard_map/attend_back/pallas_call | solution.py:1187
  372.6 1.2 reshape.154
  373.7 0.0 copy-start.6
  373.8 1.1 maximum_bitcast_fusion
  374.9 0.0 copy-start.10
  374.9 0.0 copy-start.11
  374.9 0.0 copy-start.12
  374.9 0.0 copy-start.4
  374.9 2.1 fusion.10
  377.1 0.0 copy-start.2
  377.1 0.0 copy-start.3
  377.1 1.4 copy.26
  378.5 0.0 copy-start
  378.5 0.0 copy-start.1
  378.5 1.2 multiply_add_fusion.3
  379.8 1.5 copy-done.1
  381.2 8.9 %multiply_add_fusion.1 = (f32[2,221184]{1,0:T(2,128)}, f32[2,221184]{1,0:T(2,128)}, f32[2,221184]{1,0:T(2,128)}, f32[2,221184]{1,0:T(2,128)}) fusion(f32[2,221184]{1,0:T(2,128)S(1)} %copy-done.2, f32[2,221184]{1,0:T(2,128)S(1)} %copy-done.1, f32[2,221184]{1,0:T(2,128)S(1)} %bitcast.50, f32[2,221184]{1,0:T(2,128)S(1)} %copy-done.3, f32[2,221184]{1,0:T(2,128)S(1)} %copy-done.4), kind=kLoop, calls=%fused_computation.16 | loop fusion | flops 7520256 | bytes 15925248 | tf_op jit(solution)/shard_map/add | solution.py:51
  390.1 0.8 copy.33
  391.0 0.7 copy-done.7
  391.6 1.0 copy.34
  (34 shorter events, 0.1 us)
Async XLA Ops:
  7.2 149.8 %all-gather.7.cloned.1.call-start = ((), (), s32[]{:S(2)}) async-start(), calls=%async_computation.1 | async-start | bytes 3981312 | tf_op jit(solution)/shard_map/all_gather | solution.py:1819
  11.0 1.8 copy-start.5
  11.0 2.2 copy-start.16
  12.0 3.6 copy-start.17
  12.0 3.7 copy-start.8
  12.0 192.6 %all-gather.5.cloned.1.call-start = ((), (), s32[]{:S(2)}) async-start(), calls=%async_computation | async-start | bytes 3981312 | tf_op jit(solution)/shard_map/all_gather | solution.py:1819
  305.9 67.8 %copy-start.13 = (bf16[144,768]{1,0:T(8,128)(2,1)S(1)}, bf16[144,768]{1,0:T(8,128)(2,1)}, u32[]{:S(2)}) copy-start(bf16[144,768]{1,0:T(8,128)(2,1)} %get-tuple-element.99) | copy-start | bytes 663556
  305.9 67.8 %copy-start.14 = (bf16[144,768]{1,0:T(8,128)(2,1)S(1)}, bf16[144,768]{1,0:T(8,128)(2,1)}, u32[]{:S(2)}) copy-start(bf16[144,768]{1,0:T(8,128)(2,1)} %get-tuple-element.98) | copy-start | bytes 663556
  305.9 67.8 %copy-start.15 = (bf16[144,768]{1,0:T(8,128)(2,1)S(1)}, bf16[144,768]{1,0:T(8,128)(2,1)}, u32[]{:S(2)}) copy-start(bf16[144,768]{1,0:T(8,128)(2,1)} %get-tuple-element.100) | copy-start | bytes 663556
  373.7 4.7 %copy-start.6 = (f32[73860]{0:T(1024)}, f32[73860]{0:T(1024)S(1)}, u32[]{:S(2)}) copy-start(f32[73860]{0:T(1024)S(1)} %reshape.154) | copy-start | bytes 886324
  374.9 3.6 copy-start.10
  374.9 3.6 copy-start.11
  374.9 3.6 copy-start.12
  374.9 4.8 %copy-start.4 = (f32[2,221184]{1,0:T(2,128)S(1)}, f32[2,221184]{1,0:T(2,128)}, u32[]{:S(2)}) copy-start(f32[2,221184]{1,0:T(2,128)} %param.21) | copy-start | bytes 5308420
  377.1 2.7 copy-start.2
  377.1 2.7 copy-start.3
  378.5 11.6 %copy-start = (f32[1,2,144,1536]{3,1,2,0:T(2,128)}, f32[1,2,144,1536]{3,1,2,0:T(2,128)S(1)}, u32[]{:S(2)}) copy-start(f32[1,2,144,1536]{3,1,2,0:T(2,128)S(1)} %copy.26) | copy-start | bytes 5308420
  378.5 2.7 copy-start.1
  381.2 8.9 %copy-start.9 = (bf16[768,384]{1,0:T(8,128)(2,1)S(1)}, bf16[768,384]{1,0:T(8,128)(2,1)}, u32[]{:S(2)}) copy-start(bf16[768,384]{1,0:T(8,128)(2,1)} %get-tuple-element.95) | copy-start | bytes 1769476
  390.1 1.5 copy-start.7
Sparse Core Ops, SparseCore 0:
  12.1 109.6 all-gather.6
  124.6 64.0 all-gather.4

commit v7 on v6

--- a/solution.py
+++ b/solution.py
@@ -790,8 +790,8 @@
 
 def allowed_mask(extent, block, length):
     keys = lax.broadcasted_iota(jnp.int32, (extent, QBLOCK), 0)
-    queries = lax.broadcasted_iota(jnp.int32, (extent, QBLOCK), 1) + block * QBLOCK
-    return (keys <= queries) & (keys < length)
+    queries = lax.broadcasted_iota(jnp.int32, (1, QBLOCK), 1) + block * QBLOCK
+    return keys <= jnp.minimum(queries, length - 1)
 
 
 def attend(grid, lengths, tok, table, cosine, sine, shard):

time: 406 us -> 407 us (level)
  no operation moved by 1% of the time
where the time goes in v7:
time: 407 us; the launch traced here: 400 us
  Pallas kernels  355 us (87%)
  other arithmetic  15.1 us (4%)
  between operations  14.9 us (4%)
  local copies, waits for them, and re-layouts  9.98 us (2%)
  matrix products  4.37 us (1%)
    pallas_call x2, Pallas kernels, experts_step(): pl.pallas_call(kernel, grid=(steps,), out_shape=tuple(out_shape), in_spec...  110 us
    pallas_call x1, Pallas kernels, attend_back(): pl.pallas_call(kernel, grid=(units,), out_shape=(jax.ShapeDtypeStruct((TO...  67.1 us
    pallas_call x1, Pallas kernels, attend(): pl.pallas_call(kernel, grid=(units,), out_shape=(jax.ShapeDtypeStruct((nd...  66.8 us
    pallas_call x1, Pallas kernels, first_exchange(): pl.pallas_call(kernel, out_shape=(jax.ShapeDtypeStruct((grid.slots, ndp,...  47.3 us
    pallas_call x1, Pallas kernels, middle_step(): pl.pallas_call(kernel, out_shape=tuple(out_shape), in_specs=in_specs, out...  39.1 us
    pallas_call x1, Pallas kernels, route_rows(): pl.pallas_call(kernel, out_shape=(jax.ShapeDtypeStruct((nex, TOK_DEV, D),...  25.4 us
    add x2, other arithmetic, adamw_update(): average_new = average_keep * average + (1.0 - average_keep) * weights_new  10.1 us
  transfers between devices with their start and end apart: 2, of which 0 were waited for; matrix products, arithmetic and copies ran while one was open for 1% of the time, Pallas kernels for 47%

profile of v7, /device:TPU:0, one launch (start us, length us, event | category | flops | bytes accessed | tf_op | source)
XLA Modules:
  0.0 400.4 jit_solution(7020904990406832844)
XLA Ops:
  7.2 0.0 all-gather.7.cloned.1.call-start
  7.3 1.8 convert_element_type.53
  9.1 1.9 fusion.19
  11.0 0.0 copy-start.5
  11.0 0.0 copy-start.16
  11.0 1.0 fusion.44
  12.0 0.0 all-gather.7.cloned.1.call-update
  12.0 0.0 all-gather.5.cloned.1.call-start
  12.1 0.7 all-gather.5.cloned.1.call-update
  12.8 0.2 reshape.140
  13.0 0.1 slice.34
  13.1 0.1 slice.36
  13.3 0.3 fusion.24
  13.6 0.6 reshape.142.rank_in
  14.2 0.1 concatenate.9
  14.3 0.6 pad.8.shd
  14.9 0.7 pad.9.shard_ref
  15.6 0.1 compare_convert_fusion
  15.7 1.0 multiply_convert_fusion
  16.7 47.3 %first_exchange.1 = (bf16[2,8,128,384]{3,2,1,0:T(8,128)(2,1)}, bf16[32,16,1664]{2,1,0:T(8,128)(2,1)}, bf16[4,768,384]{2,1,0:T(8,128)(2,1)}, f32[4,2,768]{2,1,0:T(2,128)}) custom-call(bf16[6,128,384]{2,1,0:T(8,128)(2,1)} %refs_12_.1, bf16[16,1664]{1,0:T(8,128)(2,1)} %pad.8.shd, bf16[768,384]{1,0:T(8,128)(2,1)} %bitcast.47, f32[4,2,768]{2,1,0:T(2,128)} %reshape.142.rank_in), custom_call_target="tpu_custom_call" | custom-call | tf_op jit(solution)/shard_map/first_exchange/pallas_call | solution.py:401
  64.1 1.0 multiply_sine_fusion
  65.0 66.8 %attend.1 = (bf16[8,9,32,128]{3,2,1,0:T(8,128)(2,1)}, bf16[32,16,4608]{2,1,0:T(8,128)(2,1)}, bf16[2,1024,384]{2,1,0:T(8,128)(2,1)}, bf16[9,32,1024]{2,1,0:T(8,12...) custom-call(s32[6]{0:T(128)} %refs_0_.1, ...), custom_call_target="tpu_custom_call" | custom-call | flops 4831838208 | bytes 8388608 | tf_op jit(solution)/shard_map/attend/pallas_call | solution.py:913
  131.8 25.4 %route_rows.1 = (bf16[4,768,384]{2,1,0:T(8,128)(2,1)}, f32[4,2,768]{2,1,0:T(2,128)}, f32[768,384]{1,0:T(8,128)}, f32[768,128]{1,0:T(8,128)}, f32[768,384]{1,0:T(...) custom-call(bf16[72,32,128]{2,1,0:T(8,128)(2,1)} %bitcast.53, ...), custom_call_target="tpu_custom_call" | custom-call | tf_op jit(solution)/shard_map/route_rows/pallas_call | solution.py:746
  157.2 0.0 all-gather.7.cloned.1.call-done
  157.2 47.4 %experts_step.2 = (f32[4,768,384]{2,1,0:T(8,128)}, f32[4,1,768]{2,1,0:T(1,128)}, f32[4,768,384]{2,1,0:T(8,128)}, bf16[128,4608]{1,0:T(8,128)(2,1)}, bf16[4,144,7...) custom-call(bf16[1152,1536]{1,0:T(8,128)(2,1)} %bitcast.64, bf16[4,768,384]{2,1,0:T(8,128)(2,1)} %get-tuple-element.67.refs_1_, ...), custom_call_target="tpu_custom_call" | custom-call | flops 19931332608 | bytes 26214400 | tf_op jit(solution)/shard_map/experts_step/pallas_call | solution.py:1587
  204.6 0.0 all-gather.5.cloned.1.call-done
  204.6 62.2 %experts_step.3 = (bf16[4,768,384]{2,1,0:T(8,128)(2,1)}, f32[4,2,768]{2,1,0:T(2,128)}, bf16[4,768,384]{2,1,0:T(8,128)(2,1)}, f32[16,4608]{1,0:T(8,128)}, bf16[4,...) custom-call(bf16[1152,1536]{1,0:T(8,128)(2,1)} %bitcast.63, ...), custom_call_target="tpu_custom_call" | custom-call | flops 19931332608 | bytes 26214400 | tf_op jit(solution)/shard_map/experts_step/pallas_call | solution.py:1587
  266.8 39.1 %middle_step.1 = (bf16[9,32,1024]{2,1,0:T(8,128)(2,1)}, f32[768,384]{1,0:T(8,128)}, bf16[384,512]{1,0:T(8,128)(2,1)}, bf16[4,144,768]{2,1,0:T(8,128)(2,1)}, bf16[144,768]{1,0:T(8,128)(2,1)}) custom-call(bf16[4,768,384]{2,1,0:T(8,128)(2,1)} %get-tuple-element.78.gin_ref, f32[4,2,768]{2,1,0:T(2,128)} %get-tuple-element.79.ggate_ref, ...), custom_call_target="tpu_custom_call" | custom-call | tf_op jit(solution)/shard_map/middle_step/pallas_call | solution.py:1743
  305.9 67.1 %attend_back.1 = (bf16[768,384]{1,0:T(8,128)(2,1)}, f32[768,384]{1,0:T(8,128)}, f32[16,6272]{1,0:T(8,128)}, bf16[144,768]{1,0:T(8,128)(2,1)}) custom-call(s32[6]{0:T(128)} %refs_0_.1, bf16[2,1024,384]{2,1,0:T(8,128)(2,1)} %bitcast.67, bf16[2,1024,384]{2,1,0:T(8,128)(2,1)} %get-tuple-element.59.refs_2_, bf16[1280,384]{1,0:T(8,128)(2,1)} %get-tuple-element.60.refs_3_, ...), custom_call_target="tpu_custom_call" | custom-call | flops 12079595520 | bytes 12582912 | tf_op jit(solution)/shard_map/attend_back/pallas_call | solution.py:1187
  373.1 1.2 reshape.154
  374.2 0.0 copy-start.6
  374.3 1.1 maximum_bitcast_fusion
  375.4 0.0 copy-start.10
  375.4 0.0 copy-start.11
  375.4 0.0 copy-start.12
  375.4 0.0 copy-start.4
  375.4 2.1 fusion.10
  377.6 0.0 copy-start.2
  377.6 0.0 copy-start.3
  377.6 1.4 copy.26
  379.0 0.0 copy-start
  379.0 0.0 copy-start.1
  379.0 1.2 multiply_add_fusion.3
  380.2 1.5 copy-done.1
  381.7 8.9 %multiply_add_fusion.1 = (f32[2,221184]{1,0:T(2,128)}, f32[2,221184]{1,0:T(2,128)}, f32[2,221184]{1,0:T(2,128)}, f32[2,221184]{1,0:T(2,128)}) fusion(f32[2,221184]{1,0:T(2,128)S(1)} %copy-done.2, f32[2,221184]{1,0:T(2,128)S(1)} %copy-done.1, f32[2,221184]{1,0:T(2,128)S(1)} %bitcast.50, f32[2,221184]{1,0:T(2,128)S(1)} %copy-done.3, f32[2,221184]{1,0:T(2,128)S(1)} %copy-done.4), kind=kLoop, calls=%fused_computation.16 | loop fusion | flops 7520256 | bytes 15925248 | tf_op jit(solution)/shard_map/add | solution.py:51
  390.6 0.8 copy.33
  391.4 0.7 copy-done.7
  392.1 1.0 copy.34
  (34 shorter events, 0.1 us)
Async XLA Ops:
  7.2 150.0 %all-gather.7.cloned.1.call-start = ((), (), s32[]{:S(2)}) async-start(), calls=%async_computation.1 | async-start | bytes 3981312 | tf_op jit(solution)/shard_map/all_gather | solution.py:1819
  11.0 1.8 copy-start.5
  11.0 2.2 copy-start.16
  12.0 3.6 copy-start.17
  12.0 3.7 copy-start.8
  12.0 192.6 %all-gather.5.cloned.1.call-start = ((), (), s32[]{:S(2)}) async-start(), calls=%async_computation | async-start | bytes 3981312 | tf_op jit(solution)/shard_map/all_gather | solution.py:1819
  305.9 68.3 %copy-start.13 = (bf16[144,768]{1,0:T(8,128)(2,1)S(1)}, bf16[144,768]{1,0:T(8,128)(2,1)}, u32[]{:S(2)}) copy-start(bf16[144,768]{1,0:T(8,128)(2,1)} %get-tuple-element.99) | copy-start | bytes 663556
  305.9 68.3 %copy-start.14 = (bf16[144,768]{1,0:T(8,128)(2,1)S(1)}, bf16[144,768]{1,0:T(8,128)(2,1)}, u32[]{:S(2)}) copy-start(bf16[144,768]{1,0:T(8,128)(2,1)} %get-tuple-element.98) | copy-start | bytes 663556
  305.9 68.3 %copy-start.15 = (bf16[144,768]{1,0:T(8,128)(2,1)S(1)}, bf16[144,768]{1,0:T(8,128)(2,1)}, u32[]{:S(2)}) copy-start(bf16[144,768]{1,0:T(8,128)(2,1)} %get-tuple-element.100) | copy-start | bytes 663556
  374.2 4.7 %copy-start.6 = (f32[73860]{0:T(1024)}, f32[73860]{0:T(1024)S(1)}, u32[]{:S(2)}) copy-start(f32[73860]{0:T(1024)S(1)} %reshape.154) | copy-start | bytes 886324
  375.4 3.6 copy-start.10
  375.4 3.6 copy-start.11
  375.4 3.6 copy-start.12
  375.4 4.8 %copy-start.4 = (f32[2,221184]{1,0:T(2,128)S(1)}, f32[2,221184]{1,0:T(2,128)}, u32[]{:S(2)}) copy-start(f32[2,221184]{1,0:T(2,128)} %param.21) | copy-start | bytes 5308420
  377.6 2.7 copy-start.2
  377.6 2.7 copy-start.3
  379.0 11.6 %copy-start = (f32[1,2,144,1536]{3,1,2,0:T(2,128)}, f32[1,2,144,1536]{3,1,2,0:T(2,128)S(1)}, u32[]{:S(2)}) copy-start(f32[1,2,144,1536]{3,1,2,0:T(2,128)S(1)} %copy.26) | copy-start | bytes 5308420
  379.0 2.7 copy-start.1
  381.7 8.9 %copy-start.9 = (bf16[768,384]{1,0:T(8,128)(2,1)S(1)}, bf16[768,384]{1,0:T(8,128)(2,1)}, u32[]{:S(2)}) copy-start(bf16[768,384]{1,0:T(8,128)(2,1)} %get-tuple-element.95) | copy-start | bytes 1769476
  390.6 1.5 copy-start.7
Sparse Core Ops, SparseCore 0:
  12.1 109.6 all-gather.6
  124.6 63.9 all-gather.4
